TPU v7x, 32 devices: a whole 2x2x4 slice. The times are simulated.
32 devices in a mesh: dp: 2 (over y), blk: 16 (over z, x, core).
Axes of the slice: x: 2, y: 2, z: 4, core: 2. Of those that a mesh axis runs over, the one named last changes fastest.
Arguments:
- tokens: bfloat16 [2, 16384, 768], P(None, ('dp', 'blk')), may hold values from -6 to 6
- memory: bfloat16 [2, 8, 20, 768], P(None, 'dp'), may hold values from -6 to 6
- chain_lengths: int32 [2, 2, 4], P(None, 'dp'), may hold values from 1 to 7, 16 in all within a row
- last_fill: int32 [2, 2, 4], P(None, 'dp'), may hold values from 1 to 512
- query_proj: bfloat16 [768, 768], replicated, may hold values from -0.21875 to 0.21875
- query_bias: bfloat16 [768], replicated, may hold values from -1.75 to 1.75
- key_proj: bfloat16 [768, 768], replicated, may hold values from -0.21875 to 0.21875
- value_proj: bfloat16 [768, 768], replicated, may hold values from -0.21875 to 0.21875
- value_bias: bfloat16 [768], replicated, may hold values from -1.75 to 1.75
- output_proj: bfloat16 [768, 768], replicated, may hold values from -3.5 to 3.5
- output_bias: bfloat16 [768], replicated, may hold values from -1.75 to 1.75
- attn_gain: bfloat16 [768], replicated, may hold values from 0.5 to 1.5
- attn_shift: bfloat16 [768], replicated, may hold values from -1.75 to 1.75
- inner_proj: bfloat16 [768, 3072], replicated, may hold values from -0.21875 to 0.21875
- inner_bias: bfloat16 [3072], replicated, may hold values from -1.75 to 1.75
- outer_proj: bfloat16 [3072, 768], replicated, may hold values from -0.109375 to 0.109375
- outer_bias: bfloat16 [768], replicated, may hold values from -1.75 to 1.75
- final_gain: bfloat16 [768], replicated, may hold values from 0.5 to 1.5
- final_shift: bfloat16 [768], replicated, may hold values from -1.75 to 1.75
- token_cotangent: bfloat16 [2, 16384, 768], P(None, ('dp', 'blk')), may hold values from -6 to 6
- memory_cotangent: bfloat16 [2, 8, 20, 768], P(None, 'dp'), may hold values from -6 to 6
Outputs:
- layer_output: bfloat16 [2, 16384, 768], P(None, ('dp', 'blk'))
- memory_output: bfloat16 [2, 8, 20, 768], P(None, 'dp')
- token_grad: bfloat16 [2, 16384, 768], P(None, ('dp', 'blk'))
- memory_grad: bfloat16 [2, 8, 20, 768], P(None, 'dp')
- grad_query_proj: float32 [768, 768], replicated
- grad_query_bias: float32 [768], replicated
- grad_key_proj: float32 [768, 768], replicated
- grad_value_proj: float32 [768, 768], replicated
- grad_value_bias: float32 [768], replicated
- grad_output_proj: float32 [768, 768], replicated
- grad_output_bias: float32 [768], replicated
- grad_attn_gain: float32 [768], replicated
- grad_attn_shift: float32 [768], replicated
- grad_inner_proj: float32 [768, 3072], replicated
- grad_inner_bias: float32 [3072], replicated
- grad_outer_proj: float32 [3072, 768], replicated
- grad_outer_bias: float32 [768], replicated
- grad_final_gain: float32 [768], replicated
- grad_final_shift: float32 [768], replicated
Inputs may be any that keep to these rules, and one draw needn't show every extreme that they name: `chain_lengths`: the lengths of each group's 4 chains add up to 16, and the longest chain of each group has 7 segments. The tokens of a chain's last segment after last_fill are padding.
All inputs are finite; a program needn't handle non-finite values.
Results may differ from a plain program's by a relative error of at most 0.02.
Values may be sent and summed in bfloat16 or wider, within the bound.
No kernel may reach another device: no remote copies, remote signals or barrier semaphores. Data moves between devices by JAX's collectives and lax.ppermute only.
A program may use at most 384 MiB of HBM per device.

v0:
```python
import jax
import jax.numpy as jnp
from jax import lax
from jax.sharding import PartitionSpec as P

H = 12


NEG = -1e30
EPS = 1e-05


def from_behind(value, axis, steps):
    count = lax.axis_size(axis)
    pairs = [(source, (source + steps) % count) for source in range(count)]
    return lax.ppermute(value, axis, pairs)


def merged(value, axis, join):
    pieces = jax.tree.map(lambda part: lax.all_gather(part, axis), value)
    head = jax.tree.map(lambda part: part[0], pieces)
    tail = jax.tree.map(lambda part: part[1:], pieces)
    total, _ = lax.scan(lambda total, slab: (join(total, slab), None), head, tail)
    return total


def normalize(values):
    centered = values - jnp.mean(values, axis=-1, keepdims=True)
    return centered * lax.rsqrt(jnp.mean(centered * centered, axis=-1, keepdims=True) + EPS)


def norm_back(values, upstream):
    return jax.vjp(normalize, values)[1](upstream)[0]


def gelu_exact(values):
    return jax.nn.gelu(values, approximate=False)


def pick_row(table, index_now):
    return lax.dynamic_index_in_dim(table, index_now, keepdims=False)


def chain_table(lengths, fill_counts, seg_len, seg_count):
    chain_ends = jnp.cumsum(lengths)
    segment = jnp.arange(seg_count, dtype=jnp.int32)
    chain_of = jnp.sum((chain_ends[None, :] <= segment[:, None]).astype(jnp.int32), axis=1)
    member = chain_of[:, None] == jnp.arange(lengths.shape[0], dtype=jnp.int32)[None, :]
    end_of = jnp.sum(jnp.where(member, chain_ends[None, :], 0), axis=1)
    fill_of = jnp.sum(jnp.where(member, fill_counts[None, :], 0), axis=1)
    used_count = jnp.where(end_of - 1 == segment, fill_of, seg_len)
    key_live = jnp.arange(seg_len, dtype=jnp.int32)[None, :] < used_count[:, None]
    return (chain_of, key_live)


def scores_of(query_rows, key_rows):
    score_scale = query_rows.shape[-1] ** (-0.5)
    return (
        jnp.einsum("qhd,khd->hqk", query_rows, key_rows, preferred_element_type=jnp.float32)
        * score_scale
    )


def state_update(run_state, scores, key_mask):
    run_max, run_total = run_state
    masked = jnp.where(key_mask[None], scores, NEG)
    new_max = jnp.maximum(run_max, jnp.max(masked, axis=-1))
    terms = jnp.where(key_mask[None], jnp.exp(masked - new_max[..., None]), 0.0)
    return (new_max, run_total * jnp.exp(run_max - new_max) + jnp.sum(terms, axis=-1))


def combine_states(earlier, latter):
    joint_max = jnp.maximum(earlier[0], latter[0])
    return (
        joint_max,
        earlier[1] * jnp.exp(earlier[0] - joint_max) + latter[1] * jnp.exp(latter[0] - joint_max),
    )


def weights_of(scores, key_mask, log_total):
    return jnp.where(key_mask[None], jnp.exp(scores - log_total[..., None]), 0.0)


def value_block(totals, query_rows, key_rows, value_rows, key_mask, log_total):
    weights = weights_of(scores_of(query_rows, key_rows), key_mask, log_total).astype(jnp.bfloat16)
    return totals + jnp.einsum(
        "hqk,khd->qhd", weights, value_rows, preferred_element_type=jnp.float32
    )


def grad_block(query_rows, key_rows, value_rows, out_grad, row_delta, key_mask, log_total):
    score_scale = query_rows.shape[-1] ** (-0.5)
    exact_weights = weights_of(scores_of(query_rows, key_rows), key_mask, log_total)
    weights = exact_weights.astype(jnp.bfloat16)
    weight_grad = jnp.einsum(
        "qhd,khd->hqk", out_grad, value_rows, preferred_element_type=jnp.float32
    )
    score_grad = (exact_weights * (weight_grad - row_delta[..., None])).astype(jnp.bfloat16)
    query_grad = (
        jnp.einsum("hqk,khd->qhd", score_grad, key_rows, preferred_element_type=jnp.float32)
        * score_scale
    )
    key_grad = (
        jnp.einsum("hqk,qhd->khd", score_grad, query_rows, preferred_element_type=jnp.float32)
        * score_scale
    )
    value_grad = jnp.einsum("hqk,qhd->khd", weights, out_grad, preferred_element_type=jnp.float32)
    return (query_grad, key_grad, value_grad)


def token_lse(run_state, query_rows, key_rows, shard_chain, shard_live, own_chain):
    key_mask = ((shard_chain == own_chain) & shard_live)[None, :]

    def update(previous):
        return state_update(previous, scores_of(query_rows, key_rows), key_mask)

    return update(run_state)


def token_values(
    totals, query_rows, key_rows, value_rows, shard_chain, shard_live, own_chain, log_total
):
    key_mask = ((shard_chain == own_chain) & shard_live)[None, :]

    def update(previous):
        return value_block(previous, query_rows, key_rows, value_rows, key_mask, log_total)

    return update(totals)


def token_grads(
    query_rows,
    key_rows,
    value_rows,
    out_grad,
    row_delta,
    shard_chain,
    shard_live,
    own_chain,
    log_total,
):
    key_mask = ((shard_chain == own_chain) & shard_live)[None, :]
    return grad_block(query_rows, key_rows, value_rows, out_grad, row_delta, key_mask, log_total)


def local(
    tokens,
    memory,
    chain_lengths,
    last_fill,
    query_proj,
    query_bias,
    key_proj,
    value_proj,
    value_bias,
    output_proj,
    output_bias,
    attn_gain,
    attn_shift,
    inner_proj,
    inner_bias,
    outer_proj,
    outer_bias,
    final_gain,
    final_shift,
    token_cotangent,
    memory_cotangent,
):
    cycle_size = lax.axis_size("blk")
    own_index = lax.axis_index("blk")
    lead_flag = (own_index == 0).astype(jnp.float32)
    seg_len = tokens.shape[1]
    model_width = tokens.shape[2]
    chain_count = memory.shape[1]
    mem_per_chain = memory.shape[2]
    mem_count = chain_count * mem_per_chain
    all_rows = seg_len + mem_count
    head_count = H
    head_dim = model_width // head_count
    weight_list = (
        query_proj,
        query_bias,
        key_proj,
        value_proj,
        value_bias,
        output_proj,
        output_bias,
        attn_gain,
        attn_shift,
        inner_proj,
        inner_bias,
        outer_proj,
        outer_bias,
        final_gain,
        final_shift,
    )
    grad_sums = [jnp.zeros(w.shape, jnp.float32) for w in weight_list]
    token_outs, memory_outs, token_grads_out, memory_grads_out = ([], [], [], [])
    for batch_index in range(tokens.shape[0]):
        chain_of, key_live = chain_table(
            chain_lengths[batch_index, 0], last_fill[batch_index, 0], seg_len, cycle_size
        )
        own_chain = pick_row(chain_of, own_index)
        own_live = pick_row(key_live, own_index)
        mem_chain = jnp.repeat(jnp.arange(chain_count, dtype=jnp.int32), mem_per_chain)
        row_block = jnp.concatenate(
            [tokens[batch_index], memory[batch_index].reshape(mem_count, model_width)], 0
        )
        row_live = jnp.concatenate(
            [own_live.astype(jnp.float32), jnp.ones((mem_count,), jnp.float32)]
        )
        row_weight = jnp.concatenate(
            [jnp.ones((seg_len,), jnp.float32), jnp.full((mem_count,), lead_flag)]
        )
        weight_low = row_weight.astype(jnp.bfloat16)[:, None]
        query_all = (
            (jnp.dot(row_block, query_proj, preferred_element_type=jnp.float32) + query_bias)
            .astype(jnp.bfloat16)
            .reshape(all_rows, head_count, head_dim)
        )
        key_all = (
            jnp.dot(row_block, key_proj, preferred_element_type=jnp.float32)
            .astype(jnp.bfloat16)
            .reshape(all_rows, head_count, head_dim)
        )
        value_all = (
            (jnp.dot(row_block, value_proj, preferred_element_type=jnp.float32) + value_bias)
            .astype(jnp.bfloat16)
            .reshape(all_rows, head_count, head_dim)
        )
        tok_query, mem_query = (query_all[:seg_len], query_all[seg_len:])
        tok_key, mem_key = (key_all[:seg_len], key_all[seg_len:])
        tok_value, mem_value = (value_all[:seg_len], value_all[seg_len:])
        tok_mem_mask = (mem_chain == own_chain)[None, :]
        mem_own_mask = (mem_chain[:, None] == own_chain) & own_live[None, :]
        mem_mem_mask = mem_chain[:, None] == mem_chain[None, :]
        zero_rows = jnp.zeros((seg_len, head_count, head_dim), jnp.float32)
        start_state = (
            jnp.full((head_count, seg_len), NEG, jnp.float32),
            jnp.zeros((head_count, seg_len), jnp.float32),
        )
        tok_state = state_update(start_state, scores_of(tok_query, mem_key), tok_mem_mask)
        tok_state = token_lse(tok_state, tok_query, tok_key, own_chain, own_live, own_chain)
        stored_keys = jnp.zeros((cycle_size,) + tok_key.shape, jnp.bfloat16)
        stored_keys = lax.dynamic_update_index_in_dim(stored_keys, tok_key, 0, 0)
        stored_values = jnp.zeros((cycle_size,) + tok_value.shape, jnp.bfloat16)
        stored_values = lax.dynamic_update_index_in_dim(stored_values, tok_value, 0, 0)

        def lse_turn(step_index, loop_state):
            key_rows, value_rows, key_store, value_store, run_state = loop_state
            key_rows, value_rows = from_behind((key_rows, value_rows), "blk", 1)
            key_store = lax.dynamic_update_index_in_dim(key_store, key_rows, step_index, 0)
            value_store = lax.dynamic_update_index_in_dim(value_store, value_rows, step_index, 0)
            shard_index = (own_index - step_index) % cycle_size
            return (
                key_rows,
                value_rows,
                key_store,
                value_store,
                token_lse(
                    run_state,
                    tok_query,
                    key_rows,
                    pick_row(chain_of, shard_index),
                    pick_row(key_live, shard_index),
                    own_chain,
                ),
            )

        loop_out = lax.fori_loop(
            1, cycle_size, lse_turn, (tok_key, tok_value, stored_keys, stored_values, tok_state)
        )
        stored_keys, stored_values, tok_state = (loop_out[2], loop_out[3], loop_out[4])
        log_tok = tok_state[0] + jnp.log(tok_state[1])
        tok_totals = value_block(zero_rows, tok_query, mem_key, mem_value, tok_mem_mask, log_tok)

        def value_turn(step_index, totals):
            shard_index = (own_index - step_index) % cycle_size
            return token_values(
                totals,
                tok_query,
                pick_row(stored_keys, step_index),
                pick_row(stored_values, step_index),
                pick_row(chain_of, shard_index),
                pick_row(key_live, shard_index),
                own_chain,
                log_tok,
            )

        tok_totals = lax.fori_loop(0, cycle_size, value_turn, tok_totals)
        mem_start = (
            jnp.full((head_count, mem_count), NEG, jnp.float32),
            jnp.zeros((head_count, mem_count), jnp.float32),
        )
        mem_part = state_update(mem_start, scores_of(mem_query, tok_key), mem_own_mask)
        mem_state = merged(mem_part, "blk", combine_states)
        mem_state = state_update(mem_state, scores_of(mem_query, mem_key), mem_mem_mask)
        log_mem = mem_state[0] + jnp.log(mem_state[1])
        mem_zero = jnp.zeros((mem_count, head_count, head_dim), jnp.float32)
        mem_totals = lax.psum(
            value_block(mem_zero, mem_query, tok_key, tok_value, mem_own_mask, log_mem).astype(
                jnp.bfloat16
            ),
            "blk",
        ).astype(jnp.float32)
        mem_totals = value_block(mem_totals, mem_query, mem_key, mem_value, mem_mem_mask, log_mem)
        attended = jnp.concatenate([tok_totals, mem_totals], 0)
        attended_low = attended.reshape(all_rows, model_width).astype(jnp.bfloat16)
        branch = (
            jnp.dot(attended_low, output_proj, preferred_element_type=jnp.float32) + output_bias
        )
        first_sum = row_block.astype(jnp.float32) + branch
        first_norm = normalize(first_sum)
        first = first_norm * attn_gain + attn_shift
        first_low = first.astype(jnp.bfloat16)
        inner = jnp.dot(first_low, inner_proj, preferred_element_type=jnp.float32) + inner_bias
        active_low = gelu_exact(inner).astype(jnp.bfloat16)
        outer = jnp.dot(active_low, outer_proj, preferred_element_type=jnp.float32) + outer_bias
        second_sum = first + outer
        final_norm = normalize(second_sum)
        final = (final_norm * final_gain + final_shift) * row_live[:, None]
        token_outs.append(final[:seg_len].astype(jnp.bfloat16))
        memory_outs.append(
            final[seg_len:].reshape(chain_count, mem_per_chain, model_width).astype(jnp.bfloat16)
        )
        cotangent = (
            jnp.concatenate(
                [
                    token_cotangent[batch_index].astype(jnp.float32),
                    memory_cotangent[batch_index]
                    .reshape(mem_count, model_width)
                    .astype(jnp.float32),
                ],
                0,
            )
            * row_live[:, None]
        )
        weighted_cot = cotangent * row_weight[:, None]
        grad_sums[13] = grad_sums[13] + jnp.sum(weighted_cot * final_norm, axis=0)
        grad_sums[14] = grad_sums[14] + jnp.sum(weighted_cot, axis=0)
        second_grad = norm_back(second_sum, cotangent * final_gain)
        outer_grad = second_grad.astype(jnp.bfloat16)
        outer_weighted = outer_grad * weight_low
        grad_sums[12] = grad_sums[12] + jnp.sum(outer_weighted.astype(jnp.float32), axis=0)
        grad_sums[11] = grad_sums[11] + jnp.einsum(
            "rf,rd->fd", active_low, outer_weighted, preferred_element_type=jnp.float32
        )
        active_grad = jnp.einsum(
            "rd,fd->rf", outer_grad, outer_proj, preferred_element_type=jnp.float32
        )
        inner_grad = jax.vjp(gelu_exact, inner)[1](active_grad)[0].astype(jnp.bfloat16)
        inner_weighted = inner_grad * weight_low
        grad_sums[10] = grad_sums[10] + jnp.sum(inner_weighted.astype(jnp.float32), axis=0)
        grad_sums[9] = grad_sums[9] + jnp.einsum(
            "rd,rf->df", first_low, inner_weighted, preferred_element_type=jnp.float32
        )
        first_grad = second_grad + jnp.einsum(
            "rf,df->rd", inner_grad, inner_proj, preferred_element_type=jnp.float32
        )
        weighted_first = first_grad * row_weight[:, None]
        grad_sums[7] = grad_sums[7] + jnp.sum(weighted_first * first_norm, axis=0)
        grad_sums[8] = grad_sums[8] + jnp.sum(weighted_first, axis=0)
        res_grad = norm_back(first_sum, first_grad * attn_gain)
        branch_grad = res_grad.astype(jnp.bfloat16)
        branch_weighted = branch_grad * weight_low
        grad_sums[6] = grad_sums[6] + jnp.sum(branch_weighted.astype(jnp.float32), axis=0)
        grad_sums[5] = grad_sums[5] + jnp.einsum(
            "rd,re->de", attended_low, branch_weighted, preferred_element_type=jnp.float32
        )
        attended_grad = (
            jnp.einsum("re,de->rd", branch_grad, output_proj, preferred_element_type=jnp.float32)
            .astype(jnp.bfloat16)
            .reshape(all_rows, head_count, head_dim)
        )
        row_delta = jnp.einsum("qhd,qhd->hq", attended_grad.astype(jnp.float32), attended)
        tok_out_grad, mem_out_grad = (attended_grad[:seg_len], attended_grad[seg_len:])
        delta_tok, delta_mem = (row_delta[:, :seg_len], row_delta[:, seg_len:])
        tok_query_grad, mem_key_part, mem_value_part = grad_block(
            tok_query, mem_key, mem_value, tok_out_grad, delta_tok, tok_mem_mask, log_tok
        )

        def grad_turn(step_index, loop_state):
            key_sums, value_sums, query_sums = loop_state
            shard_index = (own_index - step_index) % cycle_size
            query_part, key_part, value_part = token_grads(
                tok_query,
                pick_row(stored_keys, step_index),
                pick_row(stored_values, step_index),
                tok_out_grad,
                delta_tok,
                pick_row(chain_of, shard_index),
                pick_row(key_live, shard_index),
                own_chain,
                log_tok,
            )
            key_sums, value_sums = (
                from_behind((key_sums + key_part).astype(jnp.bfloat16), "blk", 1).astype(
                    jnp.float32
                ),
                from_behind((value_sums + value_part).astype(jnp.bfloat16), "blk", 1).astype(
                    jnp.float32
                ),
            )
            return (key_sums, value_sums, query_sums + query_part)

        tok_key_grad, tok_value_grad, tok_query_grad = lax.fori_loop(
            0, cycle_size, grad_turn, (zero_rows, zero_rows, tok_query_grad)
        )
        mem_query_part, own_key_extra, own_value_extra = grad_block(
            mem_query, tok_key, tok_value, mem_out_grad, delta_mem, mem_own_mask, log_mem
        )
        tok_key_grad = tok_key_grad + own_key_extra
        tok_value_grad = tok_value_grad + own_value_extra
        mem_query_grad, mem_key_grad, mem_value_grad = (
            lax.psum(mem_query_part.astype(jnp.bfloat16), "blk").astype(jnp.float32),
            lax.psum(mem_key_part.astype(jnp.bfloat16), "blk").astype(jnp.float32),
            lax.psum(mem_value_part.astype(jnp.bfloat16), "blk").astype(jnp.float32),
        )
        local_query, local_key, local_value = grad_block(
            mem_query, mem_key, mem_value, mem_out_grad, delta_mem, mem_mem_mask, log_mem
        )
        query_grad = (
            jnp.concatenate([tok_query_grad, mem_query_grad + local_query], 0)
            .reshape(all_rows, model_width)
            .astype(jnp.bfloat16)
        )
        key_grad = (
            jnp.concatenate([tok_key_grad, mem_key_grad + local_key], 0)
            .reshape(all_rows, model_width)
            .astype(jnp.bfloat16)
        )
        value_grad = (
            jnp.concatenate([tok_value_grad, mem_value_grad + local_value], 0)
            .reshape(all_rows, model_width)
            .astype(jnp.bfloat16)
        )
        query_weighted = query_grad * weight_low
        key_weighted = key_grad * weight_low
        value_weighted = value_grad * weight_low
        grad_sums[0] = grad_sums[0] + jnp.einsum(
            "rd,re->de", row_block, query_weighted, preferred_element_type=jnp.float32
        )
        grad_sums[1] = grad_sums[1] + jnp.sum(query_weighted.astype(jnp.float32), axis=0)
        grad_sums[2] = grad_sums[2] + jnp.einsum(
            "rd,re->de", row_block, key_weighted, preferred_element_type=jnp.float32
        )
        grad_sums[3] = grad_sums[3] + jnp.einsum(
            "rd,re->de", row_block, value_weighted, preferred_element_type=jnp.float32
        )
        grad_sums[4] = grad_sums[4] + jnp.sum(value_weighted.astype(jnp.float32), axis=0)
        input_grad = (
            res_grad
            + jnp.einsum("re,de->rd", query_grad, query_proj, preferred_element_type=jnp.float32)
            + jnp.einsum("re,de->rd", key_grad, key_proj, preferred_element_type=jnp.float32)
            + jnp.einsum("re,de->rd", value_grad, value_proj, preferred_element_type=jnp.float32)
        )
        token_grads_out.append(input_grad[:seg_len].astype(jnp.bfloat16))
        memory_grads_out.append(
            input_grad[seg_len:]
            .reshape(chain_count, mem_per_chain, model_width)
            .astype(jnp.bfloat16)
        )
    grad_tuple = tuple(grad_sums)
    grad_tuple = lax.psum(grad_tuple, ("dp", "blk"))
    return (
        jnp.stack(token_outs),
        jnp.stack(memory_outs),
        jnp.stack(token_grads_out),
        jnp.stack(memory_grads_out),
        grad_tuple[0],
        grad_tuple[1],
        grad_tuple[2],
        grad_tuple[3],
        grad_tuple[4],
        grad_tuple[5],
        grad_tuple[6],
        grad_tuple[7],
        grad_tuple[8],
        grad_tuple[9],
        grad_tuple[10],
        grad_tuple[11],
        grad_tuple[12],
        grad_tuple[13],
        grad_tuple[14],
    )


def solution(mesh):
    in_specs = (
        P(None, ("dp", "blk"), None),
        P(None, "dp", None, None),
        P(None, "dp", None),
        P(None, "dp", None),
        P(),
        P(),
        P(),
        P(),
        P(),
        P(),
        P(),
        P(),
        P(),
        P(),
        P(),
        P(),
        P(),
        P(),
        P(),
        P(None, ("dp", "blk"), None),
        P(None, "dp", None, None),
    )
    out_specs = (
        P(None, ("dp", "blk"), None),
        P(None, "dp", None, None),
        P(None, ("dp", "blk"), None),
        P(None, "dp", None, None),
        P(),
        P(),
        P(),
        P(),
        P(),
        P(),
        P(),
        P(),
        P(),
        P(),
        P(),
        P(),
        P(),
        P(),
        P(),
    )
    return jax.shard_map(local, mesh=mesh, in_specs=in_specs, out_specs=out_specs, check_vma=False)
```

profile of v0, /device:TPU:0, one launch (start us, length us, event | category | flops | bytes accessed | tf_op | source)
XLA Modules:
  0.0 3557.7 jit_solution(16204168924891993413)
XLA Ops:
  26.5 23.4 all_gather.17
  51.2 17.8 all-gather.2
  88.1 19.1 all_gather.19
  108.5 18.0 all-gather.3
  138.6 20.4 while.150
  160.7 20.3 while.153
  246.6 421.5 %while.148 = (s32[]{:T(128)}, bf16[512,12,64]{0,2,1:T(8,128)(2,1)}, bf16[512,12,64]{0,2,1:T(8,128)(2,1)}, bf16[16,512,12,64]{1,3,2,0:T(8,128)(2,1)}, bf16[16,512...) while((s32[]{:T(128)}, bf16[512,12,64]{0,2,1:T(8,128)(2,1)}, ...), condition=%wide.region_11.12_spmd, body=%wide.region_8.11_spmd.sunk | while | flops 427831840 | bytes 39938600 | solution.py:270
  279.6 11.2 collective-permute-done
  307.6 11.1 collective-permute-done
  335.6 11.1 collective-permute-done
  363.6 11.1 collective-permute-done
  391.6 11.1 collective-permute-done
  419.5 11.1 collective-permute-done
  447.5 11.1 collective-permute-done
  475.5 11.1 collective-permute-done
  503.4 11.1 collective-permute-done
  531.4 11.1 collective-permute-done
  559.4 11.1 collective-permute-done
  587.3 11.1 collective-permute-done
  615.4 11.1 collective-permute-done
  643.4 11.1 collective-permute-done
  672.7 144.4 %while.149 = (s32[]{:T(128)}, f32[512,12,64]{0,2,1:T(8,128)}, bf16[16,512,12,64]{1,3,2,0:T(8,128)(2,1)}, s32[]{:T(128)}, s32[16]{0:T(128)S(1)}, /*index=5*/s32[]...) while((s32[]{:T(128)}, f32[512,12,64]{0,2,1:T(8,128)}, ...), condition=%wide.region_13.14_spmd, body=%wide.region_12.13_spmd.sunk | while | flops 818283008 | bytes 5540666 | solution.py:290
  839.8 384.0 %while.151 = (s32[]{:T(128)}, bf16[512,12,64]{0,2,1:T(8,128)(2,1)}, bf16[512,12,64]{0,2,1:T(8,128)(2,1)}, bf16[16,512,12,64]{1,3,2,0:T(8,128)(2,1)}, bf16[16,512...) while((s32[]{:T(128)}, bf16[512,12,64]{0,2,1:T(8,128)(2,1)}, ...), condition=%wide.region_36.37_spmd, body=%wide.region_33.36_spmd.sunk | while | flops 427831840 | bytes 39938600 | solution.py:270
  1228.4 154.3 %while.152 = (s32[]{:T(128)}, f32[512,12,64]{0,2,1:T(8,128)}, bf16[16,512,12,64]{1,3,2,0:T(8,128)(2,1)}, s32[]{:T(128)}, s32[16]{0:T(128)}, /*index=5*/s32[]{:T(...) while((s32[]{:T(128)}, f32[512,12,64]{0,2,1:T(8,128)}, ...), condition=%wide.region_38.39_spmd, body=%wide.region_37.38_spmd.sunk | while | flops 818283008 | bytes 5540666 | solution.py:290
  1408.5 38.2 %multiply_convert_fusion.3 = (bf16[592,3072]{1,0:T(8,128)(2,1)S(1)}, f32[592,3072]{1,0:T(8,128)}, bf16[592,3072]{1,0:T(8,128)(2,1)S(1)}, f32[592,3072]{1,0:T(8,128)}, f32[592,3072]{1,0:T(8,128)}) fusion(f32[3072]{0:T(1024)S(1)} %copy-done.235, f32[592,3072]{1,0:T(8,128)S(1)} %fusion.201, bf16[768,3072]{1,0:T(8,128)(2,1)S(1)} %copy-done.260, ...), kind=kOutput, calls=%fused_computation.123 | convolution fusion | flops 3035738112 | bytes 42932864 | tf_op jit(solution)/shard_map/dot_general | solution.py:316
  1467.3 21.3 convert_reduce_fusion
  1564.4 685.0 %while.155 = (s32[]{:T(128)}, f32[512,12,64]{0,2,1:T(8,128)}, f32[512,12,64]{0,2,1:T(8,128)}, f32[512,12,64]{0,2,1:T(8,128)}, s32[]{:T(128)}, /*index=5*/s32[16]...) while((s32[]{:T(128)}, f32[512,12,64]{0,2,1:T(8,128)}, ...), condition=%wide.region_64.65_spmd.clone, body=%wide.region_63.64_spmd.clone.sunk | while | flops 2049049088 | bytes 166021696 | solution.py:406
  2252.9 679.0 %while.154 = (s32[]{:T(128)}, f32[512,12,64]{0,2,1:T(8,128)}, f32[512,12,64]{0,2,1:T(8,128)}, f32[512,12,64]{0,2,1:T(8,128)}, s32[]{:T(128)}, /*index=5*/s32[16]...) while((s32[]{:T(128)}, f32[512,12,64]{0,2,1:T(8,128)}, ...), condition=%wide.region_55.56_spmd.clone, body=%wide.region_54.55_spmd.clone.sunk | while | flops 2049049088 | bytes 175557264 | solution.py:406
  2935.8 13.2 convolution_add_fusion
  2963.9 88.1 %all-reduce.17.cloned.1.call-done = (bf16[80,12,64]{0,2,1:T(8,128)(2,1)}, bf16[80,12,64]{0,2,1:T(8,128)(2,1)}, bf16[80,12,64]{0,2,1:T(8,128)(2,1)}, bf16[80,12,6...) async-done(((bf16[80,12,64]{0,2,1:T(8,128)(2,1)}, bf16[80,12,64]{0,2,1:T(8,128)(2,1)}, bf16[80,12,64]{0,2,1:T(8,128)(2,1)}, ...) | async-done | bytes 737296 | tf_op jit(solution)/shard_map/psum | solution.py:416
  3112.2 43.0 %all-reduce.7 = (f32[768]{0:T(1024)}, f32[768]{0:T(1024)}, f32[768]{0:T(1024)}, f32[768]{0:T(1024)}, f32[768]{0:T(1024)}, /*index=5*/f32[3072]{0:T(1024)}, f32[768]{0:T(1024)}, f32[768]{0:T(1024)}, f32[768]{0:T(1024)}) all-reduce(f32[768]{0:T(1024)S(1)} %add.918, f32[768]{0:T(1024)S(1)} %add.922, ...), channel_id=1, replica_groups=mesh['dp'=2,'blk'=16] {'dp','blk'}, use_global_device_ids=true, to_apply=%region_71.72 | all-reduce | flops 9216 | bytes 73728 | tf_op jit(solution)/shard_map/psum | solution.py:464
  3156.6 371.4 %all-reduce.15.cloned.1.call-done = (f32[768,768]{1,0:T(8,128)}, f32[768,768]{1,0:T(8,128)}, f32[768,768]{1,0:T(8,128)}, f32[768,768]{1,0:T(8,128)}, f32[768,3072]{1,0:T(8,128)}, /*index=5*/f32[3072,768]{1,0:T(8,128)}) async-done(((f32[768,768]{1,0:T(8,128)}, f32[768,768]{1,0:T(8,128)}, f32[768,768]{1,0:T(8,128)}, f32[768,768]{1,0:T(8,128)}, f32[768,3072]{1,0:T(8,128)}, /*index=5*/f32[3072,768]{1,0:T(8,128)}), ...) | async-done | bytes 28311568 | tf_op jit(solution)/shard_map/psum | solution.py:464
  (2284 shorter events, 2601.9 us)
Async XLA Ops:
  7.2 1387.2 %all-reduce.19.cloned.1.call-start = ((), (), s32[]{:S(2)}) async-start(), calls=%async_computation.2 | async-start | bytes 786432 | tf_op jit(solution)/shard_map/psum | solution.py:300
  191.1 2860.9 %all-reduce.17.cloned.1.call-start = ((), (), s32[]{:S(2)}) async-start(), calls=%async_computation.1 | async-start | bytes 2359296 | tf_op jit(solution)/shard_map/psum | solution.py:416
  247.3 24.0 collective-permute-start.1
  276.4 22.9 collective-permute-start.1
  304.4 22.9 collective-permute-start.1
  332.4 22.9 collective-permute-start.1
  360.4 22.9 collective-permute-start.1
  388.4 22.9 collective-permute-start.1
  416.3 22.9 collective-permute-start.1
  444.3 22.9 collective-permute-start.1
  472.3 22.9 collective-permute-start.1
  500.2 22.9 collective-permute-start.1
  528.2 22.9 collective-permute-start.1
  556.1 22.9 collective-permute-start.1
  584.1 22.9 collective-permute-start.1
  612.2 22.9 collective-permute-start.1
  640.2 22.9 collective-permute-start.1
  839.8 22.7 collective-permute-start.3
  865.4 22.7 collective-permute-start.3
  891.0 22.7 collective-permute-start.3
  916.6 22.7 collective-permute-start.3
  942.2 22.7 collective-permute-start.3
  967.8 22.7 collective-permute-start.3
  993.3 22.7 collective-permute-start.3
  1018.9 22.7 collective-permute-start.3
  1044.5 22.7 collective-permute-start.3
  1070.1 22.7 collective-permute-start.3
  1095.7 22.7 collective-permute-start.3
  1121.3 22.7 collective-permute-start.3
  1147.0 22.7 collective-permute-start.3
  1198.2 22.7 collective-permute-start.3
  2959.2 568.8 %all-reduce.15.cloned.1.call-start = ((), (), s32[]{:S(2)}) async-start(), calls=%async_computation | async-start | bytes 56623104 | tf_op jit(solution)/shard_map/psum | solution.py:464
  (610 other events, 9796.4 us)
Sparse Core Ops, SparseCore 0:
  191.2 90.4 all-reduce.18
  2959.3 92.6 all-reduce.16
  3092.7 435.2 all-reduce.14
where the time goes:
time: 3580 us; the launch traced here: 3560 us
  matrix products  1440 us (40%)
  waiting for transfers between devices  1030 us (29%)
  other arithmetic  413 us (12%)
  local copies, waits for them, and re-layouts  400 us (11%)
  loops' own time  129 us (4%)
  blocking collectives  121 us (3%)
    ppermute x124, waiting for transfers between devices, from_behind(): return lax.ppermute(value, axis, pairs)  575 us
    psum x1, waiting for transfers between devices, local(): grad_tuple = lax.psum(grad_tuple, ('dp', 'blk'))  371 us
    dot_general x38, matrix products, grad_block(): jnp.einsum('hqk,qhd->khd', weights, out_grad, preferred_element_type=jnp....  273 us
    dot_general x38, matrix products, grad_block(): jnp.einsum('qhd,khd->hqk', out_grad, value_rows, preferred_element_type=j...  233 us
    dot_general x38, matrix products, value_block(): jnp.einsum('hqk,khd->qhd', weights, value_rows, preferred_element_type=jn...  215 us
    dot_general x70, matrix products, scores_of(): jnp.einsum('qhd,khd->hqk', query_rows, key_rows, preferred_element_type=j...  210 us
    dot_general x38, matrix products, grad_block(): jnp.einsum('hqk,khd->qhd', score_grad, key_rows, preferred_element_type=j...  166 us
    dot_general x38, matrix products, grad_block(): jnp.einsum('hqk,qhd->khd', score_grad, query_rows, preferred_element_type...  166 us
  transfers between devices with their start and end apart: 127, of which 126 were waited for; matrix products, arithmetic and copies ran while one was open for 36% of the time, Pallas kernels for 0%

commit v1 on v0

v1 whole, which is shorter than its diff:
```python
import functools

import jax
import jax.numpy as jnp
from jax import lax
from jax.experimental import pallas as pl
from jax.experimental.pallas import tpu as pltpu
from jax.sharding import PartitionSpec as P

H = 12
HD = 64
QUAD = 256
NQUAD = 3
PAIR = 128
MEMP = 32
SEG = 512
LONG = 7
NBLK = LONG + 1
CAP = NBLK * SEG
OWN = SEG + MEMP
STAT = 24
NPIECE = 14
NEG = -1e30
SHIFT_FREE = 60.0
EPS = 1e-05
F32 = jnp.float32
BF16 = jnp.bfloat16
VMEM_LIMIT = 60 * 2**20
LAST = (((1,), (1,)), ((), ()))

M_LEN, M_ROWS, M_BLOCKS, M_SPOT, M_USED, M_MEM, M_CHAIN, M_START, M_PIECE = range(9)


def plane_moves(shift_of):
    pairs = []
    for plane in range(4):
        for place in range(4):
            target = plane + shift_of(place >> 1)
            if 0 <= target < 4:
                pairs.append((4 * plane + place, 4 * target + place))
    return pairs


UP = plane_moves(lambda side: 1)
DOWN = plane_moves(lambda side: -1)
OUTWARD = plane_moves(lambda side: 1 if side else -1)
SIDE = [(i, i ^ 2) for i in range(16)]
CORE = [(i, i ^ 1) for i in range(16)]


def move(value, pairs):
    return lax.ppermute(value, "blk", pairs)


def gather_near(value):
    side = (lax.axis_index("blk") >> 1) & 1
    below = move(value, UP)
    above = move(value, DOWN)
    beside = move(value, SIDE)
    far = move(jnp.where(side == 1, below, above), OUTWARD)
    beside_below = move(beside, UP)
    beside_above = move(beside, DOWN)
    beside_far = move(far, SIDE)
    here = [value, beside, below, above, beside_below, beside_above, beside_far]
    return here + [move(part, CORE) for part in here]


def gather_all(value):
    return [lax.all_gather(value, "blk")]


def piece_of(own, other):
    plane = (other >> 2) - (own >> 2)
    same_side = ((other >> 1) & 1) == ((own >> 1) & 1)
    on_side = jnp.where(plane == 0, 0, jnp.where(plane < 0, 2, 3))
    off_side = jnp.where(plane == 0, 1, jnp.where(plane == -1, 4, jnp.where(plane == 1, 5, 6)))
    index = jnp.where(same_side, on_side, off_side)
    return index + jnp.where((other & 1) == (own & 1), 0, LONG)


def meta_body(own_ref, lengths, fills, meta, *, batches, chains, mem_rows):
    own = own_ref[0]
    for b in range(batches):
        end = jnp.int32(0)
        length, start, fill, chain = (jnp.int32(0) for _ in range(4))
        for c in range(chains):
            begin = end
            end = end + lengths[b, c]
            inside = (begin <= own) & (own < end)
            length = jnp.where(inside, lengths[b, c], length)
            start = jnp.where(inside, begin, start)
            fill = jnp.where(inside, fills[b, c], fill)
            chain = jnp.where(inside, c, chain)
        rows = MEMP + SEG * (length - 1) + fill
        spot = own - start
        meta[b, M_LEN] = length
        meta[b, M_ROWS] = rows
        meta[b, M_BLOCKS] = (rows + SEG - 1) // SEG
        meta[b, M_SPOT] = spot
        meta[b, M_USED] = jnp.where(spot == length - 1, fill, SEG)
        meta[b, M_MEM] = jnp.int32(mem_rows)
        meta[b, M_CHAIN] = chain
        meta[b, M_START] = start
        for place in range(8):
            meta[b, M_PIECE + place] = piece_of(own, start + place)


def metas_of(own, lengths, fills, mem_rows):
    smem = pl.BlockSpec(memory_space=pltpu.SMEM)
    body = functools.partial(
        meta_body, batches=lengths.shape[0], chains=lengths.shape[1], mem_rows=mem_rows
    )
    return pl.pallas_call(
        body,
        in_specs=[smem] * 3,
        out_specs=smem,
        out_shape=jax.ShapeDtypeStruct((lengths.shape[0], 16), jnp.int32),
        name="find_chain",
    )(own.reshape(1), lengths, fills)


def load_chain(meta, pieces, view_from, view_to, sems):
    length = meta[M_LEN]
    for spot in range(LONG):
        def start(source):
            pltpu.make_async_copy(view_from(source), view_to(spot), sems.at[spot]).start()

        @pl.when(spot < length)
        def _():
            if len(pieces) == 1:
                start(pieces[0].at[meta[M_START] + spot])
                return
            for index in range(len(pieces)):
                @pl.when(meta[M_PIECE + spot] == index)
                def _():
                    start(pieces[index])


def wait_chain(meta, pieces, view_from, view_to, sems):
    length = meta[M_LEN]
    source = pieces[0].at[0] if len(pieces) == 1 else pieces[0]
    for spot in range(LONG):
        @pl.when(spot < length)
        def _():
            pltpu.make_async_copy(view_from(source), view_to(spot), sems.at[spot]).wait()


def key_bias(meta):
    column = lax.broadcasted_iota(jnp.int32, (8, CAP), 1)
    dead = (column >= meta[M_ROWS]) | ((column >= meta[M_MEM]) & (column < MEMP))
    return jnp.where(dead, NEG, 0.0).astype(F32)


def by_chunks(blocks, run):
    def four(index, carry):
        run(index * 4, 4)
        return carry

    lax.fori_loop(0, blocks // 4, four, 0)

    @pl.when((blocks & 2) != 0)
    def _():
        run((blocks // 4) * 4, 2)

    @pl.when((blocks & 1) != 0)
    def _():
        run((blocks // 2) * 2, 1)


def span_of(first, count):
    return pl.ds(pl.multiple_of(first * SEG, SEG), count * SEG)


def forward_body(meta, *refs):
    pieces, refs = refs[:-16], refs[-16:]
    mem, wq, wk, wv, bq, bv, out, lse, kc, vc, qc, rows, qown, extended, acc, sems = refs
    quad = pl.program_id(0)
    width = rows.shape[1]
    length, blocks = meta[M_LEN], meta[M_BLOCKS]
    here = lambda source: source
    there = lambda spot: rows.at[pl.ds(MEMP + SEG * spot, SEG)]

    @pl.when(quad == 0)
    def _():
        load_chain(meta, pieces, here, there, sems)
        rows[0:MEMP, :] = mem[...]
        lse[...] = jnp.zeros_like(lse)

        @pl.when(blocks > length)
        def _():
            place = pl.multiple_of(MEMP + SEG * length, MEMP)
            rows[pl.ds(place, SEG - MEMP), :] = jnp.zeros((SEG - MEMP, width), BF16)

        wait_chain(meta, pieces, here, there, sems)

    def longest(values):
        halves = [
            jnp.max(jnp.sum(jnp.square(values[:, p : p + PAIR]), axis=1, keepdims=True))
            for p in range(0, QUAD, PAIR)
        ]
        return jnp.maximum(*halves)

    def project(start, count):
        span = pl.ds(pl.multiple_of(start, MEMP), count)
        part = rows[span, :]
        row = start + lax.broadcasted_iota(jnp.int32, (count, QUAD), 0)
        alive = (row < meta[M_ROWS]) & ((row < meta[M_MEM]) | (row >= MEMP))
        lower = (lax.broadcasted_iota(jnp.int32, (count, QUAD), 1) % PAIR) < HD
        key = jnp.dot(part, wk[...], preferred_element_type=F32)
        kc[span, :] = key.astype(BF16)
        value = jnp.dot(part, wv[...], preferred_element_type=F32) + bv[...].astype(F32)
        vc[span, :] = value.astype(BF16)
        value = jnp.where(alive, value, 0.0)
        one = jnp.where(alive, 1.0, 0.0)
        extended[0, span, :] = jnp.where(lower, value, one).astype(BF16)
        extended[1, span, :] = jnp.where(lower, one, value).astype(BF16)
        query = jnp.dot(part, wq[...], preferred_element_type=F32) + bq[...].astype(F32)
        query = query.astype(BF16) * jnp.asarray(HD**-0.5, BF16)
        qc[span, :] = query
        return longest(key)

    def project_block(block, top):
        return jnp.maximum(top, project(block * SEG, SEG))

    key_top = lax.fori_loop(0, blocks, project_block, jnp.float32(0.0))

    @pl.when(blocks == length)
    def _():
        project(length * SEG, MEMP)

    place = pl.multiple_of(MEMP + SEG * meta[M_SPOT], MEMP)
    qown[0:SEG, :] = qc[pl.ds(place, SEG), :]
    qown[SEG:OWN, :] = qc[0:MEMP, :]
    near = longest(qown[...].astype(F32)) * key_top <= SHIFT_FREE**2

    def head(index, carry):
        cols = pl.ds(pl.multiple_of((index // 2) * PAIR, PAIR), PAIR)
        half = index % 2
        lane = lax.broadcasted_iota(jnp.int32, (OWN, PAIR), 1)
        mine = (lane // HD) == half
        query = qown[:, cols]
        query = jnp.where(mine, query, jnp.zeros_like(query))
        acc[...] = jnp.zeros_like(acc)
        number = lane == quad * 4 + index

        def score(span):
            return lax.dot_general(query, kc[span, cols], LAST, preferred_element_type=F32)

        def gather(span, terms):
            values = extended[half, span, cols]
            return jnp.dot(terms.astype(BF16), values, preferred_element_type=F32)

        @pl.when(near)
        def _():
            def run(first, count):
                span = span_of(first, count)
                acc[...] += gather(span, jnp.exp(score(span)))

            by_chunks(blocks, run)
            lse[...] = jnp.where(number, 0.0, lse[...])

        @pl.when(jnp.logical_not(near))
        def _():
            def run(block, top):
                span = span_of(block, 1)
                column = block * SEG + lax.broadcasted_iota(jnp.int32, (OWN, SEG), 1)
                dead = (column >= meta[M_ROWS]) | ((column >= meta[M_MEM]) & (column < MEMP))
                scores = jnp.where(dead, NEG, score(span))
                new = jnp.maximum(top, jnp.max(scores, axis=1, keepdims=True))
                acc[...] = acc[...] * jnp.exp(top - new) + gather(span, jnp.exp(scores - new))
                return new

            top = lax.fori_loop(0, blocks, run, jnp.full((OWN, 1), NEG, F32))
            lse[...] = jnp.where(number, top, lse[...])

        sums = acc[...]
        total = jnp.where(mine, pltpu.roll(sums, HD, 1), sums)
        out[:, cols] = jnp.where(mine, sums * (1.0 / total), out[:, cols])
        lse[...] += jnp.where(number, jnp.log(total), 0.0)
        return carry

    lax.fori_loop(0, 4, head, 0)


def attend_forward(meta, pieces, mem, weights):
    wq, bq, wk, wv, bv = weights
    width = wq.shape[0]
    whole = lambda shape: pl.BlockSpec(shape, lambda quad, meta: (0,) * len(shape))
    column = lambda count: pl.BlockSpec((count, QUAD), lambda quad, meta: (0, quad))
    return pl.pallas_call(
        forward_body,
        grid_spec=pltpu.PrefetchScalarGridSpec(
            num_scalar_prefetch=1,
            grid=(NQUAD,),
            in_specs=[pl.BlockSpec(memory_space=pl.ANY)] * len(pieces)
            + [whole((MEMP, width))]
            + [column(width)] * 3
            + [column(1)] * 2,
            out_specs=[column(OWN), whole((OWN, PAIR))] + [column(CAP)] * 3,
            scratch_shapes=[
                pltpu.VMEM((CAP, width), BF16),
                pltpu.VMEM((OWN, QUAD), BF16),
                pltpu.VMEM((2, CAP, QUAD), BF16),
                pltpu.VMEM((OWN, PAIR), F32),
                pltpu.SemaphoreType.DMA((LONG,)),
            ],
        ),
        out_shape=[
            jax.ShapeDtypeStruct((OWN, width), F32),
            jax.ShapeDtypeStruct((OWN, PAIR), F32),
        ]
        + [jax.ShapeDtypeStruct((CAP, width), BF16)] * 3,
        compiler_params=pltpu.CompilerParams(vmem_limit_bytes=VMEM_LIMIT),
        cost_estimate=pl.CostEstimate(
            flops=40_000_000_000, bytes_accessed=30_000_000, transcendentals=23_000_000
        ),
        name="attend_forward",
    )(meta, *pieces, mem, wq, wk, wv, bq.reshape(1, -1), bv.reshape(1, -1))


def backward_body(meta, *refs):
    pieces, refs = refs[:-23], refs[-23:]
    (
        kc, vc, qc, mem_grad, mem_stats, own_lse, own_delta,
        dq, dk, dv,
        doc, stats, chain_stats, qown, kown, vown, down, bias, qacc, kacc, vacc, sems, stat_sems,
    ) = refs
    quad = pl.program_id(0)
    length = meta[M_LEN]

    @pl.when(quad == 0)
    def _():
        rows_from = lambda index: lambda ref: ref.at[0:SEG, pl.ds(index * QUAD, QUAD)]
        rows_to = lambda index: lambda spot: doc.at[index, pl.ds(MEMP + SEG * spot, SEG)]
        stat_from = lambda ref: ref.at[SEG : SEG + 2 * STAT, 0:SEG]
        stat_to = lambda spot: stats.at[spot]
        load_chain(meta, pieces, stat_from, stat_to, stat_sems)
        for index in range(NQUAD):
            load_chain(meta, pieces, rows_from(index), rows_to(index), sems.at[index])
        bias[...] = key_bias(meta)
        for index in range(NQUAD):
            doc[index, 0:MEMP, :] = mem_grad[:, index * QUAD : (index + 1) * QUAD]

            @pl.when(meta[M_BLOCKS] > length)
            def _():
                place = pl.multiple_of(MEMP + SEG * length, MEMP)
                doc[index, pl.ds(place, SEG - MEMP), :] = jnp.zeros((SEG - MEMP, QUAD), BF16)

        wait_chain(meta, pieces, stat_from, stat_to, stat_sems)
        for spot in range(NBLK):
            span = slice(SEG * spot, SEG * (spot + 1))
            if spot == LONG:
                chain_stats[:, span] = jnp.zeros((STAT, SEG), F32)
                continue

            @pl.when(spot < length)
            def _():
                pair = stats[spot].astype(F32)
                chain_stats[:, span] = pair[0:STAT] + pair[STAT : 2 * STAT]

            @pl.when(spot >= length)
            def _():
                chain_stats[:, span] = jnp.zeros((STAT, SEG), F32)

        moved = pltpu.roll(chain_stats[...], MEMP, 1)
        column = lax.broadcasted_iota(jnp.int32, (STAT, CAP), 1)
        entry = lax.broadcasted_iota(jnp.int32, (STAT, CAP), 0)
        beyond = jnp.where(entry < H, -NEG, 0.0)
        chain_stats[...] = jnp.where(column < MEMP + SEG * length, moved, beyond)
        lane = lax.broadcasted_iota(jnp.int32, (STAT, PAIR), 1)
        chain_stats[:, 0:PAIR] = jnp.where(lane < MEMP, mem_stats[...], chain_stats[:, 0:PAIR])
        for index in range(NQUAD):
            wait_chain(meta, pieces, rows_from(index), rows_to(index), sems.at[index])

    place = pl.multiple_of(MEMP + SEG * meta[M_SPOT], MEMP)
    for own, chain in ((qown, qc), (kown, kc), (vown, vc), (down, doc.at[quad])):
        own[0:SEG, :] = chain[pl.ds(place, SEG), :]
        own[SEG:OWN, :] = chain[0:MEMP, :]

    def head(index, carry):
        cols = pl.ds(pl.multiple_of((index // 2) * PAIR, PAIR), PAIR)
        number = quad * 4 + index
        lane = lax.broadcasted_iota(jnp.int32, (OWN, PAIR), 1)
        mine = (lane // HD) == (index % 2)
        masked = lambda ref: jnp.where(mine, ref[:, cols], jnp.zeros((OWN, PAIR), BF16))
        query, key, value, grad = masked(qown), masked(kown), masked(vown), masked(down)
        pick = lambda ref: jnp.sum(jnp.where(lane == number, ref[...], 0.0), axis=1, keepdims=True)
        log_total, delta = pick(own_lse), pick(own_delta)
        for acc in (qacc, kacc, vacc):
            acc[...] = jnp.zeros_like(acc)

        def run(first, count):
            span = span_of(first, count)
            keys, values = kc[span, cols], vc[span, cols]
            scores = lax.dot_general(query, keys, LAST, preferred_element_type=F32)
            weights = jnp.exp(scores + bias[0:1, span] - log_total)
            weight_grad = lax.dot_general(grad, values, LAST, preferred_element_type=F32)
            score_grad = (weights * (weight_grad - delta)).astype(BF16)
            qacc[...] += jnp.dot(score_grad, keys, preferred_element_type=F32)

            queries, grads = qc[span, cols], doc[quad, span, cols]
            scores = lax.dot_general(key, queries, LAST, preferred_element_type=F32)
            weights = jnp.exp(scores - chain_stats[pl.ds(number, 1), span])
            weight_grad = lax.dot_general(value, grads, LAST, preferred_element_type=F32)
            score_grad = (
                weights * (weight_grad - chain_stats[pl.ds(H + number, 1), span])
            ).astype(BF16)
            vacc[...] += jnp.dot(weights.astype(BF16), grads, preferred_element_type=F32)
            kacc[...] += jnp.dot(score_grad, queries, preferred_element_type=F32)

        by_chunks(meta[M_BLOCKS], run)
        row = lax.broadcasted_iota(jnp.int32, (OWN, PAIR), 0)
        alive = (row < meta[M_USED]) | ((row >= SEG) & (row < SEG + meta[M_MEM]))
        query_sum = qacc[...] * (HD**-0.5)
        key_sum = jnp.where(alive, kacc[...], 0.0)
        value_sum = jnp.where(alive, vacc[...], 0.0)
        for ref, sums in ((dq, query_sum), (dk, key_sum), (dv, value_sum)):
            ref[:, cols] = jnp.where(mine, sums.astype(BF16), ref[:, cols])
        return carry

    lax.fori_loop(0, 4, head, 0)


def attend_backward(meta, pieces, chain, mem_grad, mem_stats, own_lse, own_delta):
    width = mem_grad.shape[1]
    whole = lambda shape: pl.BlockSpec(shape, lambda quad, meta: (0,) * len(shape))
    column = lambda count: pl.BlockSpec((count, QUAD), lambda quad, meta: (0, quad))
    return pl.pallas_call(
        backward_body,
        grid_spec=pltpu.PrefetchScalarGridSpec(
            num_scalar_prefetch=1,
            grid=(NQUAD,),
            in_specs=[pl.BlockSpec(memory_space=pl.ANY)] * len(pieces)
            + [column(CAP)] * 3
            + [whole((MEMP, width)), whole((STAT, PAIR)), whole((OWN, PAIR)), whole((OWN, PAIR))],
            out_specs=[column(OWN)] * 3,
            scratch_shapes=[
                pltpu.VMEM((NQUAD, CAP, QUAD), BF16),
                pltpu.VMEM((LONG, 2 * STAT, SEG), BF16),
                pltpu.VMEM((STAT, CAP), F32),
            ]
            + [pltpu.VMEM((OWN, QUAD), BF16)] * 4
            + [
                pltpu.VMEM((8, CAP), F32),
                pltpu.VMEM((OWN, PAIR), F32),
                pltpu.VMEM((OWN, PAIR), F32),
                pltpu.VMEM((OWN, PAIR), F32),
                pltpu.SemaphoreType.DMA((NQUAD, LONG)),
                pltpu.SemaphoreType.DMA((LONG,)),
            ],
        ),
        out_shape=[jax.ShapeDtypeStruct((OWN, width), BF16)] * 3,
        compiler_params=pltpu.CompilerParams(vmem_limit_bytes=VMEM_LIMIT),
        cost_estimate=pl.CostEstimate(
            flops=90_000_000_000, bytes_accessed=30_000_000, transcendentals=46_000_000
        ),
        name="attend_backward",
    )(meta, *pieces, *chain, mem_grad, mem_stats, own_lse, own_delta)


def normalize(values):
    centered = values - jnp.mean(values, axis=-1, keepdims=True)
    scale = lax.rsqrt(jnp.mean(centered * centered, axis=-1, keepdims=True) + EPS)
    return centered * scale, scale


def norm_back(normed, scale, upstream):
    mean = jnp.mean(upstream, axis=-1, keepdims=True)
    along = jnp.mean(upstream * normed, axis=-1, keepdims=True)
    return scale * (upstream - mean - normed * along)


def gelu_both(values):
    cdf = 0.5 * (1.0 + lax.erf(values * (2.0**-0.5)))
    density = jnp.exp(-0.5 * values * values) * 0.3989422804014327
    return values * cdf, cdf + values * density


def times(left, right):
    return jnp.dot(left, right, preferred_element_type=F32)


def times_turned(left, right):
    return lax.dot_general(left, right, LAST, preferred_element_type=F32)


def weight_grad(left, right):
    return lax.dot_general(left, right, (((0,), (0,)), ((), ())), preferred_element_type=F32)


def sum_over(value, steps):
    taken = []
    for axis, bit in steps:
        count = lax.axis_size(axis)
        pairs = [(i, i ^ bit) for i in range(count)]
        half = value.shape[0] // 2
        upper = (lax.axis_index(axis) // bit) % 2
        keep = lax.dynamic_slice_in_dim(value, upper * half, half)
        send = lax.dynamic_slice_in_dim(value, (1 - upper) * half, half)
        got = lax.ppermute(send, axis, pairs)
        value = (keep.astype(F32) + got.astype(F32)).astype(value.dtype)
        taken.append((axis, pairs, upper))
    for axis, pairs, upper in reversed(taken):
        got = lax.ppermute(value, axis, pairs)
        value = jnp.where(
            upper == 0,
            jnp.concatenate([value, got], 0),
            jnp.concatenate([got, value], 0),
        )
    return value


def spread(value):
    for bit in (1, 2, 4, 8):
        value = value + lax.ppermute(value, "blk", [(i, i ^ bit) for i in range(16)])
    return value


def local(
    tokens, memory, chain_lengths, last_fill,
    query_proj, query_bias, key_proj, value_proj, value_bias, output_proj, output_bias,
    attn_gain, attn_shift, inner_proj, inner_bias, outer_proj, outer_bias,
    final_gain, final_shift, token_cotangent, memory_cotangent,
):
    own = lax.axis_index("blk").astype(jnp.int32)
    batches, _, width = tokens.shape
    chains, mem_rows = memory.shape[1:3]
    pad_mem = ((0, MEMP - mem_rows), (0, 0))
    head_of = (jnp.arange(width)[:, None] // HD == jnp.arange(PAIR)[None, :]).astype(F32)
    row = jnp.arange(OWN)

    metas = metas_of(own, chain_lengths[:, 0], last_fill[:, 0], mem_rows)
    pieces = [gather_near(tokens[0])] + [gather_all(tokens[b]) for b in range(1, batches)]

    states, token_outs, memory_outs = [], [], []
    for b in range(batches):
        meta = metas[b]
        chain, spot, used = meta[M_CHAIN], meta[M_SPOT], meta[M_USED]
        mem = jnp.pad(lax.dynamic_index_in_dim(memory[b], chain, keepdims=False), pad_mem)
        attended, lse, *chain_rows = attend_forward(
            meta, pieces[b], mem, (query_proj, query_bias, key_proj, value_proj, value_bias)
        )
        rows = jnp.concatenate([tokens[b], mem], 0)
        live = ((row < used) | ((row >= SEG) & (row < SEG + mem_rows))).astype(F32)[:, None]
        lead = (spot == 0).astype(F32)
        counted = jnp.where(row < SEG, 1.0, lead).astype(F32)[:, None]
        counted_low = counted.astype(BF16)
        attended_low = attended.astype(BF16)
        first_sum = rows.astype(F32) + times(attended_low, output_proj) + output_bias
        first_norm, first_scale = normalize(first_sum)
        first = first_norm * attn_gain + attn_shift
        first_low = first.astype(BF16)
        inner = times(first_low, inner_proj) + inner_bias
        active, slope = gelu_both(inner)
        active_low = active.astype(BF16)
        second_sum = first + times(active_low, outer_proj) + outer_bias
        final_norm, final_scale = normalize(second_sum)
        final = ((final_norm * final_gain + final_shift) * live).astype(BF16)
        token_outs.append(final[:SEG])
        hot = ((jnp.arange(chains) == chain) & (spot == 0))[:, None, None]
        to_all = lambda value, hot=hot: jnp.where(hot, value[SEG : SEG + mem_rows][None], 0).astype(BF16)
        memory_outs.append(to_all(final))

        mem_cot = jnp.pad(
            lax.dynamic_index_in_dim(memory_cotangent[b], chain, keepdims=False), pad_mem
        )
        cotangent = jnp.concatenate([token_cotangent[b], mem_cot], 0).astype(F32) * live
        weighted = cotangent * counted
        grad_final_gain = jnp.sum(weighted * final_norm, 0)
        grad_final_shift = jnp.sum(weighted, 0)
        second_grad = norm_back(final_norm, final_scale, cotangent * final_gain)
        outer_grad = second_grad.astype(BF16)
        outer_counted = outer_grad * counted_low
        inner_grad = (times_turned(outer_grad, outer_proj) * slope).astype(BF16)
        inner_counted = inner_grad * counted_low
        first_grad = second_grad + times_turned(inner_grad, inner_proj)
        weighted = first_grad * counted
        grad_attn_gain = jnp.sum(weighted * first_norm, 0)
        grad_attn_shift = jnp.sum(weighted, 0)
        res_grad = norm_back(first_norm, first_scale, first_grad * attn_gain)
        branch_grad = res_grad.astype(BF16)
        branch_counted = branch_grad * counted_low
        attended_grad = times_turned(branch_grad, output_proj).astype(BF16)
        delta = jnp.dot(
            attended_grad.astype(F32) * attended, head_of, precision=lax.Precision.HIGHEST
        )
        stats = jnp.concatenate([lse[:, :H], delta[:, :H]], 1).T
        high = lax.reduce_precision(stats[:, :SEG], 8, 7)
        both = jnp.concatenate([high, stats[:, :SEG] - high], 0).astype(BF16)
        payload = jnp.concatenate(
            [attended_grad[:SEG], jnp.pad(both, ((0, 0), (0, width - SEG)))], 0
        )
        states.append(
            dict(
                meta=meta, rows=rows, counted=counted_low, chain_rows=chain_rows, lse=lse,
                delta=delta, payload=gather_all(payload), mem_grad=attended_grad[SEG:],
                mem_stats=jnp.pad(stats[:, SEG:], ((0, 0), (0, PAIR - MEMP))),
                res_grad=res_grad, to_all=to_all,
                attended_low=attended_low, branch=branch_counted, first_low=first_low,
                inner=inner_counted, active=active_low, outer=outer_counted,
                small=[
                    jnp.sum(branch_counted.astype(F32), 0), grad_attn_gain, grad_attn_shift,
                    jnp.sum(inner_counted.astype(F32), 0), jnp.sum(outer_counted.astype(F32), 0),
                    grad_final_gain, grad_final_shift,
                ],
            )
        )

    def over_batches(left, right):
        return weight_grad(
            jnp.concatenate([s[left] for s in states], 0),
            jnp.concatenate([s[right] for s in states], 0),
        ).astype(BF16)

    small = jnp.concatenate([sum(s["small"][i] for s in states) for i in range(7)])
    early = (
        over_batches("first_low", "inner"),
        over_batches("active", "outer"),
        jnp.concatenate(
            [over_batches("attended_low", "branch"), small.astype(BF16).reshape(-1, width)], 0
        ),
    )
    grad_inner, grad_outer, grad_output = lax.psum(early, ("dp", "blk"))
    small = grad_output[width:].reshape(-1)
    grad_output = grad_output[:width]

    memory_out = spread(jnp.stack(memory_outs))

    token_grads, memory_grads = [], []
    for s in states:
        s["dq"], s["dk"], s["dv"] = attend_backward(
            s["meta"], s["payload"], s["chain_rows"], s["mem_grad"], s["mem_stats"],
            s["lse"], s["delta"],
        )
        for name in ("dq", "dk", "dv"):
            s[name + "_counted"] = s[name] * s["counted"]

    dp = lax.axis_size("dp")
    on_dp = [("dp", 1 << i) for i in range(dp.bit_length() - 1)]
    on_core, on_side, on_plane = [("blk", 1)], [("blk", 2)], [("blk", 4), ("blk", 8)]
    orders = (
        on_core + on_dp + on_side + on_plane,
        on_core + on_side + on_plane + on_dp,
        on_core + on_plane + on_dp + on_side,
    )
    grad_query, grad_key, grad_value = (
        sum_over(over_batches("rows", name + "_counted"), steps)
        for name, steps in zip(("dq", "dk", "dv"), orders)
    )
    biases = jnp.concatenate(
        [
            sum(jnp.sum(s[name + "_counted"].astype(F32), 0) for s in states)
            for name in ("dq", "dv")
        ]
    )
    for steps in (on_core, on_dp, on_side, on_plane):
        for axis, bit in steps:
            pairs = [(i, i ^ bit) for i in range(lax.axis_size(axis))]
            biases = biases + lax.ppermute(biases, axis, pairs)

    for s in states:
        grad = (
            s["res_grad"]
            + times_turned(s["dq"], query_proj)
            + times_turned(s["dk"], key_proj)
            + times_turned(s["dv"], value_proj)
        )
        token_grads.append(grad[:SEG].astype(BF16))
        memory_grads.append(s["to_all"](grad))
    memory_grad = spread(jnp.stack(memory_grads))

    wide = lambda value: value.astype(F32)
    cut = lambda first, count: wide(small[first : first + count])
    inner_width = inner_proj.shape[1]
    return (
        jnp.stack(token_outs),
        memory_out,
        jnp.stack(token_grads),
        memory_grad,
        wide(grad_query),
        biases[:width],
        wide(grad_key),
        wide(grad_value),
        biases[width:],
        wide(grad_output),
        cut(0, width),
        cut(width, width),
        cut(2 * width, width),
        wide(grad_inner),
        cut(3 * width, inner_width),
        wide(grad_outer),
        cut(3 * width + inner_width, width),
        cut(4 * width + inner_width, width),
        cut(5 * width + inner_width, width),
    )


def solution(mesh):
    row_spec = P(None, ("dp", "blk"), None)
    mem_spec = P(None, "dp", None, None)
    int_spec = P(None, "dp", None)
    in_specs = (row_spec, mem_spec, int_spec, int_spec) + (P(),) * 15 + (row_spec, mem_spec)
    out_specs = (row_spec, mem_spec, row_spec, mem_spec) + (P(),) * 15
    return jax.shard_map(local, mesh=mesh, in_specs=in_specs, out_specs=out_specs, check_vma=False)
```

time: 3580 us -> 1120 us (0.31)
  matrix products: 1440 us -> 90.3 us
  waiting for transfers between devices: 1030 us -> 493 us
  local copies, waits for them, and re-layouts: 400 us -> 31.9 us
  other arithmetic: 413 us -> 58.2 us
  Pallas kernels: 0 us -> 264 us
  starting transfers between devices: 3.1 us -> 159 us
  loops' own time: 129 us -> 0 us
  blocking collectives: 121 us -> 0 us
    dot_general x296 -> x26, matrix products: 1440 us -> 90.3 us  [the longest x12 40 us: times_turned(): return lax.dot_general(left, right, LAST, preferred_element_type=F32)]
    ppermute x124 -> x57, waiting for transfers between devices: 575 us -> 146 us  [the longest x14 92.4 us: move(): return lax.ppermute(value, 'blk', pairs)]
    pallas_call x0 -> x5, Pallas kernels: none -> 264 us  [the longest x2 150 us: attend_backward(): pl.pallas_call(backward_body, grid_spec=pltpu.PrefetchScalarGridSpec(num_...]
    psum x3 -> x1, waiting for transfers between devices: 460 us -> 253 us  [local(): grad_inner, grad_outer, grad_output = lax.psum(early, ('dp', 'blk'))]
    ppermute x124 -> x57, starting transfers between devices: 2.98 us -> 159 us  [the longest x5 80.8 us: local(): biases = biases + lax.ppermute(biases, axis, pairs)]
    reduce_sum x45 -> x6, other arithmetic: 138 us -> 8.5 us  [the longest x2 5.05 us: local(): jnp.sum(outer_counted.astype(F32), 0)]
    another operation x8 -> x0, loops' own time: 129 us -> none  [the longest x2 45 us: local(): lax.fori_loop(0, cycle_size, grad_turn, (zero_rows, zero_rows, tok_query_...]
    convert_element_type x73 -> x36, other arithmetic: 147 us -> 29.5 us  [the longest x8 19.8 us: local(): wide = lambda value: value.astype(F32)]
  transfers between devices with their start and end apart: 127 -> 61, of which waited for: 126 -> 24; matrix products, arithmetic and copies ran while one was open for 36% -> 7% of each run, Pallas kernels for 0% -> 17%
where the time goes in v1:
time: 1120 us
  waiting for transfers between devices  493 us (44%)
  Pallas kernels  264 us (24%)
  starting transfers between devices  159 us (14%)
  matrix products  90.3 us (8%)
  other arithmetic  58.2 us (5%)
  local copies, waits for them, and re-layouts  31.9 us (3%)
  between operations  21.4 us (2%)
    psum x1, waiting for transfers between devices, local(): grad_inner, grad_outer, grad_output = lax.psum(early, ('dp', 'blk'))  253 us
    pallas_call x2, Pallas kernels, attend_backward(): pl.pallas_call(backward_body, grid_spec=pltpu.PrefetchScalarGridSpec(num_...  150 us
    pallas_call x2, Pallas kernels, attend_forward(): pl.pallas_call(forward_body, grid_spec=pltpu.PrefetchScalarGridSpec(num_s...  113 us
    all_gather x3, waiting for transfers between devices, gather_all(): return [lax.all_gather(value, 'blk')]  94.2 us
    ppermute x14, waiting for transfers between devices, move(): return lax.ppermute(value, 'blk', pairs)  92.4 us
    ppermute x5, starting transfers between devices, local(): biases = biases + lax.ppermute(biases, axis, pairs)  80.8 us
    dot_general x12, matrix products, times_turned(): return lax.dot_general(left, right, LAST, preferred_element_type=F32)  40 us
    ppermute x14, starting transfers between devices, move(): return lax.ppermute(value, 'blk', pairs)  29 us
  transfers between devices with their start and end apart: 61, of which 24 were waited for; matrix products, arithmetic and copies ran while one was open for 7% of the time, Pallas kernels for 17%

profile of v1, /device:TPU:0, one launch (start us, length us, event | category | flops | bytes accessed | tf_op | source)
XLA Modules:
  0.0 1117.7 jit_solution(9395078070504818646)
XLA Ops:
  11.4 6.5 collective-permute-start.1
  19.8 29.4 %collective-permute-done.2.refs_3_ = bf16[512,768]{1,0:T(8,128)(2,1)S(1)} collective-permute-done((bf16[512,768]{1,0:T(8,128)(2,1)S(1)}, bf16[512,768]{1,0:T(8,128)(2,1)S(1)}, u32[]{:S(2)}, u32[]{:S(2)}) %collective-permute-start.2) | collective-permute-done | bytes 786464 | tf_op jit(solution)/shard_map/ppermute | solution.py:52
  60.8 15.0 %collective-permute-start.3 = (bf16[512,768]{1,0:T(8,128)(2,1)}, bf16[512,768]{1,0:T(8,128)(2,1)}, u32[]{:S(2)}, u32[]{:S(2)}) collective-permute-start(bf16[512,768]{1,0:T(8,128)(2,1)} %collective-permute-done.refs_1_), channel_id=1, source_target_pairs={{0,4},{1,5},{2,6},{3,7},{4,8},{5,9},{6,10},{7,11},{8,12},{9,13},{1... | collective-permute-start | bytes 2359304 | tf_op jit(solution)/shard_map/ppermute | solution.py:52
  75.8 21.8 %collective-permute-done.5 = bf16[512,768]{1,0:T(8,128)(2,1)} collective-permute-done((bf16[512,768]{1,0:T(8,128)(2,1)S(1)}, bf16[512,768]{1,0:T(8,128)(2,1)}, u32[]{:S(2)}, u32[]{:S(2)}) %collective-permute-start.5) | collective-permute-done | bytes 786464 | tf_op jit(solution)/shard_map/ppermute | solution.py:52
  101.1 41.1 %collective-permute-done.4.refs_5_ = bf16[512,768]{1,0:T(8,128)(2,1)} collective-permute-done((bf16[512,768]{1,0:T(8,128)(2,1)}, bf16[512,768]{1,0:T(8,128)(2,1)}, u32[]{:S(2)}, u32[]{:S(2)}) %collective-permute-start.4) | collective-permute-done | bytes 786464 | tf_op jit(solution)/shard_map/ppermute | solution.py:52
  154.2 81.3 %attend_forward.2 = (f32[544,768]{1,0:T(8,128)}, f32[544,128]{1,0:T(8,128)}, bf16[4096,768]{1,0:T(8,128)(2,1)}, bf16[4096,768]{1,0:T(8,128)(2,1)}, bf16[4096,768]{1,0:T(8,128)(2,1)}) custom-call(s32[16]{0:T(128)} %get-tuple-element.139.meta, bf16[512,768]{1,0:T(8,128)(2,1)} %copy-done.36, bf16[512,768]{1,0:T(8,128)(2,1)} %collective-permute-done.refs_1_, ...), custom_call_target="tpu_custom_call" | custom-call | flops 40000000000 | bytes 30000000 | tf_op jit(solution)/shard_map/attend_forward/pallas_call | solution.py:290
  239.7 31.2 %attend_forward.3 = (f32[544,768]{1,0:T(8,128)}, f32[544,128]{1,0:T(8,128)}, bf16[4096,768]{1,0:T(8,128)(2,1)}, bf16[4096,768]{1,0:T(8,128)(2,1)}, bf16[4096,768]{1,0:T(8,128)(2,1)}) custom-call(s32[16]{0:T(128)} %get-tuple-element.140.meta, bf16[16,512,768]{2,1,0:T(8,128)(2,1)} %all-gather.6.cloned.1.call-done.refs_0_, bf16[32,768]{1,0:T(8,128)(2,1)} %pad.28.refs_1_, ...), custom_call_target="tpu_custom_call" | custom-call | flops 40000000000 | bytes 30000000 | tf_op jit(solution)/shard_map/attend_forward/pallas_call | solution.py:290
  276.5 6.1 fusion.139
  282.7 8.3 multiply_convert_fusion.1
  295.4 3.1 fusion.138
  301.6 9.9 convert_reduce_fusion.1
  311.5 4.4 multiply_reduce_fusion.3
  318.2 9.9 convert_reduce_fusion
  328.1 4.6 convert_reduce_fusion.5
  335.9 10.8 fusion.20
  346.8 7.9 fusion.23
  380.1 252.7 %all-reduce.11.cloned.1.call-done = (bf16[778,768]{1,0:T(8,128)(2,1)}, bf16[768,3072]{1,0:T(8,128)(2,1)}, bf16[3072,768]{1,0:T(8,128)(2,1)}) async-done(((bf16[778,768]{1,0:T(8,128)(2,1)}, bf16[768,3072]{1,0:T(8,128)(2,1)}, bf16[3072,768]{1,0:T(8,128)(2,1)}), (bf16[778,768]{1,0:T(8,128)(2,1)}, bf16[768,3072]{1,0:T(8,128)(2,1)}, bf16[3072,768]{1,0:T(8,128)(2,1)})) %all-reduce.11.cloned.1.call-update) | async-done | bytes 10632208 | tf_op jit(solution)/shard_map/psum | solution.py:623
  634.2 7.5 convert_element_type.532
  641.7 4.5 convert_element_type.536
  648.4 94.1 %all-gather.8.cloned.1.call-done = bf16[8960,768]{1,0:T(8,128)(2,1)} async-done(((bf16[560,768]{1,0:T(8,128)(2,1)}), bf16[8960,768]{1,0:T(8,128)(2,1)}) %all-gather.8.cloned.1.call-update) | async-done | bytes 13762576 | tf_op jit(solution)/shard_map/all_gather | solution.py:69
  742.5 109.2 %attend_backward.2 = (bf16[544,768]{1,0:T(8,128)(2,1)}, bf16[544,768]{1,0:T(8,128)(2,1)}, bf16[544,768]{1,0:T(8,128)(2,1)}) custom-call(s32[16]{0:T(128)} %get-tuple-element.139.meta, bf16[16,560,768]{2,1,0:T(8,128)(2,1)} %bitcast.91, bf16[4096,768]{1,0:T(8,128)(2,1)} %get-tuple-element.38.refs_1_, bf16[4096,768]{1,0:T(8,128)(2,1)} %get-tuple-element.39.refs_2_, ...), custom_call_target="tpu_custom_call" | custom-call | flops 89999998976 | bytes 30000000 | tf_op jit(solution)/shard_map/attend_backward/pallas_call | solution.py:428
  856.2 41.3 %attend_backward.3 = (bf16[544,768]{1,0:T(8,128)(2,1)}, bf16[544,768]{1,0:T(8,128)(2,1)}, bf16[544,768]{1,0:T(8,128)(2,1)}) custom-call(s32[16]{0:T(128)} %get-tuple-element.140.meta, bf16[16,560,768]{2,1,0:T(8,128)(2,1)} %bitcast.92, bf16[4096,768]{1,0:T(8,128)(2,1)} %get-tuple-element.45.refs_1_, bf16[4096,768]{1,0:T(8,128)(2,1)} %get-tuple-element.46.refs_2_, ...), custom_call_target="tpu_custom_call" | custom-call | flops 89999998976 | bytes 30000000 | tf_op jit(solution)/shard_map/attend_backward/pallas_call | solution.py:428
  916.7 3.6 collective-permute-done.33
  920.3 63.6 %collective-permute-start.34 = (f32[1536]{0:T(1024)S(1)}, f32[1536]{0:T(1024)S(1)}, u32[]{:S(2)}, u32[]{:S(2)}) collective-permute-start(f32[1536]{0:T(1024)S(1)} %add.479), channel_id=1, source_target_pairs={{0,2},{1,3},{2,0},{3,1},{4,6},{5,7},{6,4},{7,5},{8,10},{9,11},{10,... | collective-permute-start | bytes 18440 | tf_op jit(solution)/shard_map/ppermute | solution.py:659
  987.2 6.0 collective-permute-done.15
  993.1 14.5 %collective-permute-start.35 = (f32[1536]{0:T(1024)S(1)}, f32[1536]{0:T(1024)S(1)}, u32[]{:S(2)}, u32[]{:S(2)}) collective-permute-start(f32[1536]{0:T(1024)S(1)} %add.480), channel_id=1, source_target_pairs={{0,4},{1,5},{2,6},{3,7},{4,0},{5,1},{6,2},{7,3},{8,12},{9,13},{10,... | collective-permute-start | bytes 18440 | tf_op jit(solution)/shard_map/ppermute | solution.py:659
  1014.5 3.8 collective-permute-done.38
  1020.3 6.1 collective-permute-done.48
  1039.9 3.9 collective-permute-start.25
  1050.6 3.2 collective-permute-start.42
  1074.9 10.5 collective-permute-done.54
  1097.1 5.5 collective-permute-done.17
  (454 shorter events, 175.1 us)
Async XLA Ops:
  7.2 232.5 %all-gather.6.cloned.1.call-start = ((), (), s32[]{:S(2)}) async-start(), calls=%async_computation | async-start | bytes 13369344 | tf_op jit(solution)/shard_map/all_gather | solution.py:69
  10.1 622.8 %all-reduce.11.cloned.1.call-start = ((), (), s32[]{:S(2)}) async-start(), calls=%async_computation.3 | async-start | bytes 21282816 | tf_op jit(solution)/shard_map/psum | solution.py:623
  10.1 39.1 %collective-permute-start.2 = (bf16[512,768]{1,0:T(8,128)(2,1)S(1)}, bf16[512,768]{1,0:T(8,128)(2,1)S(1)}, u32[]{:S(2)}, u32[]{:S(2)}) collective-permute-start(bf16[512,768]{1,0:T(8,128)(2,1)S(1)} %get-tuple-element.104.refs_0_), channel_id=1, source_target_pairs={{4,0},{5,1},{6,2},{7,3},{8,4},{9,5},{10,6},{11,7},{12,8},{13,9},{1... | collective-permute-start | bytes 2359304 | tf_op jit(solution)/shard_map/ppermute | solution.py:52
  11.4 37.8 %collective-permute-start.1 = (bf16[512,768]{1,0:T(8,128)(2,1)S(1)}, bf16[512,768]{1,0:T(8,128)(2,1)}, u32[]{:S(2)}, u32[]{:S(2)}) collective-permute-start(bf16[512,768]{1,0:T(8,128)(2,1)S(1)} %get-tuple-element.104.refs_0_), channel_id=1, source_target_pairs={{0,4},{1,5},{2,6},{3,7},{4,8},{5,9},{6,10},{7,11},{8,12},{9,13},{1... | collective-permute-start | bytes 2359304 | tf_op jit(solution)/shard_map/ppermute | solution.py:52
  17.9 41.6 %collective-permute-start = (bf16[512,768]{1,0:T(8,128)(2,1)S(1)}, bf16[512,768]{1,0:T(8,128)(2,1)}, u32[]{:S(2)}, u32[]{:S(2)}) collective-permute-start(bf16[512,768]{1,0:T(8,128)(2,1)S(1)} %get-tuple-element.104.refs_0_), channel_id=1, source_target_pairs={{0,2},{1,3},{2,0},{3,1},{4,6},{5,7},{6,4},{7,5},{8,10},{9,11},{10,... | collective-permute-start | bytes 2359304 | tf_op jit(solution)/shard_map/ppermute | solution.py:52
  49.4 48.1 %collective-permute-start.5 = (bf16[512,768]{1,0:T(8,128)(2,1)S(1)}, bf16[512,768]{1,0:T(8,128)(2,1)}, u32[]{:S(2)}, u32[]{:S(2)}) collective-permute-start(bf16[512,768]{1,0:T(8,128)(2,1)S(1)} %broadcast_select_fusion), channel_id=1, source_target_pairs={{2,6},{3,7},{4,0},{5,1},{6,10},{7,11},{8,4},{9,5},{10,14},{11,15},... | collective-permute-start | bytes 2359304 | tf_op jit(solution)/shard_map/ppermute | solution.py:52
  50.7 49.8 %collective-permute-start.7 = (bf16[512,768]{1,0:T(8,128)(2,1)S(1)}, bf16[512,768]{1,0:T(8,128)(2,1)}, u32[]{:S(2)}, u32[]{:S(2)}) collective-permute-start(bf16[512,768]{1,0:T(8,128)(2,1)S(1)} %get-tuple-element.104.refs_0_), channel_id=1, source_target_pairs={{0,1},{1,0},{2,3},{3,2},{4,5},{5,4},{6,7},{7,6},{8,9},{9,8},{10,11... | collective-permute-start | bytes 2359304 | tf_op jit(solution)/shard_map/ppermute | solution.py:52
  58.9 41.7 %collective-permute-start.10 = (bf16[512,768]{1,0:T(8,128)(2,1)S(1)}, bf16[512,768]{1,0:T(8,128)(2,1)S(1)}, u32[]{:S(2)}, u32[]{:S(2)}) collective-permute-start(bf16[512,768]{1,0:T(8,128)(2,1)S(1)} %collective-permute-done.2.refs_3_), channel_id=1, source_target_pairs={{0,1},{1,0},{2,3},{3,2},{4,5},{5,4},{6,7},{7,6},{8,9},{9,8},{10,11... | collective-permute-start | bytes 2359304 | tf_op jit(solution)/shard_map/ppermute | solution.py:52
  59.5 82.8 %collective-permute-start.4 = (bf16[512,768]{1,0:T(8,128)(2,1)}, bf16[512,768]{1,0:T(8,128)(2,1)}, u32[]{:S(2)}, u32[]{:S(2)}) collective-permute-start(bf16[512,768]{1,0:T(8,128)(2,1)} %collective-permute-done.refs_1_), channel_id=1, source_target_pairs={{4,0},{5,1},{6,2},{7,3},{8,4},{9,5},{10,6},{11,7},{12,8},{13,9},{1... | collective-permute-start | bytes 2359304 | tf_op jit(solution)/shard_map/ppermute | solution.py:52
  60.8 81.5 %collective-permute-start.3 = (bf16[512,768]{1,0:T(8,128)(2,1)}, bf16[512,768]{1,0:T(8,128)(2,1)}, u32[]{:S(2)}, u32[]{:S(2)}) collective-permute-start(bf16[512,768]{1,0:T(8,128)(2,1)} %collective-permute-done.refs_1_), channel_id=1, source_target_pairs={{0,4},{1,5},{2,6},{3,7},{4,8},{5,9},{6,10},{7,11},{8,12},{9,13},{1... | collective-permute-start | bytes 2359304 | tf_op jit(solution)/shard_map/ppermute | solution.py:52
  97.5 45.2 %collective-permute-start.6 = (bf16[512,768]{1,0:T(8,128)(2,1)}, bf16[512,768]{1,0:T(8,128)(2,1)}, u32[]{:S(2)}, u32[]{:S(2)}) collective-permute-start(bf16[512,768]{1,0:T(8,128)(2,1)} %collective-permute-done.5), channel_id=1, source_target_pairs={{0,2},{1,3},{2,0},{3,1},{4,6},{5,7},{6,4},{7,5},{8,10},{9,11},{10,... | collective-permute-start | bytes 2359304 | tf_op jit(solution)/shard_map/ppermute | solution.py:52
  100.5 53.7 %collective-permute-start.9 = (bf16[512,768]{1,0:T(8,128)(2,1)}, bf16[512,768]{1,0:T(8,128)(2,1)}, u32[]{:S(2)}, u32[]{:S(2)}) collective-permute-start(bf16[512,768]{1,0:T(8,128)(2,1)} %collective-permute-done.1.refs_2_), channel_id=1, source_target_pairs={{0,1},{1,0},{2,3},{3,2},{4,5},{5,4},{6,7},{7,6},{8,9},{9,8},{10,11... | collective-permute-start | bytes 2359304 | tf_op jit(solution)/shard_map/ppermute | solution.py:52
  100.6 53.6 %collective-permute-start.8 = (bf16[512,768]{1,0:T(8,128)(2,1)}, bf16[512,768]{1,0:T(8,128)(2,1)}, u32[]{:S(2)}, u32[]{:S(2)}) collective-permute-start(bf16[512,768]{1,0:T(8,128)(2,1)} %collective-permute-done.refs_1_), channel_id=1, source_target_pairs={{0,1},{1,0},{2,3},{3,2},{4,5},{5,4},{6,7},{7,6},{8,9},{9,8},{10,11... | collective-permute-start | bytes 2359304 | tf_op jit(solution)/shard_map/ppermute | solution.py:52
  142.2 12.0 %collective-permute-start.12 = (bf16[512,768]{1,0:T(8,128)(2,1)}, bf16[512,768]{1,0:T(8,128)(2,1)}, u32[]{:S(2)}, u32[]{:S(2)}) collective-permute-start(bf16[512,768]{1,0:T(8,128)(2,1)} %collective-permute-done.4.refs_5_), channel_id=1, source_target_pairs={{0,1},{1,0},{2,3},{3,2},{4,5},{5,4},{6,7},{7,6},{8,9},{9,8},{10,11... | collective-permute-start | bytes 2359304 | tf_op jit(solution)/shard_map/ppermute | solution.py:52
  142.2 12.0 %collective-permute-start.11 = (bf16[512,768]{1,0:T(8,128)(2,1)}, bf16[512,768]{1,0:T(8,128)(2,1)}, u32[]{:S(2)}, u32[]{:S(2)}) collective-permute-start(bf16[512,768]{1,0:T(8,128)(2,1)} %collective-permute-done.3.refs_4_), channel_id=1, source_target_pairs={{0,1},{1,0},{2,3},{3,2},{4,5},{5,4},{6,7},{7,6},{8,9},{9,8},{10,11... | collective-permute-start | bytes 2359304 | tf_op jit(solution)/shard_map/ppermute | solution.py:52
  357.6 384.9 %all-gather.8.cloned.1.call-start = ((), (), s32[]{:S(2)}) async-start(), calls=%async_computation.1 | async-start | bytes 14622720 | tf_op jit(solution)/shard_map/all_gather | solution.py:69
  365.6 490.6 %all-gather.10.cloned.1.call-start = ((), (), s32[]{:S(2)}) async-start(), calls=%async_computation.2 | async-start | bytes 14622720 | tf_op jit(solution)/shard_map/all_gather | solution.py:69
  907.8 103.5 %collective-permute-start.37 = (bf16[384,768]{1,0:T(8,128)(2,1)S(1)}, bf16[384,768]{1,0:T(8,128)(2,1)S(1)}, u32[]{:S(2)}, u32[]{:S(2)}) collective-permute-start(bf16[384,768]{1,0:T(8,128)(2,1)S(1)} %constant_dynamic-slice_fusion.9), channel_id=1, source_target_pairs={{0,1},{1,0},{2,3},{3,2},{4,5},{5,4},{6,7},{7,6},{8,9},{9,8},{10,11... | collective-permute-start | bytes 1769480 | tf_op jit(solution)/shard_map/ppermute | solution.py:500
  912.2 71.7 %collective-permute-start.14 = (bf16[2,4,20,768]{3,1,2,0:T(4,128)(2,1)S(1)}, bf16[2,4,20,768]{3,1,2,0:T(4,128)(2,1)S(1)}, u32[]{:S(2)}, u32[]{:S(2)}) collective-permute-start(bf16[2,4,20,768]{3,1,2,0:T(4,128)(2,1)S(1)} %pad_maximum_fusion.6), channel_id=1, source_target_pairs={{0,1},{1,0},{2,3},{3,2},{4,5},{5,4},{6,7},{7,6},{8,9},{9,8},{10,11... | collective-permute-start | bytes 737288 | tf_op jit(solution)/shard_map/ppermute | solution.py:515
  916.3 68.0 %collective-permute-start.18 = (bf16[2,4,20,768]{3,1,2,0:T(4,128)(2,1)S(1)}, bf16[2,4,20,768]{3,1,2,0:T(4,128)(2,1)S(1)}, u32[]{:S(2)}, u32[]{:S(2)}) collective-permute-start(bf16[2,4,20,768]{3,1,2,0:T(4,128)(2,1)S(1)} %pad_maximum_fusion.7), channel_id=1, source_target_pairs={{0,1},{1,0},{2,3},{3,2},{4,5},{5,4},{6,7},{7,6},{8,9},{9,8},{10,11... | collective-permute-start | bytes 737288 | tf_op jit(solution)/shard_map/ppermute | solution.py:515
  920.3 66.4 %collective-permute-start.34 = (f32[1536]{0:T(1024)S(1)}, f32[1536]{0:T(1024)S(1)}, u32[]{:S(2)}, u32[]{:S(2)}) collective-permute-start(f32[1536]{0:T(1024)S(1)} %add.479), channel_id=1, source_target_pairs={{0,2},{1,3},{2,0},{3,1},{4,6},{5,7},{6,4},{7,5},{8,10},{9,11},{10,... | collective-permute-start | bytes 18440 | tf_op jit(solution)/shard_map/ppermute | solution.py:659
  984.5 23.4 %collective-permute-start.19 = (bf16[2,4,20,768]{3,1,2,0:T(4,128)(2,1)S(1)}, bf16[2,4,20,768]{3,1,2,0:T(4,128)(2,1)S(1)}, u32[]{:S(2)}, u32[]{:S(2)}) collective-permute-start(bf16[2,4,20,768]{3,1,2,0:T(4,128)(2,1)S(1)} %fusion.129), channel_id=1, source_target_pairs={{0,2},{1,3},{2,0},{3,1},{4,6},{5,7},{6,4},{7,5},{8,10},{9,11},{10,... | collective-permute-start | bytes 737288 | tf_op jit(solution)/shard_map/ppermute | solution.py:515
  986.6 24.9 %collective-permute-start.47 = (bf16[384,768]{1,0:T(8,128)(2,1)S(1)}, bf16[384,768]{1,0:T(8,128)(2,1)S(1)}, u32[]{:S(2)}, u32[]{:S(2)}) collective-permute-start(bf16[384,768]{1,0:T(8,128)(2,1)S(1)} %constant_dynamic-slice_fusion.4), channel_id=1, source_target_pairs={{0,1},{1,0},{2,3},{3,2},{4,5},{5,4},{6,7},{7,6},{8,9},{9,8},{10,11... | collective-permute-start | bytes 1769480 | tf_op jit(solution)/shard_map/ppermute | solution.py:500
  986.7 25.5 %collective-permute-start.22 = (bf16[384,768]{1,0:T(8,128)(2,1)S(1)}, bf16[384,768]{1,0:T(8,128)(2,1)S(1)}, u32[]{:S(2)}, u32[]{:S(2)}) collective-permute-start(bf16[384,768]{1,0:T(8,128)(2,1)S(1)} %constant_dynamic-slice_fusion.14), channel_id=1, source_target_pairs={{0,1},{1,0},{2,3},{3,2},{4,5},{5,4},{6,7},{7,6},{8,9},{9,8},{10,11... | collective-permute-start | bytes 1769480 | tf_op jit(solution)/shard_map/ppermute | solution.py:500
  993.1 93.1 %collective-permute-start.35 = (f32[1536]{0:T(1024)S(1)}, f32[1536]{0:T(1024)S(1)}, u32[]{:S(2)}, u32[]{:S(2)}) collective-permute-start(f32[1536]{0:T(1024)S(1)} %add.480), channel_id=1, source_target_pairs={{0,4},{1,5},{2,6},{3,7},{4,0},{5,1},{6,2},{7,3},{8,12},{9,13},{10,... | collective-permute-start | bytes 18440 | tf_op jit(solution)/shard_map/ppermute | solution.py:659
  1007.9 80.3 %collective-permute-start.16 = (bf16[2,4,20,768]{3,1,2,0:T(4,128)(2,1)S(1)}, bf16[2,4,20,768]{3,1,2,0:T(4,128)(2,1)S(1)}, u32[]{:S(2)}, u32[]{:S(2)}) collective-permute-start(bf16[2,4,20,768]{3,1,2,0:T(4,128)(2,1)S(1)} %fusion.177), channel_id=1, source_target_pairs={{0,4},{1,5},{2,6},{3,7},{4,0},{5,1},{6,2},{7,3},{8,12},{9,13},{10,... | collective-permute-start | bytes 737288 | tf_op jit(solution)/shard_map/ppermute | solution.py:515
  1011.3 79.4 %collective-permute-start.20 = (bf16[2,4,20,768]{3,1,2,0:T(4,128)(2,1)S(1)}, bf16[2,4,20,768]{3,1,2,0:T(4,128)(2,1)S(1)}, u32[]{:S(2)}, u32[]{:S(2)}) collective-permute-start(bf16[2,4,20,768]{3,1,2,0:T(4,128)(2,1)S(1)} %fusion.176), channel_id=1, source_target_pairs={{0,4},{1,5},{2,6},{3,7},{4,0},{5,1},{6,2},{7,3},{8,12},{9,13},{10,... | collective-permute-start | bytes 737288 | tf_op jit(solution)/shard_map/ppermute | solution.py:515
  1012.2 14.2 %collective-permute-start.48 = (bf16[192,768]{1,0:T(8,128)(2,1)S(1)}, bf16[192,768]{1,0:T(8,128)(2,1)S(1)}, u32[]{:S(2)}, u32[]{:S(2)}) collective-permute-start(bf16[192,768]{1,0:T(8,128)(2,1)S(1)} %constant_dynamic-slice_fusion.3), channel_id=1, source_target_pairs={{0,4},{1,5},{2,6},{3,7},{4,0},{5,1},{6,2},{7,3},{8,12},{9,13},{10,... | collective-permute-start | bytes 884744 | tf_op jit(solution)/shard_map/ppermute | solution.py:500
  1071.0 14.3 %collective-permute-start.54 = (bf16[96,768]{1,0:T(8,128)(2,1)S(1)}, bf16[96,768]{1,0:T(8,128)(2,1)S(1)}, u32[]{:S(2)}, u32[]{:S(2)}) collective-permute-start(bf16[96,768]{1,0:T(8,128)(2,1)S(1)} %maximum_select_fusion.11), channel_id=1, source_target_pairs={{0,8},{1,9},{2,10},{3,11},{4,12},{5,13},{6,14},{7,15},{8,0},{9,1},... | collective-permute-start | bytes 442376 | tf_op jit(solution)/shard_map/ppermute | solution.py:504
  1092.1 13.1 %collective-permute-start.21 = (bf16[2,4,20,768]{3,1,2,0:T(4,128)(2,1)S(1)}, bf16[2,4,20,768]{3,1,2,0:T(4,128)(2,1)S(1)}, u32[]{:S(2)}, u32[]{:S(2)}) collective-permute-start(bf16[2,4,20,768]{3,1,2,0:T(4,128)(2,1)S(1)} %add.454), channel_id=1, source_target_pairs={{0,8},{1,9},{2,10},{3,11},{4,12},{5,13},{6,14},{7,15},{8,0},{9,1},... | collective-permute-start | bytes 737288 | tf_op jit(solution)/shard_map/ppermute | solution.py:515
  1094.4 13.3 %collective-permute-start.31 = (bf16[384,768]{1,0:T(8,128)(2,1)S(1)}, bf16[384,768]{1,0:T(8,128)(2,1)S(1)}, u32[]{:S(2)}, u32[]{:S(2)}) collective-permute-start(bf16[384,768]{1,0:T(8,128)(2,1)S(1)} %maximum_select_fusion.3), channel_id=1, source_target_pairs={{0,1},{1,0},{2,3},{3,2},{4,5},{5,4},{6,7},{7,6},{8,9},{9,8},{10,11... | collective-permute-start | bytes 1769480 | tf_op jit(solution)/shard_map/ppermute | solution.py:504
  1095.1 14.2 %collective-permute-start.56 = (bf16[384,768]{1,0:T(8,128)(2,1)S(1)}, bf16[384,768]{1,0:T(8,128)(2,1)S(1)}, u32[]{:S(2)}, u32[]{:S(2)}) collective-permute-start(bf16[384,768]{1,0:T(8,128)(2,1)S(1)} %maximum_select_fusion.5), channel_id=1, source_target_pairs={{0,1},{1,0},{2,3},{3,2},{4,5},{5,4},{6,7},{7,6},{8,9},{9,8},{10,11... | collective-permute-start | bytes 1769480 | tf_op jit(solution)/shard_map/ppermute | solution.py:504
  (102 other events, 1174.0 us)
Sparse Core Ops, SparseCore 0:
  10.9 134.9 all-gather.5
  357.7 275.0 all-reduce.10
  635.4 107.0 all-gather.7
  745.5 106.3 all-gather.9

commit v2 on v1

--- a/solution.py
+++ b/solution.py
@@ -19,7 +19,11 @@
 CAP = NBLK * SEG
 OWN = SEG + MEMP
 STAT = 24
+BACK_COST = 10_000_000_000
+LATE_ROWS = 256
 NPIECE = 14
+ROWS = 32
+COLS = 512
 NEG = -1e30
 SHIFT_FREE = 60.0
 EPS = 1e-05
@@ -43,7 +47,13 @@
 
 UP = plane_moves(lambda side: 1)
 DOWN = plane_moves(lambda side: -1)
-OUTWARD = plane_moves(lambda side: 1 if side else -1)
+FAR = [
+    (4 * plane + place, 4 * target + (place ^ 2))
+    for plane in range(4)
+    for place in range(4)
+    for target in [plane + (2 if place >> 1 else -2)]
+    if 0 <= target < 4
+]
 SIDE = [(i, i ^ 2) for i in range(16)]
 CORE = [(i, i ^ 1) for i in range(16)]
 
@@ -52,17 +62,15 @@
     return lax.ppermute(value, "blk", pairs)
 
 
-def gather_near(value):
-    side = (lax.axis_index("blk") >> 1) & 1
-    below = move(value, UP)
-    above = move(value, DOWN)
-    beside = move(value, SIDE)
-    far = move(jnp.where(side == 1, below, above), OUTWARD)
-    beside_below = move(beside, UP)
-    beside_above = move(beside, DOWN)
-    beside_far = move(far, SIDE)
-    here = [value, beside, below, above, beside_below, beside_above, beside_far]
-    return here + [move(part, CORE) for part in here]
+def gather_near(value, hold=lambda stage, parts: parts):
+    below, above, beside, far = (move(value, pairs) for pairs in (UP, DOWN, SIDE, FAR))
+    below, above, beside, far = hold(0, [below, above, beside, far])
+    moved = [move(beside, UP), move(beside, DOWN)]
+    first = [move(part, CORE) for part in (value, beside, below, above, far)]
+    moved_and_first = hold(1, moved + first)
+    moved, first = moved_and_first[:2], moved_and_first[2:]
+    second = hold(2, [move(part, CORE) for part in moved])
+    return [value, beside, below, above, *moved, far] + first[:4] + second + first[4:]
 
 
 def gather_all(value):
@@ -157,14 +165,10 @@
         return carry
 
     lax.fori_loop(0, blocks // 4, four, 0)
-
-    @pl.when((blocks & 2) != 0)
-    def _():
-        run((blocks // 4) * 4, 2)
-
-    @pl.when((blocks & 1) != 0)
-    def _():
-        run((blocks // 2) * 2, 1)
+    for count in (1, 2, 3):
+        @pl.when(blocks % 4 == count)
+        def _():
+            run((blocks // 4) * 4, count)
 
 
 def span_of(first, count):
@@ -183,7 +187,7 @@
     @pl.when(quad == 0)
     def _():
         load_chain(meta, pieces, here, there, sems)
-        rows[0:MEMP, :] = mem[...]
+        rows[0:MEMP, :] = mem[meta[M_CHAIN]]
         lse[...] = jnp.zeros_like(lse)
 
         @pl.when(blocks > length)
@@ -293,7 +297,7 @@
             num_scalar_prefetch=1,
             grid=(NQUAD,),
             in_specs=[pl.BlockSpec(memory_space=pl.ANY)] * len(pieces)
-            + [whole((MEMP, width))]
+            + [whole((mem.shape[0], MEMP, width))]
             + [column(width)] * 3
             + [column(1)] * 2,
             out_specs=[column(OWN), whole((OWN, PAIR))] + [column(CAP)] * 3,
@@ -318,28 +322,29 @@
     )(meta, *pieces, mem, wq, wk, wv, bq.reshape(1, -1), bv.reshape(1, -1))
 
 
-def backward_body(meta, *refs):
-    pieces, refs = refs[:-23], refs[-23:]
+def backward_body(start, count, meta, *refs):
+    pieces, refs = refs[:-22], refs[-22:]
     (
-        kc, vc, qc, mem_grad, mem_stats, own_lse, own_delta,
+        kc, vc, qc, mem_grad, mem_stats, own_stats,
         dq, dk, dv,
         doc, stats, chain_stats, qown, kown, vown, down, bias, qacc, kacc, vacc, sems, stat_sems,
     ) = refs
-    quad = pl.program_id(0)
+    step = pl.program_id(0)
+    quad = start + step
     length = meta[M_LEN]
 
-    @pl.when(quad == 0)
+    @pl.when(step == 0)
     def _():
-        rows_from = lambda index: lambda ref: ref.at[0:SEG, pl.ds(index * QUAD, QUAD)]
+        rows_from = lambda index: lambda ref: ref.at[0:SEG, pl.ds((start + index) * QUAD, QUAD)]
         rows_to = lambda index: lambda spot: doc.at[index, pl.ds(MEMP + SEG * spot, SEG)]
         stat_from = lambda ref: ref.at[SEG : SEG + 2 * STAT, 0:SEG]
         stat_to = lambda spot: stats.at[spot]
         load_chain(meta, pieces, stat_from, stat_to, stat_sems)
-        for index in range(NQUAD):
+        for index in range(count):
             load_chain(meta, pieces, rows_from(index), rows_to(index), sems.at[index])
         bias[...] = key_bias(meta)
-        for index in range(NQUAD):
-            doc[index, 0:MEMP, :] = mem_grad[:, index * QUAD : (index + 1) * QUAD]
+        for index in range(count):
+            doc[index, 0:MEMP, :] = mem_grad[:, (start + index) * QUAD : (start + index + 1) * QUAD]
 
             @pl.when(meta[M_BLOCKS] > length)
             def _():
@@ -368,12 +373,13 @@
         beyond = jnp.where(entry < H, -NEG, 0.0)
         chain_stats[...] = jnp.where(column < MEMP + SEG * length, moved, beyond)
         lane = lax.broadcasted_iota(jnp.int32, (STAT, PAIR), 1)
-        chain_stats[:, 0:PAIR] = jnp.where(lane < MEMP, mem_stats[...], chain_stats[:, 0:PAIR])
-        for index in range(NQUAD):
+        at_front = pltpu.roll(mem_stats[...], MEMP, 1)
+        chain_stats[:, 0:PAIR] = jnp.where(lane < MEMP, at_front, chain_stats[:, 0:PAIR])
+        for index in range(count):
             wait_chain(meta, pieces, rows_from(index), rows_to(index), sems.at[index])
 
     place = pl.multiple_of(MEMP + SEG * meta[M_SPOT], MEMP)
-    for own, chain in ((qown, qc), (kown, kc), (vown, vc), (down, doc.at[quad])):
+    for own, chain in ((qown, qc), (kown, kc), (vown, vc), (down, doc.at[step])):
         own[0:SEG, :] = chain[pl.ds(place, SEG), :]
         own[SEG:OWN, :] = chain[0:MEMP, :]
 
@@ -384,13 +390,13 @@
         mine = (lane // HD) == (index % 2)
         masked = lambda ref: jnp.where(mine, ref[:, cols], jnp.zeros((OWN, PAIR), BF16))
         query, key, value, grad = masked(qown), masked(kown), masked(vown), masked(down)
-        pick = lambda ref: jnp.sum(jnp.where(lane == number, ref[...], 0.0), axis=1, keepdims=True)
-        log_total, delta = pick(own_lse), pick(own_delta)
+        pick = lambda at: jnp.sum(jnp.where(lane == at, own_stats[...], 0.0), axis=1, keepdims=True)
+        log_total, delta = pick(number), pick(H + number)
         for acc in (qacc, kacc, vacc):
             acc[...] = jnp.zeros_like(acc)
 
-        def run(first, count):
-            span = span_of(first, count)
+        def run(first, size):
+            span = span_of(first, size)
             keys, values = kc[span, cols], vc[span, cols]
             scores = lax.dot_general(query, keys, LAST, preferred_element_type=F32)
             weights = jnp.exp(scores + bias[0:1, span] - log_total)
@@ -398,7 +404,7 @@
             score_grad = (weights * (weight_grad - delta)).astype(BF16)
             qacc[...] += jnp.dot(score_grad, keys, preferred_element_type=F32)
 
-            queries, grads = qc[span, cols], doc[quad, span, cols]
+            queries, grads = qc[span, cols], doc[step, span, cols]
             scores = lax.dot_general(key, queries, LAST, preferred_element_type=F32)
             weights = jnp.exp(scores - chain_stats[pl.ds(number, 1), span])
             weight_grad = lax.dot_general(value, grads, LAST, preferred_element_type=F32)
@@ -421,21 +427,22 @@
     lax.fori_loop(0, 4, head, 0)
 
 
-def attend_backward(meta, pieces, chain, mem_grad, mem_stats, own_lse, own_delta):
+def attend_backward(meta, pieces, chain, mem_grad, mem_stats, own_stats, start, count):
     width = mem_grad.shape[1]
     whole = lambda shape: pl.BlockSpec(shape, lambda quad, meta: (0,) * len(shape))
-    column = lambda count: pl.BlockSpec((count, QUAD), lambda quad, meta: (0, quad))
+    chain_column = pl.BlockSpec((CAP, QUAD), lambda step, meta: (0, start + step))
+    own_column = pl.BlockSpec((OWN, QUAD), lambda step, meta: (0, step))
     return pl.pallas_call(
-        backward_body,
+        functools.partial(backward_body, start, count),
         grid_spec=pltpu.PrefetchScalarGridSpec(
             num_scalar_prefetch=1,
-            grid=(NQUAD,),
+            grid=(count,),
             in_specs=[pl.BlockSpec(memory_space=pl.ANY)] * len(pieces)
-            + [column(CAP)] * 3
-            + [whole((MEMP, width)), whole((STAT, PAIR)), whole((OWN, PAIR)), whole((OWN, PAIR))],
-            out_specs=[column(OWN)] * 3,
+            + [chain_column] * 3
+            + [whole((MEMP, width)), whole((STAT, PAIR)), whole((OWN, PAIR))],
+            out_specs=[own_column] * 3,
             scratch_shapes=[
-                pltpu.VMEM((NQUAD, CAP, QUAD), BF16),
+                pltpu.VMEM((count, CAP, QUAD), BF16),
                 pltpu.VMEM((LONG, 2 * STAT, SEG), BF16),
                 pltpu.VMEM((STAT, CAP), F32),
             ]
@@ -445,20 +452,20 @@
                 pltpu.VMEM((OWN, PAIR), F32),
                 pltpu.VMEM((OWN, PAIR), F32),
                 pltpu.VMEM((OWN, PAIR), F32),
-                pltpu.SemaphoreType.DMA((NQUAD, LONG)),
+                pltpu.SemaphoreType.DMA((count, LONG)),
                 pltpu.SemaphoreType.DMA((LONG,)),
             ],
         ),
-        out_shape=[jax.ShapeDtypeStruct((OWN, width), BF16)] * 3,
+        out_shape=[jax.ShapeDtypeStruct((OWN, count * QUAD), BF16)] * 3,
         compiler_params=pltpu.CompilerParams(vmem_limit_bytes=VMEM_LIMIT),
         cost_estimate=pl.CostEstimate(
-            flops=90_000_000_000, bytes_accessed=30_000_000, transcendentals=46_000_000
+            flops=BACK_COST, bytes_accessed=1_000_000, transcendentals=0
         ),
         name="attend_backward",
-    )(meta, *pieces, *chain, mem_grad, mem_stats, own_lse, own_delta)
-
-
-def normalize(values):
+    )(meta, *pieces, *chain, mem_grad, mem_stats, own_stats)
+
+
+def norm_stats(values):
     centered = values - jnp.mean(values, axis=-1, keepdims=True)
     scale = lax.rsqrt(jnp.mean(centered * centered, axis=-1, keepdims=True) + EPS)
     return centered * scale, scale
@@ -470,50 +477,326 @@
     return scale * (upstream - mean - normed * along)
 
 
-def gelu_both(values):
-    cdf = 0.5 * (1.0 + lax.erf(values * (2.0**-0.5)))
-    density = jnp.exp(-0.5 * values * values) * 0.3989422804014327
-    return values * cdf, cdf + values * density
-
-
-def times(left, right):
-    return jnp.dot(left, right, preferred_element_type=F32)
-
-
-def times_turned(left, right):
+def turned(left, right):
     return lax.dot_general(left, right, LAST, preferred_element_type=F32)
+
+
+def crossed(left, right):
+    return lax.dot_general(left, right, (((0,), (0,)), ((), ())), preferred_element_type=F32)
+
+
+def middle_body(
+    meta, attended, lse, tokens, memory, token_cot, memory_cot,
+    wo, bo, gain1, shift1, bi, b2, gain2, shift2, wi_from, w2_from,
+    final, final_mem, payload, mem_grad, mem_stats, own_stats, res_grad, rows,
+    attended_low, branch_out, first_low, inner_out, active, outer_out, sums, inner_sum,
+    wi, w2, first, norm1, scale1, total, second_grad, outer_grad, slope, weight_sems,
+):
+    width, inner_width = wi.shape
+    wi_copy = pltpu.make_async_copy(wi_from, wi, weight_sems.at[0])
+    w2_copy = pltpu.make_async_copy(w2_from, w2, weight_sems.at[1])
+    wi_copy.start()
+    w2_copy.start()
+    chain = meta[M_CHAIN]
+    lead = jnp.where(meta[M_SPOT] == 0, 1.0, 0.0)
+    rows[0:SEG, :] = tokens[...]
+    rows[SEG:OWN, :] = memory[chain]
+    attended_low[...] = attended[...].astype(BF16)
+    total[...] = jnp.dot(attended_low[...], wo[...], preferred_element_type=F32)
+    sums[...] = jnp.zeros_like(sums)
+    inner_sum[...] = jnp.zeros_like(inner_sum)
+    vector = lambda ref: ref[...].astype(F32)
+
+    def by_rows(run):
+        def step(index, carry):
+            start = pl.multiple_of(index * ROWS, ROWS)
+            row = start + lax.broadcasted_iota(jnp.int32, (ROWS, 1), 0)
+            live = (row < meta[M_USED]) | ((row >= SEG) & (row < SEG + meta[M_MEM]))
+            counted = jnp.where(row < SEG, 1.0, lead)
+            run(pl.ds(start, ROWS), live, counted)
+            return carry
+
+        lax.fori_loop(0, OWN // ROWS, step, 0)
+
+    def by_columns(run):
+        def step(index, carry):
+            run(pl.ds(pl.multiple_of(index * COLS, COLS), COLS))
+            return carry
+
+        lax.fori_loop(0, inner_width // COLS, step, 0)
+
+    def add(place, value):
+        sums[place : place + 1, :] += jnp.sum(value, axis=0, keepdims=True)
+
+    def first_part(span, live, counted):
+        value = rows[span, :].astype(F32) + total[span, :] + vector(bo)
+        normed, scale = norm_stats(value)
+        norm1[span, :] = normed
+        scale1[span, :] = jnp.broadcast_to(scale, (ROWS, PAIR))
+        value = normed * vector(gain1) + vector(shift1)
+        first[span, :] = value
+        first_low[span, :] = value.astype(BF16)
+
+    by_rows(first_part)
+    wi_copy.wait()
+    w2_copy.wait()
+    total[...] = jnp.zeros_like(total)
+
+    def inner_part(cols):
+        inner = jnp.dot(first_low[...], wi[:, cols], preferred_element_type=F32)
+        inner = inner + bi[:, cols].astype(F32)
+        cdf = 0.5 * (1.0 + lax.erf(inner * (2.0**-0.5)))
+        density = jnp.exp(-0.5 * inner * inner) * 0.3989422804014327
+        slope[:, cols] = cdf + inner * density
+        low = (inner * cdf).astype(BF16)
+        active[:, cols] = low
+        total[...] += jnp.dot(low, w2[cols, :], preferred_element_type=F32)
+
+    by_columns(inner_part)
+
+    def final_part(span, live, counted):
+        normed, scale = norm_stats(first[span, :] + total[span, :] + vector(b2))
+        value = jnp.where(live, normed * vector(gain2) + vector(shift2), 0.0)
+        rows_low = value.astype(BF16)
+        outer_out[span, :] = rows_low
+        start = span.start
+
+        @pl.when(start < SEG)
+        def _():
+            cot = token_cot[span, :].astype(F32)
+            first_back(span, live, counted, normed, scale, cot)
+
+        @pl.when(start >= SEG)
+        def _():
+            cot = memory_cot[chain].astype(F32)
+            first_back(span, live, counted, normed, scale, cot)
+
+    def first_back(span, live, counted, normed, scale, cot):
+        cot = jnp.where(live, cot, 0.0)
+        weighted = cot * counted
+        add(4, weighted * normed)
+        add(5, weighted)
+        grad = norm_back(normed, scale, cot * vector(gain2))
+        second_grad[span, :] = grad
+        outer_grad[span, :] = grad.astype(BF16)
+        add(3, grad.astype(BF16).astype(F32) * counted)
+
+    by_rows(final_part)
+    final[...] = outer_out[0:SEG, :]
+    final_mem[...] = outer_out[SEG:OWN, :]
+    outer_out[0:SEG, :] = outer_grad[0:SEG, :]
+    outer_out[SEG:OWN, :] = outer_grad[SEG:OWN, :] * lead.astype(BF16)
+    total[...] = jnp.zeros_like(total)
+
+    def inner_back(cols):
+        grad = (turned(outer_grad[...], w2[cols, :]) * slope[:, cols]).astype(BF16)
+        total[...] += turned(grad, wi[:, cols])
+        tail = grad[SEG:OWN] * lead.astype(BF16)
+        inner_out[0:SEG, cols] = grad[0:SEG]
+        inner_out[SEG:OWN, cols] = tail
+        inner_sum[:, cols] = jnp.sum(grad[0:SEG].astype(F32), axis=0, keepdims=True) + jnp.sum(
+            tail.astype(F32), axis=0, keepdims=True
+        )
+
+    by_columns(inner_back)
+
+    def last_part(span, live, counted):
+        grad = second_grad[span, :] + total[span, :]
+        normed = norm1[span, :]
+        weighted = grad * counted
+        add(1, weighted * normed)
+        add(2, weighted)
+        grad = norm_back(normed, scale1[span, 0:1], grad * vector(gain1))
+        res_grad[span, :] = grad
+        low = grad.astype(BF16)
+        outer_grad[span, :] = low
+        low = (low.astype(F32) * counted).astype(BF16)
+        branch_out[span, :] = low
+        add(0, low.astype(F32))
+
+    by_rows(last_part)
+    total[...] = turned(outer_grad[...], wo[...])
+    feature = lax.broadcasted_iota(jnp.int32, (width, PAIR), 0)
+    lane = lax.broadcasted_iota(jnp.int32, (width, PAIR), 1)
+    head_of = jnp.where(feature // HD == lane - H, 1.0, 0.0).astype(BF16)
+
+    def delta_part(span, live, counted):
+        low = total[span, :].astype(BF16)
+        outer_grad[span, :] = low
+        product = low.astype(F32) * attended[span, :]
+        high = product.astype(BF16)
+        rest = (product - high.astype(F32)).astype(BF16)
+        delta = jnp.dot(high, head_of, preferred_element_type=F32)
+        delta = delta + jnp.dot(rest, head_of, preferred_element_type=F32)
+        own_stats[span, :] = lse[span, :] + delta
+
+    by_rows(delta_part)
+    payload[0:SEG, :] = outer_grad[0:SEG, :]
+    mem_grad[...] = outer_grad[SEG:OWN, :]
+    stats = jnp.transpose(own_stats[0:SEG, :])[0:STAT]
+    high = stats.astype(BF16)
+    rest = (stats - high.astype(F32)).astype(BF16)
+    both = jnp.concatenate([high.astype(F32), rest.astype(F32)], 0).astype(BF16)
+    payload[SEG : SEG + 2 * STAT, 0:SEG] = both
+    payload[SEG : SEG + 2 * STAT, SEG:width] = jnp.zeros((2 * STAT, width - SEG), BF16)
+    mem_stats[...] = jnp.transpose(own_stats[OWN - PAIR : OWN, :])[0:STAT]
+
+
+def middle(meta, attended, lse, tokens, memory, token_cot, memory_cot, weights):
+    wo, bo, gain1, shift1, wi, bi, w2, b2, gain2, shift2 = weights
+    width, inner_width = wi.shape
+    vmem, line = pl.BlockSpec(memory_space=pltpu.VMEM), lambda value: value.reshape(1, -1)
+    hbm = pl.BlockSpec(memory_space=pl.ANY)
+    shape = jax.ShapeDtypeStruct
+    return pl.pallas_call(
+        middle_body,
+        in_specs=[pl.BlockSpec(memory_space=pltpu.SMEM)] + [vmem] * 14 + [hbm] * 2,
+        out_specs=[vmem] * 16,
+        out_shape=[
+            shape((SEG, width), BF16),
+            shape((MEMP, width), BF16),
+            shape((SEG + 2 * STAT, width), BF16),
+            shape((MEMP, width), BF16),
+            shape((STAT, PAIR), F32),
+            shape((OWN, PAIR), F32),
+            shape((OWN, width), F32),
+            shape((OWN, width), BF16),
+            shape((OWN, width), BF16),
+            shape((OWN, width), BF16),
+            shape((OWN, width), BF16),
+            shape((OWN, inner_width), BF16),
+            shape((OWN, inner_width), BF16),
+            shape((OWN, width), BF16),
+            shape((8, width), F32),
+            shape((1, inner_width), F32),
+        ],
+        scratch_shapes=[
+            pltpu.VMEM((width, inner_width), BF16),
+            pltpu.VMEM((inner_width, width), BF16),
+            pltpu.VMEM((OWN, width), F32),
+            pltpu.VMEM((OWN, width), F32),
+            pltpu.VMEM((OWN, PAIR), F32),
+            pltpu.VMEM((OWN, width), F32),
+            pltpu.VMEM((OWN, width), F32),
+            pltpu.VMEM((OWN, width), BF16),
+            pltpu.VMEM((OWN, inner_width), F32),
+            pltpu.SemaphoreType.DMA((2,)),
+        ],
+        compiler_params=pltpu.CompilerParams(vmem_limit_bytes=VMEM_LIMIT),
+        cost_estimate=pl.CostEstimate(
+            flops=12_000_000_000, bytes_accessed=40_000_000, transcendentals=2_000_000
+        ),
+        name="middle",
+    )(
+        meta, attended, lse, tokens, memory, token_cot, memory_cot,
+        wo, line(bo), line(gain1), line(shift1), line(bi), line(b2), line(gain2), line(shift2),
+        wi, w2,
+    )
+
+
+def late_body(metas, group, *refs, batches, chains, parts):
+    refs = list(refs)
+    take = lambda count: [refs.pop(0) for _ in range(count)]
+    rows, res_mem = take(batches), take(batches)
+    grads = [[take(len(parts[b])) for _ in range(3)] for b in range(batches)]
+    weights = take(3)
+    out, masked = take(2)
+    width = weights[0].shape[0]
+    out[3 * width :, :] = jnp.zeros((out.shape[0] - 3 * width, width), BF16)
+    for b in range(batches):
+        lead = jnp.where(metas[b, M_SPOT] == 0, 1.0, 0.0)
+        masked[b, 0:SEG, :] = rows[b][0:SEG, :]
+        masked[b, SEG:OWN, :] = rows[b][SEG:OWN, :] * lead.astype(BF16)
+        grad = res_mem[b][SEG:OWN, :]
+        for k in range(3):
+            first = 0
+            for part, ref in zip(parts[b], grads[b][k]):
+                grad = grad + turned(ref[SEG:OWN, :], weights[k][:, first : first + part])
+                first += part
+        place = ((group[0] * batches + b) * chains + metas[b, M_CHAIN]) * MEMP
+        place = pl.multiple_of(3 * width + 16 + place, 16)
+        out[pl.ds(place, MEMP), :] = (grad * lead).astype(BF16)
+    cuts = sorted({sum(p[:i]) for p in parts for i in range(len(p) + 1)})
+    for k in range(3):
+        for low, high in zip(cuts[:-1], cuts[1:]):
+            total, line = None, None
+            for b in range(batches):
+                lead = jnp.where(metas[b, M_SPOT] == 0, 1.0, 0.0)
+                first = 0
+                for part, ref in zip(parts[b], grads[b][k]):
+                    if first <= low and high <= first + part:
+                        grad = ref[:, low - first : high - first]
+                    first += part
+                value = crossed(masked[b], grad)
+                total = value if total is None else total + value
+                if k != 1:
+                    grad = grad.astype(F32)
+                    value = jnp.sum(grad[0:SEG], 0, keepdims=True)
+                    value = value + jnp.sum(grad[SEG:OWN], 0, keepdims=True) * lead
+                    line = value if line is None else line + value
+            out[k * width : (k + 1) * width, low:high] = total.astype(BF16)
+            if k != 1:
+                row = lax.broadcasted_iota(jnp.int32, (16, high - low), 0)
+                span = slice(3 * width, 3 * width + 16)
+                old = out[span, low:high].astype(F32)
+                out[span, low:high] = jnp.where(row == k // 2, line, old).astype(BF16)
+
+
+def late_sums(metas, group, groups, chains, rows, res, grads, weights):
+    batches, width = len(rows), weights[0].shape[0]
+    parts = [[part.shape[1] for part in one[0]] for one in grads]
+    count = 3 * width + 16 + groups * batches * chains * MEMP
+    count += -count % LATE_ROWS
+    vmem, smem = pl.BlockSpec(memory_space=pltpu.VMEM), pl.BlockSpec(memory_space=pltpu.SMEM)
+    flat = [part for one in grads for name in one for part in name]
+    return pl.pallas_call(
+        functools.partial(late_body, batches=batches, chains=chains, parts=parts),
+        in_specs=[smem] * 2 + [vmem] * (2 * batches + len(flat) + 3),
+        out_specs=vmem,
+        out_shape=jax.ShapeDtypeStruct((count, width), BF16),
+        scratch_shapes=[pltpu.VMEM((batches, OWN, width), BF16)],
+        compiler_params=pltpu.CompilerParams(vmem_limit_bytes=VMEM_LIMIT),
+        name="late_sums",
+    )(metas, group.reshape(1), *rows, *res, *flat, *weights)
 
 
 def weight_grad(left, right):
     return lax.dot_general(left, right, (((0,), (0,)), ((), ())), preferred_element_type=F32)
 
 
-def sum_over(value, steps):
-    taken = []
-    for axis, bit in steps:
-        count = lax.axis_size(axis)
-        pairs = [(i, i ^ bit) for i in range(count)]
-        half = value.shape[0] // 2
-        upper = (lax.axis_index(axis) // bit) % 2
-        keep = lax.dynamic_slice_in_dim(value, upper * half, half)
-        send = lax.dynamic_slice_in_dim(value, (1 - upper) * half, half)
-        got = lax.ppermute(send, axis, pairs)
-        value = (keep.astype(F32) + got.astype(F32)).astype(value.dtype)
-        taken.append((axis, pairs, upper))
-    for axis, pairs, upper in reversed(taken):
-        got = lax.ppermute(value, axis, pairs)
-        value = jnp.where(
-            upper == 0,
-            jnp.concatenate([value, got], 0),
-            jnp.concatenate([got, value], 0),
-        )
-    return value
-
-
-def spread(value):
-    for bit in (1, 2, 4, 8):
-        value = value + lax.ppermute(value, "blk", [(i, i ^ bit) for i in range(16)])
-    return value
+def swap(value, mask):
+    sizes = lax.axis_size("dp") * lax.axis_size("blk")
+    return lax.ppermute(value, ("dp", "blk"), [(i, i ^ mask) for i in range(sizes)])
+
+
+def sum_everywhere(value, beside):
+    blk = lax.axis_size("blk")
+    place = lax.axis_index("dp") * blk + lax.axis_index("blk")
+    groups = [(1,), (2, blk), (4, 8)]
+    bit = 2 * blk
+    while bit < blk * lax.axis_size("dp"):
+        groups.append((bit,))
+        bit *= 2
+    masks_of = lambda group: [
+        sum(bit for i, bit in enumerate(group) if (k >> i) & 1) for k in range(1 << len(group))
+    ]
+    own_of = lambda group: sum(((place // bit) % 2) << i for i, bit in enumerate(group))
+    for group in groups:
+        masks, own = masks_of(group), own_of(group)
+        size = value.shape[0] // len(masks)
+        part = lambda k: lax.dynamic_slice_in_dim(value, (own ^ k) * size, size)
+        got = [swap(part(k), mask) for k, mask in enumerate(masks) if k]
+        value = sum((g.astype(F32) for g in got), part(0).astype(F32)).astype(BF16)
+    for index, group in enumerate(reversed(groups)):
+        if index + 1 == len(groups):
+            value, beside = lax.optimization_barrier((value, beside))
+        masks, own = masks_of(group), own_of(group)
+        size = value.shape[0]
+        got = [value] + [swap(value, mask) for mask in masks[1:]]
+        value = jnp.zeros((size * len(masks), value.shape[1]), BF16)
+        for k, part in enumerate(got):
+            value = lax.dynamic_update_slice_in_dim(value, part, (own ^ k) * size, 0)
+    return value, beside
 
 
 def local(
@@ -523,86 +806,44 @@
     final_gain, final_shift, token_cotangent, memory_cotangent,
 ):
     own = lax.axis_index("blk").astype(jnp.int32)
+    group = lax.axis_index("dp").astype(jnp.int32)
+    groups = lax.axis_size("dp")
     batches, _, width = tokens.shape
     chains, mem_rows = memory.shape[1:3]
-    pad_mem = ((0, MEMP - mem_rows), (0, 0))
-    head_of = (jnp.arange(width)[:, None] // HD == jnp.arange(PAIR)[None, :]).astype(F32)
-    row = jnp.arange(OWN)
+    pad_mem = ((0, 0), (0, 0), (0, MEMP - mem_rows), (0, 0))
+    memory, memory_cotangent = jnp.pad(memory, pad_mem), jnp.pad(memory_cotangent, pad_mem)
 
     metas = metas_of(own, chain_lengths[:, 0], last_fill[:, 0], mem_rows)
-    pieces = [gather_near(tokens[0])] + [gather_all(tokens[b]) for b in range(1, batches)]
-
-    states, token_outs, memory_outs = [], [], []
+    near = gather_near(tokens[0])
+    later, near = lax.optimization_barrier(([tokens[b] for b in range(1, batches)], near))
+    pieces = [near] + [gather_all(part) for part in later]
+    meta_of = [metas[b] for b in range(batches)]
+
+    states = []
     for b in range(batches):
-        meta = metas[b]
-        chain, spot, used = meta[M_CHAIN], meta[M_SPOT], meta[M_USED]
-        mem = jnp.pad(lax.dynamic_index_in_dim(memory[b], chain, keepdims=False), pad_mem)
+        meta = meta_of[b]
         attended, lse, *chain_rows = attend_forward(
-            meta, pieces[b], mem, (query_proj, query_bias, key_proj, value_proj, value_bias)
+            meta, pieces[b], memory[b], (query_proj, query_bias, key_proj, value_proj, value_bias)
         )
-        rows = jnp.concatenate([tokens[b], mem], 0)
-        live = ((row < used) | ((row >= SEG) & (row < SEG + mem_rows))).astype(F32)[:, None]
-        lead = (spot == 0).astype(F32)
-        counted = jnp.where(row < SEG, 1.0, lead).astype(F32)[:, None]
-        counted_low = counted.astype(BF16)
-        attended_low = attended.astype(BF16)
-        first_sum = rows.astype(F32) + times(attended_low, output_proj) + output_bias
-        first_norm, first_scale = normalize(first_sum)
-        first = first_norm * attn_gain + attn_shift
-        first_low = first.astype(BF16)
-        inner = times(first_low, inner_proj) + inner_bias
-        active, slope = gelu_both(inner)
-        active_low = active.astype(BF16)
-        second_sum = first + times(active_low, outer_proj) + outer_bias
-        final_norm, final_scale = normalize(second_sum)
-        final = ((final_norm * final_gain + final_shift) * live).astype(BF16)
-        token_outs.append(final[:SEG])
-        hot = ((jnp.arange(chains) == chain) & (spot == 0))[:, None, None]
-        to_all = lambda value, hot=hot: jnp.where(hot, value[SEG : SEG + mem_rows][None], 0).astype(BF16)
-        memory_outs.append(to_all(final))
-
-        mem_cot = jnp.pad(
-            lax.dynamic_index_in_dim(memory_cotangent[b], chain, keepdims=False), pad_mem
+        (
+            final, final_mem, payload, mem_grad, mem_stats, own_stats, res_grad, rows,
+            attended_low, branch, first_low, inner, active, outer, sums, inner_sum,
+        ) = middle(
+            meta, attended, lse, tokens[b], memory[b], token_cotangent[b], memory_cotangent[b],
+            (
+                output_proj, output_bias, attn_gain, attn_shift, inner_proj, inner_bias,
+                outer_proj, outer_bias, final_gain, final_shift,
+            ),
         )
-        cotangent = jnp.concatenate([token_cotangent[b], mem_cot], 0).astype(F32) * live
-        weighted = cotangent * counted
-        grad_final_gain = jnp.sum(weighted * final_norm, 0)
-        grad_final_shift = jnp.sum(weighted, 0)
-        second_grad = norm_back(final_norm, final_scale, cotangent * final_gain)
-        outer_grad = second_grad.astype(BF16)
-        outer_counted = outer_grad * counted_low
-        inner_grad = (times_turned(outer_grad, outer_proj) * slope).astype(BF16)
-        inner_counted = inner_grad * counted_low
-        first_grad = second_grad + times_turned(inner_grad, inner_proj)
-        weighted = first_grad * counted
-        grad_attn_gain = jnp.sum(weighted * first_norm, 0)
-        grad_attn_shift = jnp.sum(weighted, 0)
-        res_grad = norm_back(first_norm, first_scale, first_grad * attn_gain)
-        branch_grad = res_grad.astype(BF16)
-        branch_counted = branch_grad * counted_low
-        attended_grad = times_turned(branch_grad, output_proj).astype(BF16)
-        delta = jnp.dot(
-            attended_grad.astype(F32) * attended, head_of, precision=lax.Precision.HIGHEST
-        )
-        stats = jnp.concatenate([lse[:, :H], delta[:, :H]], 1).T
-        high = lax.reduce_precision(stats[:, :SEG], 8, 7)
-        both = jnp.concatenate([high, stats[:, :SEG] - high], 0).astype(BF16)
-        payload = jnp.concatenate(
-            [attended_grad[:SEG], jnp.pad(both, ((0, 0), (0, width - SEG)))], 0
-        )
+        if b + 1 < batches:
+            meta_of[b + 1], payload = lax.optimization_barrier((meta_of[b + 1], payload))
         states.append(
             dict(
-                meta=meta, rows=rows, counted=counted_low, chain_rows=chain_rows, lse=lse,
-                delta=delta, payload=gather_all(payload), mem_grad=attended_grad[SEG:],
-                mem_stats=jnp.pad(stats[:, SEG:], ((0, 0), (0, PAIR - MEMP))),
-                res_grad=res_grad, to_all=to_all,
-                attended_low=attended_low, branch=branch_counted, first_low=first_low,
-                inner=inner_counted, active=active_low, outer=outer_counted,
-                small=[
-                    jnp.sum(branch_counted.astype(F32), 0), grad_attn_gain, grad_attn_shift,
-                    jnp.sum(inner_counted.astype(F32), 0), jnp.sum(outer_counted.astype(F32), 0),
-                    grad_final_gain, grad_final_shift,
-                ],
+                meta=meta, rows=rows, chain_rows=chain_rows, payload=payload, mem_grad=mem_grad,
+                mem_stats=mem_stats, own_stats=own_stats, res_grad=res_grad, final=final,
+                final_mem=final_mem, attended_low=attended_low, branch=branch,
+                first_low=first_low, inner=inner, active=active, outer=outer, sums=sums,
+                inner_sum=inner_sum,
             )
         )
 
@@ -612,86 +853,99 @@
             jnp.concatenate([s[right] for s in states], 0),
         ).astype(BF16)
 
-    small = jnp.concatenate([sum(s["small"][i] for s in states) for i in range(7)])
+    slots = (jnp.arange(groups)[:, None, None, None, None] == group) & (
+        jnp.arange(chains)[:, None, None]
+        == jnp.where(metas[:, M_SPOT] == 0, metas[:, M_CHAIN], -1)[:, None, None, None]
+    )
+    final_mem = jnp.stack([s["final_mem"] for s in states])[None, :, None]
     early = (
         over_batches("first_low", "inner"),
         over_batches("active", "outer"),
+        over_batches("attended_low", "branch"),
         jnp.concatenate(
-            [over_batches("attended_low", "branch"), small.astype(BF16).reshape(-1, width)], 0
+            [
+                jnp.where(slots, final_mem, 0).astype(BF16).reshape(-1, width),
+                sum(s["sums"] for s in states).astype(BF16),
+                sum(s["inner_sum"] for s in states).astype(BF16).reshape(-1, width),
+            ],
+            0,
         ),
     )
-    grad_inner, grad_outer, grad_output = lax.psum(early, ("dp", "blk"))
-    small = grad_output[width:].reshape(-1)
-    grad_output = grad_output[:width]
-
-    memory_out = spread(jnp.stack(memory_outs))
-
-    token_grads, memory_grads = [], []
+    early, *held = lax.optimization_barrier((early, *[s["meta"] for s in states]))
+    for s, meta in zip(states, held):
+        s["meta"] = meta
+    early = lax.psum(early, ("dp", "blk"))
+
+    def backward(s, payload, *quads):
+        return attend_backward(
+            s["meta"], payload, s["chain_rows"], s["mem_grad"], s["mem_stats"], s["own_stats"],
+            *quads,
+        )
+
+    def hold(stage, parts):
+        got = [backward(s, s["gathered"], stage, 1) for s in states[:-1]]
+        got, parts = lax.optimization_barrier((got, parts))
+        for s, grads in zip(states, got):
+            s["grads"] = [old + [new] for old, new in zip(s.get("grads", [[]] * 3), grads)]
+        return parts
+
+    for s in states[:-1]:
+        s["gathered"] = gather_all(s["payload"])
+    last = states[-1]
+    near = gather_near(last["payload"], hold)
+    last["grads"] = [[grad] for grad in backward(last, near, 0, NQUAD)]
+    last["grads"], early = lax.optimization_barrier((last["grads"], early))
+    grad_inner, grad_outer, grad_output, rest = early
+    late = late_sums(
+        metas, group, groups, chains, [s["rows"] for s in states],
+        [s["res_grad"] for s in states], [s["grads"] for s in states],
+        (query_proj, key_proj, value_proj),
+    )
+
+    def own_slots(rows):
+        rows = rows.reshape(groups, batches, chains, MEMP, width)
+        return lax.dynamic_index_in_dim(rows, group, keepdims=False)[:, :, :mem_rows]
+
+    wide_early = [part.astype(F32) for part in (grad_inner, grad_outer, grad_output)]
+    late, (grad_inner, grad_outer, grad_output) = sum_everywhere(late, wide_early)
+    grad_query, grad_key, grad_value = (late[i * width : (i + 1) * width] for i in range(3))
+    biases = late[3 * width : 3 * width + 2].astype(F32)
+    count = groups * batches * chains * MEMP
+    memory_grad = own_slots(late[3 * width + 16 : 3 * width + 16 + count])
+    memory_out = own_slots(rest[:count])
+    sums, inner_sum = rest[count : count + 8], rest[count + 8 :].reshape(1, -1)
+    token_outs = [s["final"] for s in states]
+    token_grads = []
     for s in states:
-        s["dq"], s["dk"], s["dv"] = attend_backward(
-            s["meta"], s["payload"], s["chain_rows"], s["mem_grad"], s["mem_stats"],
-            s["lse"], s["delta"],
-        )
-        for name in ("dq", "dk", "dv"):
-            s[name + "_counted"] = s[name] * s["counted"]
-
-    dp = lax.axis_size("dp")
-    on_dp = [("dp", 1 << i) for i in range(dp.bit_length() - 1)]
-    on_core, on_side, on_plane = [("blk", 1)], [("blk", 2)], [("blk", 4), ("blk", 8)]
-    orders = (
-        on_core + on_dp + on_side + on_plane,
-        on_core + on_side + on_plane + on_dp,
-        on_core + on_plane + on_dp + on_side,
-    )
-    grad_query, grad_key, grad_value = (
-        sum_over(over_batches("rows", name + "_counted"), steps)
-        for name, steps in zip(("dq", "dk", "dv"), orders)
-    )
-    biases = jnp.concatenate(
-        [
-            sum(jnp.sum(s[name + "_counted"].astype(F32), 0) for s in states)
-            for name in ("dq", "dv")
-        ]
-    )
-    for steps in (on_core, on_dp, on_side, on_plane):
-        for axis, bit in steps:
-            pairs = [(i, i ^ bit) for i in range(lax.axis_size(axis))]
-            biases = biases + lax.ppermute(biases, axis, pairs)
-
-    for s in states:
-        grad = (
-            s["res_grad"]
-            + times_turned(s["dq"], query_proj)
-            + times_turned(s["dk"], key_proj)
-            + times_turned(s["dv"], value_proj)
-        )
-        token_grads.append(grad[:SEG].astype(BF16))
-        memory_grads.append(s["to_all"](grad))
-    memory_grad = spread(jnp.stack(memory_grads))
+        grad = s["res_grad"][:SEG]
+        for parts, weights in zip(s["grads"], (query_proj, key_proj, value_proj)):
+            first = 0
+            for part in parts:
+                grad = grad + turned(part[:SEG], weights[:, first : first + part.shape[1]])
+                first += part.shape[1]
+        token_grads.append(grad.astype(BF16))
 
     wide = lambda value: value.astype(F32)
-    cut = lambda first, count: wide(small[first : first + count])
-    inner_width = inner_proj.shape[1]
     return (
         jnp.stack(token_outs),
         memory_out,
         jnp.stack(token_grads),
         memory_grad,
         wide(grad_query),
-        biases[:width],
+        biases[0],
         wide(grad_key),
         wide(grad_value),
-        biases[width:],
+        biases[1],
         wide(grad_output),
-        cut(0, width),
-        cut(width, width),
-        cut(2 * width, width),
+        wide(sums[0]),
+        wide(sums[1]),
+        wide(sums[2]),
         wide(grad_inner),
-        cut(3 * width, inner_width),
+        wide(inner_sum[0]),
         wide(grad_outer),
-        cut(3 * width + inner_width, width),
-        cut(4 * width + inner_width, width),
-        cut(5 * width + inner_width, width),
+        wide(sums[3]),
+        wide(sums[4]),
+        wide(sums[5]),
     )
 
 

time: 1120 us -> 822 us (0.73)
  waiting for transfers between devices: 493 us -> 280 us
  matrix products: 90.3 us -> 29.2 us
  Pallas kernels: 264 us -> 298 us
  other arithmetic: 58.2 us -> 25 us
  starting transfers between devices: 159 us -> 146 us
    psum x1, waiting for transfers between devices: 253 us -> 63.7 us  [local(): early = lax.psum(early, ('dp', 'blk'))]
    ppermute x43 -> x14, starting transfers between devices: 130 us -> 51.5 us  [swap(): lax.ppermute(value, ('dp', 'blk'), [(i, i ^ mask) for i in range(sizes)])]
    ppermute x14 -> x26, starting transfers between devices: 29 us -> 94 us  [move(): return lax.ppermute(value, 'blk', pairs)]
    pallas_call x2 -> x7, Pallas kernels: 150 us -> 214 us  [the longest x4 118 us: attend_backward(): pl.pallas_call(functools.partial(backward_body, start, count), grid_spec=...]
    dot_general x20 -> x12, matrix products: 64.5 us -> 8.99 us  [turned(): return lax.dot_general(left, right, LAST, preferred_element_type=F32)]
    all_gather x3 -> x2, waiting for transfers between devices: 94.2 us -> 48.2 us  [gather_all(): return [lax.all_gather(value, 'blk')]]
    pallas_call x2, Pallas kernels: 113 us -> 82.1 us  [attend_forward(): pl.pallas_call(forward_body, grid_spec=pltpu.PrefetchScalarGridSpec(num_s...]
    ppermute x14 -> x26, waiting for transfers between devices: 92.4 us -> 118 us  [move(): return lax.ppermute(value, 'blk', pairs)]
  transfers between devices with their start and end apart: 61 -> 43, of which waited for: 24 -> 20; matrix products, arithmetic and copies ran while one was open for 7% -> 8% of each run, Pallas kernels for 17% -> 34%
where the time goes in v2:
time: 822 us; the launch traced here: 824 us
  Pallas kernels  298 us (36%)
  waiting for transfers between devices  280 us (34%)
  starting transfers between devices  146 us (18%)
  local copies, waits for them, and re-layouts  29.6 us (4%)
  matrix products  29.2 us (4%)
  other arithmetic  25 us (3%)
  between operations  15.4 us (2%)
    pallas_call x4, Pallas kernels, attend_backward(): pl.pallas_call(functools.partial(backward_body, start, count), grid_spec=...  118 us
    ppermute x26, waiting for transfers between devices, move(): return lax.ppermute(value, 'blk', pairs)  118 us
    ppermute x26, starting transfers between devices, move(): return lax.ppermute(value, 'blk', pairs)  94 us
    pallas_call x2, Pallas kernels, attend_forward(): pl.pallas_call(forward_body, grid_spec=pltpu.PrefetchScalarGridSpec(num_s...  82.1 us
    pallas_call x2, Pallas kernels, middle(): pl.pallas_call(middle_body, in_specs=[pl.BlockSpec(memory_space=pltpu.SME...  81.3 us
    psum x1, waiting for transfers between devices, local(): early = lax.psum(early, ('dp', 'blk'))  63.7 us
    ppermute x14, starting transfers between devices, swap(): lax.ppermute(value, ('dp', 'blk'), [(i, i ^ mask) for i in range(sizes)])  51.5 us
    ppermute x14, waiting for transfers between devices, swap(): lax.ppermute(value, ('dp', 'blk'), [(i, i ^ mask) for i in range(sizes)])  50.9 us
  transfers between devices with their start and end apart: 43, of which 20 were waited for; matrix products, arithmetic and copies ran while one was open for 8% of the time, Pallas kernels for 34%

profile of v2, /device:TPU:0, one launch (start us, length us, event | category | flops | bytes accessed | tf_op | source)
XLA Modules:
  0.0 823.6 jit_solution(5768562462019496757)
XLA Ops:
  18.4 11.9 %collective-permute-done.refs_1_ = bf16[512,768]{1,0:T(8,128)(2,1)S(1)} collective-permute-done((bf16[512,768]{1,0:T(8,128)(2,1)S(1)}, bf16[512,768]{1,0:T(8,128)(2,1)S(1)}, u32[]{:S(2)}, u32[]{:S(2)}) %collective-permute-start) | collective-permute-done | bytes 786464 | tf_op jit(solution)/shard_map/ppermute | solution.py:62
  30.4 3.8 collective-permute-start.3
  38.4 11.6 %collective-permute-done.3.refs_4_ = bf16[512,768]{1,0:T(8,128)(2,1)S(1)} collective-permute-done((bf16[512,768]{1,0:T(8,128)(2,1)S(1)}, bf16[512,768]{1,0:T(8,128)(2,1)S(1)}, u32[]{:S(2)}, u32[]{:S(2)}) %collective-permute-start.3) | collective-permute-done | bytes 786464 | tf_op jit(solution)/shard_map/ppermute | solution.py:62
  50.0 5.7 collective-permute-done.4.refs_5_
  70.4 31.1 %attend_forward.2 = (f32[544,768]{1,0:T(8,128)}, f32[544,128]{1,0:T(8,128)}, bf16[4096,768]{1,0:T(8,128)(2,1)}, bf16[4096,768]{1,0:T(8,128)(2,1)}, bf16[4096,768]{1,0:T(8,128)(2,1)}) custom-call(s32[16]{0:T(128)} %get-tuple-element.172.meta, bf16[512,768]{1,0:T(8,128)(2,1)} %copy-done.22, bf16[512,768]{1,0:T(8,128)(2,1)} %copy-done.45, ...), custom_call_target="tpu_custom_call" | custom-call | flops 40000000000 | bytes 30000000 | tf_op jit(solution)/shard_map/attend_forward/pallas_call | solution.py:294
  101.5 40.7 %middle.2 = (bf16[512,768]{1,0:T(8,128)(2,1)}, bf16[32,768]{1,0:T(8,128)(2,1)}, bf16[560,768]{1,0:T(8,128)(2,1)}, bf16[32,768]{1,0:T(8,128)(2,1)}, f32[24,128]{1...) custom-call(s32[16]{0:T(128)} %get-tuple-element.172.meta, ...), custom_call_target="tpu_custom_call" | custom-call | flops 12000000000 | bytes 40000000 | tf_op jit(solution)/shard_map/middle/pallas_call | solution.py:651
  143.0 48.2 %all-gather.5.cloned.1.call-done = bf16[8192,768]{1,0:T(8,128)(2,1)} async-done(((bf16[512,768]{1,0:T(8,128)(2,1)}), bf16[8192,768]{1,0:T(8,128)(2,1)}) %all-gather.5.cloned.1.call-update) | async-done | bytes 12582928 | tf_op jit(solution)/shard_map/all_gather | solution.py:77
  191.2 51.0 %attend_forward.3 = (f32[544,768]{1,0:T(8,128)}, f32[544,128]{1,0:T(8,128)}, bf16[4096,768]{1,0:T(8,128)(2,1)}, bf16[4096,768]{1,0:T(8,128)(2,1)}, bf16[4096,768]{1,0:T(8,128)(2,1)}) custom-call(s32[16]{0:T(128)} %get-tuple-element.170.meta, bf16[16,512,768]{2,1,0:T(8,128)(2,1)} %bitcast.62, bf16[4,32,768]{2,1,0:T(8,128)(2,1)} %get-tuple-element.287.refs_1_.memory, ...), custom_call_target="tpu_custom_call" | custom-call | flops 40000000000 | bytes 30000000 | tf_op jit(solution)/shard_map/attend_forward/pallas_call | solution.py:294
  242.2 40.7 %middle.3 = (bf16[512,768]{1,0:T(8,128)(2,1)}, bf16[32,768]{1,0:T(8,128)(2,1)}, bf16[560,768]{1,0:T(8,128)(2,1)}, bf16[32,768]{1,0:T(8,128)(2,1)}, f32[24,128]{1...) custom-call(s32[16]{0:T(128)} %get-tuple-element.170.meta, ...), custom_call_target="tpu_custom_call" | custom-call | flops 12000000000 | bytes 40000000 | tf_op jit(solution)/shard_map/middle/pallas_call | solution.py:651
  286.6 4.1 fusion.27
  290.7 8.0 fusion.11
  298.7 8.2 fusion.8
  308.1 67.4 %collective-permute-start.13 = (bf16[560,768]{1,0:T(8,128)(2,1)S(1)}, bf16[560,768]{1,0:T(8,128)(2,1)S(1)}, u32[]{:S(2)}, u32[]{:S(2)}) collective-permute-start(bf16[560,768]{1,0:T(8,128)(2,1)S(1)} %copy-done.38), channel_id=1, source_target_pairs={{0,4},{1,5},{2,6},{3,7},{4,8},{5,9},{6,10},{7,11},{8,12},{9,13},{1... | collective-permute-start | bytes 2580488 | tf_op jit(solution)/shard_map/ppermute | solution.py:62
  378.5 17.2 %attend_backward.4 = (bf16[544,256]{1,0:T(8,128)(2,1)}, bf16[544,256]{1,0:T(8,128)(2,1)}, bf16[544,256]{1,0:T(8,128)(2,1)}) custom-call(s32[16]{0:T(128)} %get-tuple-element.172.meta, bf16[16,560,768]{2,1,0:T(8,128)(2,1)} %bitcast.59, bf16[4096,768]{1,0:T(8,128)(2,1)} %get-tuple-element.174.refs_1_, bf16[4096,768]{1,0:T(8,128)(2,1)} %get-tuple-element.175.refs_2_, ...), custom_call_target="tpu_custom_call" | custom-call | flops 10000000000 | bytes 1000000 | tf_op jit(solution)/shard_map/attend_backward/pallas_call | solution.py:435
  395.7 17.3 %collective-permute-done.13.refs_2_ = bf16[560,768]{1,0:T(8,128)(2,1)S(1)} collective-permute-done((bf16[560,768]{1,0:T(8,128)(2,1)S(1)}, bf16[560,768]{1,0:T(8,128)(2,1)S(1)}, u32[]{:S(2)}, u32[]{:S(2)}) %collective-permute-start.13) | collective-permute-done | bytes 860192 | tf_op jit(solution)/shard_map/ppermute | solution.py:62
  413.0 4.3 collective-permute-done.14.refs_3_
  417.3 6.1 collective-permute-start.17
  425.5 21.1 %collective-permute-done.17.refs_4_ = bf16[560,768]{1,0:T(8,128)(2,1)} collective-permute-done((bf16[560,768]{1,0:T(8,128)(2,1)S(1)}, bf16[560,768]{1,0:T(8,128)(2,1)}, u32[]{:S(2)}, u32[]{:S(2)}) %collective-permute-start.17) | collective-permute-done | bytes 860192 | tf_op jit(solution)/shard_map/ppermute | solution.py:62
  446.6 17.0 %attend_backward.5 = (bf16[544,256]{1,0:T(8,128)(2,1)}, bf16[544,256]{1,0:T(8,128)(2,1)}, bf16[544,256]{1,0:T(8,128)(2,1)}) custom-call(s32[16]{0:T(128)} %get-tuple-element.172.meta, bf16[16,560,768]{2,1,0:T(8,128)(2,1)} %bitcast.60, bf16[4096,768]{1,0:T(8,128)(2,1)} %get-tuple-element.174.refs_1_, bf16[4096,768]{1,0:T(8,128)(2,1)} %get-tuple-element.175.refs_2_, ...), custom_call_target="tpu_custom_call" | custom-call | flops 10000000000 | bytes 1000000 | tf_op jit(solution)/shard_map/attend_backward/pallas_call | solution.py:435
  463.7 40.6 %collective-permute-done.18.refs_5_ = bf16[560,768]{1,0:T(8,128)(2,1)} collective-permute-done((bf16[560,768]{1,0:T(8,128)(2,1)S(1)}, bf16[560,768]{1,0:T(8,128)(2,1)}, u32[]{:S(2)}, u32[]{:S(2)}) %collective-permute-start.18) | collective-permute-done | bytes 860192 | tf_op jit(solution)/shard_map/ppermute | solution.py:62
  504.8 17.4 %attend_backward.6 = (bf16[544,256]{1,0:T(8,128)(2,1)}, bf16[544,256]{1,0:T(8,128)(2,1)}, bf16[544,256]{1,0:T(8,128)(2,1)}) custom-call(s32[16]{0:T(128)} %get-tuple-element.172.meta, bf16[16,560,768]{2,1,0:T(8,128)(2,1)} %bitcast.61, bf16[4096,768]{1,0:T(8,128)(2,1)} %get-tuple-element.174.refs_1_, bf16[4096,768]{1,0:T(8,128)(2,1)} %get-tuple-element.175.refs_2_, ...), custom_call_target="tpu_custom_call" | custom-call | flops 10000000000 | bytes 1000000 | tf_op jit(solution)/shard_map/attend_backward/pallas_call | solution.py:435
  523.5 66.7 %attend_backward.7 = (bf16[544,768]{1,0:T(8,128)(2,1)}, bf16[544,768]{1,0:T(8,128)(2,1)}, bf16[544,768]{1,0:T(8,128)(2,1)}) custom-call(s32[16]{0:T(128)} %get-tuple-element.170.meta, bf16[560,768]{1,0:T(8,128)(2,1)} %get-tuple-element.171.refs_0_, bf16[560,768]{1,0:T(8,128)(2,1)} %copy-done.41, bf16[560,768]{1,0:T(8,128)(2,1)} %copy-done.39, ...), custom_call_target="tpu_custom_call" | custom-call | flops 10000000000 | bytes 1000000 | tf_op jit(solution)/shard_map/attend_backward/pallas_call | solution.py:435
  590.2 63.7 %all-reduce.5.cloned.1.call-done = (bf16[768,3072]{1,0:T(8,128)(2,1)}, bf16[3072,768]{1,0:T(8,128)(2,1)}, bf16[768,768]{1,0:T(8,128)(2,1)}, bf16[524,768]{1,0:T(8,128)(2,1)}) async-done(((bf16[768,3072]{1,0:T(8,128)(2,1)}, bf16[3072,768]{1,0:T(8,128)(2,1)}, bf16[768,768]{1,0:T(8,128)(2,1)}, bf16[524,768]{1,0:T(8,128)(2,1)}), (bf16[768,3072]{1,0:T(8,128)(2,1)}, bf16[3072,768]{1,0:T(8,128)(2,1)}, ...) | async-done | bytes 11421712 | tf_op jit(solution)/shard_map/psum | solution.py:877
  653.9 14.8 %late_sums.1 = bf16[3072,768]{1,0:T(8,128)(2,1)} custom-call(s32[2,16]{1,0:T(2,128)} %find_chain.1.metas, s32[1]{0:T(128)} %bitcast.24.group, bf16[544,768]{1,0:T(8,128)(2,1)} %get-tuple-element.230.refs_0_, bf16[544,768]{1,0:T(8,128)(2,1)} %get-tuple-element.231.refs_1_, f32[544,768]{1,0:T(8,128)} %get-tuple-element.216.refs_2_, ...), custom_call_target="tpu_custom_call" | custom-call | tf_op jit(solution)/shard_map/late_sums/pallas_call | solution.py:752
  682.9 11.8 %collective-permute-done.29 = bf16[384,768]{1,0:T(8,128)(2,1)S(1)} collective-permute-done((bf16[384,768]{1,0:T(8,128)(2,1)S(1)}, bf16[384,768]{1,0:T(8,128)(2,1)S(1)}, u32[]{:S(2)}, u32[]{:S(2)}) %collective-permute-start.29) | collective-permute-done | bytes 589856 | tf_op jit(solution)/shard_map/ppermute | solution.py:769
  694.8 11.8 %collective-permute-done.28 = bf16[384,768]{1,0:T(8,128)(2,1)S(1)} collective-permute-done((bf16[384,768]{1,0:T(8,128)(2,1)S(1)}, bf16[384,768]{1,0:T(8,128)(2,1)S(1)}, u32[]{:S(2)}, u32[]{:S(2)}) %collective-permute-start.28) | collective-permute-done | bytes 589856 | tf_op jit(solution)/shard_map/ppermute | solution.py:769
  708.8 37.4 %collective-permute-start.31 = (bf16[96,768]{1,0:T(8,128)(2,1)S(1)}, bf16[96,768]{1,0:T(8,128)(2,1)S(1)}, u32[]{:S(2)}, u32[]{:S(2)}) collective-permute-start(bf16[96,768]{1,0:T(8,128)(2,1)S(1)} %get-tuple-element.284), channel_id=1, source_target_pairs={{0,8},{1,9},{2,10},{3,11},{4,12},{5,13},{6,14},{7,15},{8,0},{9,1},... | collective-permute-start | bytes 442376 | tf_op jit(solution)/shard_map/ppermute | solution.py:769
  747.1 8.9 %collective-permute-done.31 = bf16[96,768]{1,0:T(8,128)(2,1)S(1)} collective-permute-done((bf16[96,768]{1,0:T(8,128)(2,1)S(1)}, bf16[96,768]{1,0:T(8,128)(2,1)S(1)}, u32[]{:S(2)}, u32[]{:S(2)}) %collective-permute-start.31) | collective-permute-done | bytes 147488 | tf_op jit(solution)/shard_map/ppermute | solution.py:769
  763.0 7.1 collective-permute-done.34
  774.6 5.0 convert_element_type.148
  779.7 4.7 convert_element_type.149
  787.9 7.5 collective-permute-done.37
  (294 shorter events, 95.3 us)
Async XLA Ops:
  7.2 184.0 %all-gather.5.cloned.1.call-start = ((), (), s32[]{:S(2)}) async-start(), calls=%async_computation | async-start | bytes 13369344 | tf_op jit(solution)/shard_map/all_gather | solution.py:77
  9.8 20.5 %collective-permute-start = (bf16[512,768]{1,0:T(8,128)(2,1)S(1)}, bf16[512,768]{1,0:T(8,128)(2,1)S(1)}, u32[]{:S(2)}, u32[]{:S(2)}) collective-permute-start(bf16[512,768]{1,0:T(8,128)(2,1)S(1)} %get-tuple-element.129.refs_0_.tokens), channel_id=1, source_target_pairs={{0,2},{1,3},{2,0},{3,1},{4,6},{5,7},{6,4},{7,5},{8,10},{9,11},{10,... | collective-permute-start | bytes 2359304 | tf_op jit(solution)/shard_map/ppermute | solution.py:62
  12.8 21.3 %collective-permute-start.1 = (bf16[512,768]{1,0:T(8,128)(2,1)S(1)}, bf16[512,768]{1,0:T(8,128)(2,1)S(1)}, u32[]{:S(2)}, u32[]{:S(2)}) collective-permute-start(bf16[512,768]{1,0:T(8,128)(2,1)S(1)} %get-tuple-element.129.refs_0_.tokens), channel_id=1, source_target_pairs={{0,4},{1,5},{2,6},{3,7},{4,8},{5,9},{6,10},{7,11},{8,12},{9,13},{1... | collective-permute-start | bytes 2359304 | tf_op jit(solution)/shard_map/ppermute | solution.py:62
  16.3 21.4 %collective-permute-start.2 = (bf16[512,768]{1,0:T(8,128)(2,1)S(1)}, bf16[512,768]{1,0:T(8,128)(2,1)S(1)}, u32[]{:S(2)}, u32[]{:S(2)}) collective-permute-start(bf16[512,768]{1,0:T(8,128)(2,1)S(1)} %get-tuple-element.129.refs_0_.tokens), channel_id=1, source_target_pairs={{4,0},{5,1},{6,2},{7,3},{8,4},{9,5},{10,6},{11,7},{12,8},{13,9},{1... | collective-permute-start | bytes 2359304 | tf_op jit(solution)/shard_map/ppermute | solution.py:62
  17.6 20.1 %collective-permute-start.5 = (bf16[512,768]{1,0:T(8,128)(2,1)S(1)}, bf16[512,768]{1,0:T(8,128)(2,1)S(1)}, u32[]{:S(2)}, u32[]{:S(2)}) collective-permute-start(bf16[512,768]{1,0:T(8,128)(2,1)S(1)} %get-tuple-element.129.refs_0_.tokens), channel_id=1, source_target_pairs={{2,8},{3,9},{6,12},{7,13},{8,2},{9,3},{12,6},{13,7},{18,24},{19,25... | collective-permute-start | bytes 2359304 | tf_op jit(solution)/shard_map/ppermute | solution.py:62
  18.4 19.9 %collective-permute-start.6 = (bf16[512,768]{1,0:T(8,128)(2,1)S(1)}, bf16[512,768]{1,0:T(8,128)(2,1)S(1)}, u32[]{:S(2)}, u32[]{:S(2)}) collective-permute-start(bf16[512,768]{1,0:T(8,128)(2,1)S(1)} %get-tuple-element.129.refs_0_.tokens), channel_id=1, source_target_pairs={{0,1},{1,0},{2,3},{3,2},{4,5},{5,4},{6,7},{7,6},{8,9},{9,8},{10,11... | collective-permute-start | bytes 2359304 | tf_op jit(solution)/shard_map/ppermute | solution.py:62
  30.4 19.6 %collective-permute-start.3 = (bf16[512,768]{1,0:T(8,128)(2,1)S(1)}, bf16[512,768]{1,0:T(8,128)(2,1)S(1)}, u32[]{:S(2)}, u32[]{:S(2)}) collective-permute-start(bf16[512,768]{1,0:T(8,128)(2,1)S(1)} %collective-permute-done.refs_1_), channel_id=1, source_target_pairs={{0,4},{1,5},{2,6},{3,7},{4,8},{5,9},{6,10},{7,11},{8,12},{9,13},{1... | collective-permute-start | bytes 2359304 | tf_op jit(solution)/shard_map/ppermute | solution.py:62
  34.1 21.5 %collective-permute-start.4 = (bf16[512,768]{1,0:T(8,128)(2,1)S(1)}, bf16[512,768]{1,0:T(8,128)(2,1)S(1)}, u32[]{:S(2)}, u32[]{:S(2)}) collective-permute-start(bf16[512,768]{1,0:T(8,128)(2,1)S(1)} %collective-permute-done.refs_1_), channel_id=1, source_target_pairs={{4,0},{5,1},{6,2},{7,3},{8,4},{9,5},{10,6},{11,7},{12,8},{13,9},{1... | collective-permute-start | bytes 2359304 | tf_op jit(solution)/shard_map/ppermute | solution.py:62
  37.7 18.0 %collective-permute-start.7 = (bf16[512,768]{1,0:T(8,128)(2,1)S(1)}, bf16[512,768]{1,0:T(8,128)(2,1)S(1)}, u32[]{:S(2)}, u32[]{:S(2)}) collective-permute-start(bf16[512,768]{1,0:T(8,128)(2,1)S(1)} %collective-permute-done.refs_1_), channel_id=1, source_target_pairs={{0,1},{1,0},{2,3},{3,2},{4,5},{5,4},{6,7},{7,6},{8,9},{9,8},{10,11... | collective-permute-start | bytes 2359304 | tf_op jit(solution)/shard_map/ppermute | solution.py:62
  37.7 18.5 %collective-permute-start.8 = (bf16[512,768]{1,0:T(8,128)(2,1)S(1)}, bf16[512,768]{1,0:T(8,128)(2,1)S(1)}, u32[]{:S(2)}, u32[]{:S(2)}) collective-permute-start(bf16[512,768]{1,0:T(8,128)(2,1)S(1)} %collective-permute-done.1.refs_2_), channel_id=1, source_target_pairs={{0,1},{1,0},{2,3},{3,2},{4,5},{5,4},{6,7},{7,6},{8,9},{9,8},{10,11... | collective-permute-start | bytes 2359304 | tf_op jit(solution)/shard_map/ppermute | solution.py:62
  38.2 18.0 %collective-permute-start.9 = (bf16[512,768]{1,0:T(8,128)(2,1)S(1)}, bf16[512,768]{1,0:T(8,128)(2,1)S(1)}, u32[]{:S(2)}, u32[]{:S(2)}) collective-permute-start(bf16[512,768]{1,0:T(8,128)(2,1)S(1)} %collective-permute-done.2.refs_3_), channel_id=1, source_target_pairs={{0,1},{1,0},{2,3},{3,2},{4,5},{5,4},{6,7},{7,6},{8,9},{9,8},{10,11... | collective-permute-start | bytes 2359304 | tf_op jit(solution)/shard_map/ppermute | solution.py:62
  60.0 318.5 %all-gather.7.cloned.1.call-start = ((), (), s32[]{:S(2)}) async-start(), calls=%async_computation.1 | async-start | bytes 14622720 | tf_op jit(solution)/shard_map/all_gather | solution.py:77
  142.2 511.7 %all-reduce.5.cloned.1.call-start = ((), (), s32[]{:S(2)}) async-start(), calls=%async_computation.2 | async-start | bytes 22855680 | tf_op jit(solution)/shard_map/psum | solution.py:877
  308.1 104.9 %collective-permute-start.13 = (bf16[560,768]{1,0:T(8,128)(2,1)S(1)}, bf16[560,768]{1,0:T(8,128)(2,1)S(1)}, u32[]{:S(2)}, u32[]{:S(2)}) collective-permute-start(bf16[560,768]{1,0:T(8,128)(2,1)S(1)} %copy-done.38), channel_id=1, source_target_pairs={{0,4},{1,5},{2,6},{3,7},{4,8},{5,9},{6,10},{7,11},{8,12},{9,13},{1... | collective-permute-start | bytes 2580488 | tf_op jit(solution)/shard_map/ppermute | solution.py:62
  375.5 41.7 %collective-permute-start.14 = (bf16[560,768]{1,0:T(8,128)(2,1)S(1)}, bf16[560,768]{1,0:T(8,128)(2,1)S(1)}, u32[]{:S(2)}, u32[]{:S(2)}) collective-permute-start(bf16[560,768]{1,0:T(8,128)(2,1)S(1)} %copy-done.38), channel_id=1, source_target_pairs={{4,0},{5,1},{6,2},{7,3},{8,4},{9,5},{10,6},{11,7},{12,8},{13,9},{1... | collective-permute-start | bytes 2580488 | tf_op jit(solution)/shard_map/ppermute | solution.py:62
  376.8 40.5 %collective-permute-start.15 = (bf16[560,768]{1,0:T(8,128)(2,1)S(1)}, bf16[560,768]{1,0:T(8,128)(2,1)S(1)}, u32[]{:S(2)}, u32[]{:S(2)}) collective-permute-start(bf16[560,768]{1,0:T(8,128)(2,1)S(1)} %copy-done.38), channel_id=1, source_target_pairs={{0,2},{1,3},{2,0},{3,1},{4,6},{5,7},{6,4},{7,5},{8,10},{9,11},{10,... | collective-permute-start | bytes 2580488 | tf_op jit(solution)/shard_map/ppermute | solution.py:62
  376.9 40.4 %collective-permute-start.16 = (bf16[560,768]{1,0:T(8,128)(2,1)S(1)}, bf16[560,768]{1,0:T(8,128)(2,1)}, u32[]{:S(2)}, u32[]{:S(2)}) collective-permute-start(bf16[560,768]{1,0:T(8,128)(2,1)S(1)} %copy-done.38), channel_id=1, source_target_pairs={{2,8},{3,9},{6,12},{7,13},{8,2},{9,3},{12,6},{13,7},{18,24},{19,25... | collective-permute-start | bytes 2580488 | tf_op jit(solution)/shard_map/ppermute | solution.py:62
  378.5 46.7 %collective-permute-start.19 = (bf16[560,768]{1,0:T(8,128)(2,1)S(1)}, bf16[560,768]{1,0:T(8,128)(2,1)}, u32[]{:S(2)}, u32[]{:S(2)}) collective-permute-start(bf16[560,768]{1,0:T(8,128)(2,1)S(1)} %copy-done.38), channel_id=1, source_target_pairs={{0,1},{1,0},{2,3},{3,2},{4,5},{5,4},{6,7},{7,6},{8,9},{9,8},{10,11... | collective-permute-start | bytes 2580488 | tf_op jit(solution)/shard_map/ppermute | solution.py:62
  417.3 29.3 %collective-permute-start.17 = (bf16[560,768]{1,0:T(8,128)(2,1)S(1)}, bf16[560,768]{1,0:T(8,128)(2,1)}, u32[]{:S(2)}, u32[]{:S(2)}) collective-permute-start(bf16[560,768]{1,0:T(8,128)(2,1)S(1)} %collective-permute-done.15.refs_1_), channel_id=1, source_target_pairs={{0,4},{1,5},{2,6},{3,7},{4,8},{5,9},{6,10},{7,11},{8,12},{9,13},{1... | collective-permute-start | bytes 2580488 | tf_op jit(solution)/shard_map/ppermute | solution.py:62
  423.4 80.9 %collective-permute-start.18 = (bf16[560,768]{1,0:T(8,128)(2,1)S(1)}, bf16[560,768]{1,0:T(8,128)(2,1)}, u32[]{:S(2)}, u32[]{:S(2)}) collective-permute-start(bf16[560,768]{1,0:T(8,128)(2,1)S(1)} %collective-permute-done.15.refs_1_), channel_id=1, source_target_pairs={{4,0},{5,1},{6,2},{7,3},{8,4},{9,5},{10,6},{11,7},{12,8},{13,9},{1... | collective-permute-start | bytes 2580488 | tf_op jit(solution)/shard_map/ppermute | solution.py:62
  424.6 79.6 %collective-permute-start.20 = (bf16[560,768]{1,0:T(8,128)(2,1)S(1)}, bf16[560,768]{1,0:T(8,128)(2,1)}, u32[]{:S(2)}, u32[]{:S(2)}) collective-permute-start(bf16[560,768]{1,0:T(8,128)(2,1)S(1)} %collective-permute-done.15.refs_1_), channel_id=1, source_target_pairs={{0,1},{1,0},{2,3},{3,2},{4,5},{5,4},{6,7},{7,6},{8,9},{9,8},{10,11... | collective-permute-start | bytes 2580488 | tf_op jit(solution)/shard_map/ppermute | solution.py:62
  424.9 79.3 %collective-permute-start.21 = (bf16[560,768]{1,0:T(8,128)(2,1)S(1)}, bf16[560,768]{1,0:T(8,128)(2,1)}, u32[]{:S(2)}, u32[]{:S(2)}) collective-permute-start(bf16[560,768]{1,0:T(8,128)(2,1)S(1)} %collective-permute-done.13.refs_2_), channel_id=1, source_target_pairs={{0,1},{1,0},{2,3},{3,2},{4,5},{5,4},{6,7},{7,6},{8,9},{9,8},{10,11... | collective-permute-start | bytes 2580488 | tf_op jit(solution)/shard_map/ppermute | solution.py:62
  425.2 79.0 %collective-permute-start.22 = (bf16[560,768]{1,0:T(8,128)(2,1)S(1)}, bf16[560,768]{1,0:T(8,128)(2,1)S(1)}, u32[]{:S(2)}, u32[]{:S(2)}) collective-permute-start(bf16[560,768]{1,0:T(8,128)(2,1)S(1)} %collective-permute-done.14.refs_3_), channel_id=1, source_target_pairs={{0,1},{1,0},{2,3},{3,2},{4,5},{5,4},{6,7},{7,6},{8,9},{9,8},{10,11... | collective-permute-start | bytes 2580488 | tf_op jit(solution)/shard_map/ppermute | solution.py:62
  446.6 57.7 %collective-permute-start.23 = (bf16[560,768]{1,0:T(8,128)(2,1)}, bf16[560,768]{1,0:T(8,128)(2,1)}, u32[]{:S(2)}, u32[]{:S(2)}) collective-permute-start(bf16[560,768]{1,0:T(8,128)(2,1)} %collective-permute-done.16.refs_6_), channel_id=1, source_target_pairs={{0,1},{1,0},{2,3},{3,2},{4,5},{5,4},{6,7},{7,6},{8,9},{9,8},{10,11... | collective-permute-start | bytes 2580488 | tf_op jit(solution)/shard_map/ppermute | solution.py:62
  504.3 18.0 %collective-permute-start.24 = (bf16[560,768]{1,0:T(8,128)(2,1)}, bf16[560,768]{1,0:T(8,128)(2,1)S(1)}, u32[]{:S(2)}, u32[]{:S(2)}) collective-permute-start(bf16[560,768]{1,0:T(8,128)(2,1)} %collective-permute-done.17.refs_4_), channel_id=1, source_target_pairs={{0,1},{1,0},{2,3},{3,2},{4,5},{5,4},{6,7},{7,6},{8,9},{9,8},{10,11... | collective-permute-start | bytes 2580488 | tf_op jit(solution)/shard_map/ppermute | solution.py:62
  504.3 17.9 %collective-permute-start.25 = (bf16[560,768]{1,0:T(8,128)(2,1)}, bf16[560,768]{1,0:T(8,128)(2,1)S(1)}, u32[]{:S(2)}, u32[]{:S(2)}) collective-permute-start(bf16[560,768]{1,0:T(8,128)(2,1)} %collective-permute-done.18.refs_5_), channel_id=1, source_target_pairs={{0,1},{1,0},{2,3},{3,2},{4,5},{5,4},{6,7},{7,6},{8,9},{9,8},{10,11... | collective-permute-start | bytes 2580488 | tf_op jit(solution)/shard_map/ppermute | solution.py:62
  679.6 26.9 %collective-permute-start.28 = (bf16[384,768]{1,0:T(8,128)(2,1)S(1)}, bf16[384,768]{1,0:T(8,128)(2,1)S(1)}, u32[]{:S(2)}, u32[]{:S(2)}) collective-permute-start(bf16[384,768]{1,0:T(8,128)(2,1)S(1)} %get-tuple-element.277), channel_id=1, source_target_pairs={{0,16},{1,17},{2,18},{3,19},{4,20},{5,21},{6,22},{7,23},{8,24},{9,... | collective-permute-start | bytes 1769480 | tf_op jit(solution)/shard_map/ppermute | solution.py:769
  680.4 26.2 %collective-permute-start.27 = (bf16[384,768]{1,0:T(8,128)(2,1)S(1)}, bf16[384,768]{1,0:T(8,128)(2,1)S(1)}, u32[]{:S(2)}, u32[]{:S(2)}) collective-permute-start(bf16[384,768]{1,0:T(8,128)(2,1)S(1)} %get-tuple-element.275), channel_id=1, source_target_pairs={{0,2},{1,3},{2,0},{3,1},{4,6},{5,7},{6,4},{7,5},{8,10},{9,11},{10,... | collective-permute-start | bytes 1769480 | tf_op jit(solution)/shard_map/ppermute | solution.py:769
  706.9 40.2 %collective-permute-start.32 = (bf16[96,768]{1,0:T(8,128)(2,1)S(1)}, bf16[96,768]{1,0:T(8,128)(2,1)S(1)}, u32[]{:S(2)}, u32[]{:S(2)}) collective-permute-start(bf16[96,768]{1,0:T(8,128)(2,1)S(1)} %get-tuple-element.283), channel_id=1, source_target_pairs={{0,12},{1,13},{2,14},{3,15},{4,8},{5,9},{6,10},{7,11},{8,4},{9,5},... | collective-permute-start | bytes 442376 | tf_op jit(solution)/shard_map/ppermute | solution.py:769
  708.8 47.3 %collective-permute-start.31 = (bf16[96,768]{1,0:T(8,128)(2,1)S(1)}, bf16[96,768]{1,0:T(8,128)(2,1)S(1)}, u32[]{:S(2)}, u32[]{:S(2)}) collective-permute-start(bf16[96,768]{1,0:T(8,128)(2,1)S(1)} %get-tuple-element.284), channel_id=1, source_target_pairs={{0,8},{1,9},{2,10},{3,11},{4,12},{5,13},{6,14},{7,15},{8,0},{9,1},... | collective-permute-start | bytes 442376 | tf_op jit(solution)/shard_map/ppermute | solution.py:769
  771.3 24.2 %collective-permute-start.37 = (bf16[384,768]{1,0:T(8,128)(2,1)S(1)}, bf16[384,768]{1,0:T(8,128)(2,1)}, u32[]{:S(2)}, u32[]{:S(2)}) collective-permute-start(bf16[384,768]{1,0:T(8,128)(2,1)S(1)} %constant_dynamic-update-slice_fusion.6), channel_id=1, source_target_pairs={{0,16},{1,17},{2,18},{3,19},{4,20},{5,21},{6,22},{7,23},{8,24},{9,... | collective-permute-start | bytes 1769480 | tf_op jit(solution)/shard_map/ppermute | solution.py:769
  773.0 23.6 %collective-permute-start.38 = (bf16[384,768]{1,0:T(8,128)(2,1)S(1)}, bf16[384,768]{1,0:T(8,128)(2,1)}, u32[]{:S(2)}, u32[]{:S(2)}) collective-permute-start(bf16[384,768]{1,0:T(8,128)(2,1)S(1)} %constant_dynamic-update-slice_fusion.6), channel_id=1, source_target_pairs={{0,18},{1,19},{2,16},{3,17},{4,22},{5,23},{6,20},{7,21},{8,26},{9,... | collective-permute-start | bytes 1769480 | tf_op jit(solution)/shard_map/ppermute | solution.py:769
  (84 other events, 1537.6 us)
Sparse Core Ops, SparseCore 0:
  60.1 131.0 all-gather.4
  194.1 135.4 all-gather.6
  336.6 317.2 all-reduce.4

commit v3 on v2

--- a/solution.py
+++ b/solution.py
@@ -22,8 +22,8 @@
 BACK_COST = 10_000_000_000
 LATE_ROWS = 256
 NPIECE = 14
-ROWS = 32
-COLS = 512
+ROWS = 272
+COLS = 1024
 NEG = -1e30
 SHIFT_FREE = 60.0
 EPS = 1e-05
@@ -47,13 +47,7 @@
 
 UP = plane_moves(lambda side: 1)
 DOWN = plane_moves(lambda side: -1)
-FAR = [
-    (4 * plane + place, 4 * target + (place ^ 2))
-    for plane in range(4)
-    for place in range(4)
-    for target in [plane + (2 if place >> 1 else -2)]
-    if 0 <= target < 4
-]
+OUTWARD = plane_moves(lambda side: 1 if side else -1)
 SIDE = [(i, i ^ 2) for i in range(16)]
 CORE = [(i, i ^ 1) for i in range(16)]
 
@@ -62,15 +56,13 @@
     return lax.ppermute(value, "blk", pairs)
 
 
-def gather_near(value, hold=lambda stage, parts: parts):
-    below, above, beside, far = (move(value, pairs) for pairs in (UP, DOWN, SIDE, FAR))
-    below, above, beside, far = hold(0, [below, above, beside, far])
-    moved = [move(beside, UP), move(beside, DOWN)]
-    first = [move(part, CORE) for part in (value, beside, below, above, far)]
-    moved_and_first = hold(1, moved + first)
-    moved, first = moved_and_first[:2], moved_and_first[2:]
-    second = hold(2, [move(part, CORE) for part in moved])
-    return [value, beside, below, above, *moved, far] + first[:4] + second + first[4:]
+def gather_near(value):
+    side = (lax.axis_index("blk") >> 1) & 1
+    below, above, beside = move(value, UP), move(value, DOWN), move(value, SIDE)
+    far = move(jnp.where(side == 1, below, above), OUTWARD)
+    moved = [move(beside, UP), move(beside, DOWN), move(far, SIDE)]
+    here = [value, beside, below, above] + moved
+    return here + [move(part, CORE) for part in here]
 
 
 def gather_all(value):
@@ -490,7 +482,7 @@
     wo, bo, gain1, shift1, bi, b2, gain2, shift2, wi_from, w2_from,
     final, final_mem, payload, mem_grad, mem_stats, own_stats, res_grad, rows,
     attended_low, branch_out, first_low, inner_out, active, outer_out, sums, inner_sum,
-    wi, w2, first, norm1, scale1, total, second_grad, outer_grad, slope, weight_sems,
+    wi, w2, first, norm1, scale1, total, second_grad, outer_grad, slope, cots, weight_sems,
 ):
     width, inner_width = wi.shape
     wi_copy = pltpu.make_async_copy(wi_from, wi, weight_sems.at[0])
@@ -501,6 +493,8 @@
     lead = jnp.where(meta[M_SPOT] == 0, 1.0, 0.0)
     rows[0:SEG, :] = tokens[...]
     rows[SEG:OWN, :] = memory[chain]
+    cots[0:SEG, :] = token_cot[...]
+    cots[SEG:OWN, :] = memory_cot[chain]
     attended_low[...] = attended[...].astype(BF16)
     total[...] = jnp.dot(attended_low[...], wo[...], preferred_element_type=F32)
     sums[...] = jnp.zeros_like(sums)
@@ -559,19 +553,7 @@
         value = jnp.where(live, normed * vector(gain2) + vector(shift2), 0.0)
         rows_low = value.astype(BF16)
         outer_out[span, :] = rows_low
-        start = span.start
-
-        @pl.when(start < SEG)
-        def _():
-            cot = token_cot[span, :].astype(F32)
-            first_back(span, live, counted, normed, scale, cot)
-
-        @pl.when(start >= SEG)
-        def _():
-            cot = memory_cot[chain].astype(F32)
-            first_back(span, live, counted, normed, scale, cot)
-
-    def first_back(span, live, counted, normed, scale, cot):
+        cot = cots[span, :].astype(F32)
         cot = jnp.where(live, cot, 0.0)
         weighted = cot * counted
         add(4, weighted * normed)
@@ -680,6 +662,7 @@
             pltpu.VMEM((OWN, width), F32),
             pltpu.VMEM((OWN, width), BF16),
             pltpu.VMEM((OWN, inner_width), F32),
+            pltpu.VMEM((OWN, width), BF16),
             pltpu.SemaphoreType.DMA((2,)),
         ],
         compiler_params=pltpu.CompilerParams(vmem_limit_bytes=VMEM_LIMIT),
@@ -788,7 +771,7 @@
         got = [swap(part(k), mask) for k, mask in enumerate(masks) if k]
         value = sum((g.astype(F32) for g in got), part(0).astype(F32)).astype(BF16)
     for index, group in enumerate(reversed(groups)):
-        if index + 1 == len(groups):
+        if index == 1:
             value, beside = lax.optimization_barrier((value, beside))
         masks, own = masks_of(group), own_of(group)
         size = value.shape[0]
@@ -874,27 +857,18 @@
     early, *held = lax.optimization_barrier((early, *[s["meta"] for s in states]))
     for s, meta in zip(states, held):
         s["meta"] = meta
-    early = lax.psum(early, ("dp", "blk"))
-
-    def backward(s, payload, *quads):
-        return attend_backward(
-            s["meta"], payload, s["chain_rows"], s["mem_grad"], s["mem_stats"], s["own_stats"],
-            *quads,
+        s["gathered"] = gather_all(s["payload"])
+    for s in states:
+        s["grads"] = attend_backward(
+            s["meta"], s["gathered"], s["chain_rows"], s["mem_grad"], s["mem_stats"],
+            s["own_stats"], 0, NQUAD,
         )
-
-    def hold(stage, parts):
-        got = [backward(s, s["gathered"], stage, 1) for s in states[:-1]]
-        got, parts = lax.optimization_barrier((got, parts))
-        for s, grads in zip(states, got):
-            s["grads"] = [old + [new] for old, new in zip(s.get("grads", [[]] * 3), grads)]
-        return parts
-
-    for s in states[:-1]:
-        s["gathered"] = gather_all(s["payload"])
-    last = states[-1]
-    near = gather_near(last["payload"], hold)
-    last["grads"] = [[grad] for grad in backward(last, near, 0, NQUAD)]
-    last["grads"], early = lax.optimization_barrier((last["grads"], early))
+        if s is states[0]:
+            s["grads"], states[-1]["gathered"], early = lax.optimization_barrier(
+                (s["grads"], states[-1]["gathered"], early)
+            )
+            early = lax.psum(early, ("dp", "blk"))
+        s["grads"] = [[grad] for grad in s["grads"]]
     grad_inner, grad_outer, grad_output, rest = early
     late = late_sums(
         metas, group, groups, chains, [s["rows"] for s in states],

time: 822 us -> 789 us (0.960); the launches traced: 824 us -> 802 us
  waiting for transfers between devices: 280 us -> 217 us
  Pallas kernels: 298 us -> 358 us
  starting transfers between devices: 146 us -> 132 us
    ppermute x26 -> x14, starting transfers between devices: 94 us -> 16.1 us  [move(): return lax.ppermute(value, 'blk', pairs)]
    ppermute x26 -> x14, waiting for transfers between devices: 118 us -> 51.4 us  [move(): return lax.ppermute(value, 'blk', pairs)]
    ppermute x14, starting transfers between devices: 51.5 us -> 116 us  [swap(): lax.ppermute(value, ('dp', 'blk'), [(i, i ^ mask) for i in range(sizes)])]
    pallas_call x4 -> x2, Pallas kernels: 118 us -> 160 us  [attend_backward(): pl.pallas_call(functools.partial(backward_body, start, count), grid_spec=...]
    pallas_call x2, Pallas kernels: 82.1 us -> 121 us  [attend_forward(): pl.pallas_call(forward_body, grid_spec=pltpu.PrefetchScalarGridSpec(num_s...]
    ppermute x14, waiting for transfers between devices: 50.9 us -> 87.8 us  [swap(): lax.ppermute(value, ('dp', 'blk'), [(i, i ^ mask) for i in range(sizes)])]
    all_gather x2 -> x3, waiting for transfers between devices: 48.2 us -> 21 us  [gather_all(): return [lax.all_gather(value, 'blk')]]
    pallas_call x2, Pallas kernels: 81.3 us -> 59.5 us  [middle(): pl.pallas_call(middle_body, in_specs=[pl.BlockSpec(memory_space=pltpu.SME...]
  transfers between devices with their start and end apart: 43 -> 32, of which waited for: 20 -> 20; matrix products, arithmetic and copies ran while one was open for 8% -> 7% of each run, Pallas kernels for 34% -> 45%
where the time goes in v3:
time: 789 us; the launch traced here: 802 us
  Pallas kernels  358 us (45%)
  waiting for transfers between devices  217 us (28%)
  starting transfers between devices  132 us (17%)
  other arithmetic  31.4 us (4%)
  local copies, waits for them, and re-layouts  24.9 us (3%)
  matrix products  24.1 us (3%)
  between operations  14.8 us (2%)
    pallas_call x2, Pallas kernels, attend_backward(): pl.pallas_call(functools.partial(backward_body, start, count), grid_spec=...  160 us
    pallas_call x2, Pallas kernels, attend_forward(): pl.pallas_call(forward_body, grid_spec=pltpu.PrefetchScalarGridSpec(num_s...  121 us
    ppermute x14, starting transfers between devices, swap(): lax.ppermute(value, ('dp', 'blk'), [(i, i ^ mask) for i in range(sizes)])  116 us
    ppermute x14, waiting for transfers between devices, swap(): lax.ppermute(value, ('dp', 'blk'), [(i, i ^ mask) for i in range(sizes)])  87.8 us
    pallas_call x2, Pallas kernels, middle(): pl.pallas_call(middle_body, in_specs=[pl.BlockSpec(memory_space=pltpu.SME...  59.5 us
    psum x1, waiting for transfers between devices, local(): early = lax.psum(early, ('dp', 'blk'))  56.9 us
    ppermute x14, waiting for transfers between devices, move(): return lax.ppermute(value, 'blk', pairs)  51.4 us
    all_gather x3, waiting for transfers between devices, gather_all(): return [lax.all_gather(value, 'blk')]  21 us
  transfers between devices with their start and end apart: 32, of which 20 were waited for; matrix products, arithmetic and copies ran while one was open for 7% of the time, Pallas kernels for 45%

profile of v3, /device:TPU:0, one launch (start us, length us, event | category | flops | bytes accessed | tf_op | source)
XLA Modules:
  0.0 802.1 jit_solution(16915629740132707939)
XLA Ops:
  10.0 5.1 collective-permute-start.1
  17.9 14.2 %collective-permute-done.1.refs_2_ = bf16[512,768]{1,0:T(8,128)(2,1)S(1)} collective-permute-done((bf16[512,768]{1,0:T(8,128)(2,1)}, bf16[512,768]{1,0:T(8,128)(2,1)S(1)}, u32[]{:S(2)}, u32[]{:S(2)}) %collective-permute-start.1) | collective-permute-done | bytes 786464 | tf_op jit(solution)/shard_map/ppermute | solution.py:56
  32.1 4.2 collective-permute-done.2.refs_3_
  38.9 4.6 collective-permute-start.3
  45.1 14.8 %collective-permute-done.5 = bf16[512,768]{1,0:T(8,128)(2,1)S(1)} collective-permute-done((bf16[512,768]{1,0:T(8,128)(2,1)S(1)}, bf16[512,768]{1,0:T(8,128)(2,1)S(1)}, u32[]{:S(2)}, u32[]{:S(2)}) %collective-permute-start.5) | collective-permute-done | bytes 786464 | tf_op jit(solution)/shard_map/ppermute | solution.py:56
  61.2 13.1 %collective-permute-done.4.refs_5_ = bf16[512,768]{1,0:T(8,128)(2,1)S(1)} collective-permute-done((bf16[512,768]{1,0:T(8,128)(2,1)}, bf16[512,768]{1,0:T(8,128)(2,1)S(1)}, u32[]{:S(2)}, u32[]{:S(2)}) %collective-permute-start.4) | collective-permute-done | bytes 786464 | tf_op jit(solution)/shard_map/ppermute | solution.py:56
  90.2 90.2 %attend_forward.2 = (f32[544,768]{1,0:T(8,128)}, f32[544,128]{1,0:T(8,128)}, bf16[4096,768]{1,0:T(8,128)(2,1)}, bf16[4096,768]{1,0:T(8,128)(2,1)}, bf16[4096,768]{1,0:T(8,128)(2,1)}) custom-call(s32[16]{0:T(128)} %get-tuple-element.143.meta, bf16[512,768]{1,0:T(8,128)(2,1)} %get-tuple-element.102.refs_0_.tokens, ...), custom_call_target="tpu_custom_call" | custom-call | flops 40000000000 | bytes 30000000 | tf_op jit(solution)/shard_map/attend_forward/pallas_call | solution.py:286
  180.3 29.7 %middle.2 = (bf16[512,768]{1,0:T(8,128)(2,1)}, bf16[32,768]{1,0:T(8,128)(2,1)}, bf16[560,768]{1,0:T(8,128)(2,1)}, bf16[32,768]{1,0:T(8,128)(2,1)}, f32[24,128]{1...) custom-call(s32[16]{0:T(128)} %get-tuple-element.143.meta, ...), custom_call_target="tpu_custom_call" | custom-call | flops 12000000000 | bytes 40000000 | tf_op jit(solution)/shard_map/middle/pallas_call | solution.py:633
  210.2 31.2 %attend_forward.3 = (f32[544,768]{1,0:T(8,128)}, f32[544,128]{1,0:T(8,128)}, bf16[4096,768]{1,0:T(8,128)(2,1)}, bf16[4096,768]{1,0:T(8,128)(2,1)}, bf16[4096,768]{1,0:T(8,128)(2,1)}) custom-call(s32[16]{0:T(128)} %get-tuple-element.165.meta, bf16[16,512,768]{2,1,0:T(8,128)(2,1)} %bitcast.61, bf16[4,32,768]{2,1,0:T(8,128)(2,1)} %get-tuple-element.233.refs_1_.memory, ...), custom_call_target="tpu_custom_call" | custom-call | flops 40000000000 | bytes 30000000 | tf_op jit(solution)/shard_map/attend_forward/pallas_call | solution.py:286
  241.4 29.8 %middle.3 = (bf16[512,768]{1,0:T(8,128)(2,1)}, bf16[32,768]{1,0:T(8,128)(2,1)}, bf16[560,768]{1,0:T(8,128)(2,1)}, bf16[32,768]{1,0:T(8,128)(2,1)}, f32[24,128]{1...) custom-call(s32[16]{0:T(128)} %get-tuple-element.165.meta, ...), custom_call_target="tpu_custom_call" | custom-call | flops 12000000000 | bytes 40000000 | tf_op jit(solution)/shard_map/middle/pallas_call | solution.py:633
  275.7 2.8 fusion.27
  279.4 8.0 %fusion.11 = bf16[768,3072]{1,0:T(8,128)(2,1)} fusion(bf16[544,3072]{1,0:T(8,128)(2,1)S(1)} %copy-done.42, bf16[544,3072]{1,0:T(8,128)(2,1)S(1)} %copy-done.41, bf16[544,768]{1,0:T(8,128)(2,1)S(1)} %copy-done.48, bf16[544,768]{1,0:T(8,128)(2,1)S(1)} %copy-done.47), kind=kOutput, calls=%fused_computation.9 | convolution fusion | flops 5152899072 | bytes 13074432 | tf_op jit(solution)/shard_map/dot_general | solution.py:747
  287.5 8.2 %fusion.8 = bf16[3072,768]{1,0:T(8,128)(2,1)} fusion(bf16[544,3072]{1,0:T(8,128)(2,1)S(1)} %copy-done.50, bf16[544,3072]{1,0:T(8,128)(2,1)S(1)} %copy-done.49, bf16[544,768]{1,0:T(8,128)(2,1)S(1)} %copy-done.52, bf16[544,768]{1,0:T(8,128)(2,1)S(1)} %copy-done.51), kind=kOutput, calls=%fused_computation.8 | convolution fusion | flops 5152899072 | bytes 13074432 | tf_op jit(solution)/shard_map/dot_general | solution.py:747
  295.7 21.0 %all-gather.9.cloned.1.call-done = bf16[8960,768]{1,0:T(8,128)(2,1)} async-done(((bf16[560,768]{1,0:T(8,128)(2,1)}), bf16[8960,768]{1,0:T(8,128)(2,1)}) %all-gather.9.cloned.1.call-update) | async-done | bytes 13762576 | tf_op jit(solution)/shard_map/all_gather | solution.py:69
  316.7 119.3 %attend_backward.2 = (bf16[544,768]{1,0:T(8,128)(2,1)}, bf16[544,768]{1,0:T(8,128)(2,1)}, bf16[544,768]{1,0:T(8,128)(2,1)}) custom-call(s32[16]{0:T(128)} %get-tuple-element.143.meta, bf16[16,560,768]{2,1,0:T(8,128)(2,1)} %bitcast.59, bf16[4096,768]{1,0:T(8,128)(2,1)} %get-tuple-element.145.refs_1_, bf16[4096,768]{1,0:T(8,128)(2,1)} %get-tuple-element.146.refs_2_, ...), custom_call_target="tpu_custom_call" | custom-call | flops 10000000000 | bytes 1000000 | tf_op jit(solution)/shard_map/attend_backward/pallas_call | solution.py:427
  436.0 41.2 %attend_backward.3 = (bf16[544,768]{1,0:T(8,128)(2,1)}, bf16[544,768]{1,0:T(8,128)(2,1)}, bf16[544,768]{1,0:T(8,128)(2,1)}) custom-call(s32[16]{0:T(128)} %get-tuple-element.165.meta, bf16[16,560,768]{2,1,0:T(8,128)(2,1)} %bitcast.60, bf16[4096,768]{1,0:T(8,128)(2,1)} %get-tuple-element.167.refs_1_, bf16[4096,768]{1,0:T(8,128)(2,1)} %get-tuple-element.168.refs_2_, ...), custom_call_target="tpu_custom_call" | custom-call | flops 10000000000 | bytes 1000000 | tf_op jit(solution)/shard_map/attend_backward/pallas_call | solution.py:427
  477.2 14.9 %late_sums.1 = bf16[3072,768]{1,0:T(8,128)(2,1)} custom-call(s32[2,16]{1,0:T(2,128)} %find_chain.1.metas, s32[1]{0:T(128)} %bitcast.25.group, bf16[544,768]{1,0:T(8,128)(2,1)} %get-tuple-element.176.refs_0_, bf16[544,768]{1,0:T(8,128)(2,1)} %get-tuple-element.177.refs_1_, f32[544,768]{1,0:T(8,128)} %get-tuple-element.160.refs_2_, ...), custom_call_target="tpu_custom_call" | custom-call | tf_op jit(solution)/shard_map/late_sums/pallas_call | solution.py:735
  494.4 4.3 collective-permute-done.14
  498.7 3.2 add_convert_fusion
  503.0 96.7 %collective-permute-start.15 = (bf16[384,768]{1,0:T(8,128)(2,1)}, bf16[384,768]{1,0:T(8,128)(2,1)S(1)}, u32[]{:S(2)}, u32[]{:S(2)}) collective-permute-start(bf16[384,768]{1,0:T(8,128)(2,1)} %get-tuple-element.221), channel_id=1, source_target_pairs={{0,2},{1,3},{2,0},{3,1},{4,6},{5,7},{6,4},{7,5},{8,10},{9,11},{10,... | collective-permute-start | bytes 1769480 | tf_op jit(solution)/shard_map/ppermute | solution.py:752
  601.1 14.8 %collective-permute-done.15 = bf16[384,768]{1,0:T(8,128)(2,1)S(1)} collective-permute-done((bf16[384,768]{1,0:T(8,128)(2,1)}, bf16[384,768]{1,0:T(8,128)(2,1)S(1)}, u32[]{:S(2)}, u32[]{:S(2)}) %collective-permute-start.15) | collective-permute-done | bytes 589856 | tf_op jit(solution)/shard_map/ppermute | solution.py:752
  615.9 15.7 %collective-permute-done.16 = bf16[384,768]{1,0:T(8,128)(2,1)} collective-permute-done((bf16[384,768]{1,0:T(8,128)(2,1)}, bf16[384,768]{1,0:T(8,128)(2,1)}, u32[]{:S(2)}, u32[]{:S(2)}) %collective-permute-start.16) | collective-permute-done | bytes 589856 | tf_op jit(solution)/shard_map/ppermute | solution.py:752
  638.3 5.3 collective-permute-done.18
  643.6 12.9 %collective-permute-done.19 = bf16[96,768]{1,0:T(8,128)(2,1)S(1)} collective-permute-done((bf16[96,768]{1,0:T(8,128)(2,1)S(1)}, bf16[96,768]{1,0:T(8,128)(2,1)S(1)}, u32[]{:S(2)}, u32[]{:S(2)}) %collective-permute-start.19) | collective-permute-done | bytes 147488 | tf_op jit(solution)/shard_map/ppermute | solution.py:752
  656.7 6.0 collective-permute-start.21
  667.9 10.7 %collective-permute-done.22 = bf16[96,768]{1,0:T(8,128)(2,1)S(1)} collective-permute-done((bf16[96,768]{1,0:T(8,128)(2,1)S(1)}, bf16[96,768]{1,0:T(8,128)(2,1)S(1)}, u32[]{:S(2)}, u32[]{:S(2)}) %collective-permute-start.22) | collective-permute-done | bytes 147488 | tf_op jit(solution)/shard_map/ppermute | solution.py:752
  679.6 56.9 %all-reduce.5.cloned.1.call-done = (bf16[524,768]{1,0:T(8,128)(2,1)}, bf16[768,3072]{1,0:T(8,128)(2,1)}, bf16[3072,768]{1,0:T(8,128)(2,1)}, bf16[768,768]{1,0:T(8,128)(2,1)}) async-done(((bf16[524,768]{1,0:T(8,128)(2,1)}, bf16[768,3072]{1,0:T(8,128)(2,1)}, bf16[3072,768]{1,0:T(8,128)(2,1)}, bf16[768,768]{1,0:T(8,128)(2,1)}), (bf16[524,768]{1,0:T(8,128)(2,1)}, bf16[768,3072]{1,0:T(8,128)(2,1)}, ...) | async-done | bytes 11421712 | tf_op jit(solution)/shard_map/psum | solution.py:870
  736.5 7.5 convert_element_type.148
  744.0 4.5 convert_element_type.149
  755.5 10.8 %collective-permute-done.24 = bf16[384,768]{1,0:T(8,128)(2,1)S(1)} collective-permute-done((bf16[384,768]{1,0:T(8,128)(2,1)S(1)}, bf16[384,768]{1,0:T(8,128)(2,1)S(1)}, u32[]{:S(2)}, u32[]{:S(2)}) %collective-permute-start.24) | collective-permute-done | bytes 589856 | tf_op jit(solution)/shard_map/ppermute | solution.py:752
  766.3 12.3 %collective-permute-done.25 = bf16[384,768]{1,0:T(8,128)(2,1)S(1)} collective-permute-done((bf16[384,768]{1,0:T(8,128)(2,1)S(1)}, bf16[384,768]{1,0:T(8,128)(2,1)S(1)}, u32[]{:S(2)}, u32[]{:S(2)}) %collective-permute-start.25) | collective-permute-done | bytes 589856 | tf_op jit(solution)/shard_map/ppermute | solution.py:752
  790.4 3.1 slice_convert_fusion
  (224 shorter events, 70.3 us)
Async XLA Ops:
  7.2 203.0 %all-gather.7.cloned.1.call-start = ((), (), s32[]{:S(2)}) async-start(), calls=%async_computation | async-start | bytes 13369344 | tf_op jit(solution)/shard_map/all_gather | solution.py:69
  10.0 22.2 %collective-permute-start.1 = (bf16[512,768]{1,0:T(8,128)(2,1)}, bf16[512,768]{1,0:T(8,128)(2,1)S(1)}, u32[]{:S(2)}, u32[]{:S(2)}) collective-permute-start(bf16[512,768]{1,0:T(8,128)(2,1)} %get-tuple-element.102.refs_0_.tokens), channel_id=1, source_target_pairs={{0,4},{1,5},{2,6},{3,7},{4,8},{5,9},{6,10},{7,11},{8,12},{9,13},{1... | collective-permute-start | bytes 2359304 | tf_op jit(solution)/shard_map/ppermute | solution.py:56
  15.1 21.2 %collective-permute-start.2 = (bf16[512,768]{1,0:T(8,128)(2,1)}, bf16[512,768]{1,0:T(8,128)(2,1)}, u32[]{:S(2)}, u32[]{:S(2)}) collective-permute-start(bf16[512,768]{1,0:T(8,128)(2,1)} %get-tuple-element.102.refs_0_.tokens), channel_id=1, source_target_pairs={{4,0},{5,1},{6,2},{7,3},{8,4},{9,5},{10,6},{11,7},{12,8},{13,9},{1... | collective-permute-start | bytes 2359304 | tf_op jit(solution)/shard_map/ppermute | solution.py:56
  16.4 22.5 %collective-permute-start = (bf16[512,768]{1,0:T(8,128)(2,1)}, bf16[512,768]{1,0:T(8,128)(2,1)}, u32[]{:S(2)}, u32[]{:S(2)}) collective-permute-start(bf16[512,768]{1,0:T(8,128)(2,1)} %get-tuple-element.102.refs_0_.tokens), channel_id=1, source_target_pairs={{0,2},{1,3},{2,0},{3,1},{4,6},{5,7},{6,4},{7,5},{8,10},{9,11},{10,... | collective-permute-start | bytes 2359304 | tf_op jit(solution)/shard_map/ppermute | solution.py:56
  37.5 22.4 %collective-permute-start.5 = (bf16[512,768]{1,0:T(8,128)(2,1)S(1)}, bf16[512,768]{1,0:T(8,128)(2,1)S(1)}, u32[]{:S(2)}, u32[]{:S(2)}) collective-permute-start(bf16[512,768]{1,0:T(8,128)(2,1)S(1)} %broadcast_select_fusion), channel_id=1, source_target_pairs={{2,6},{3,7},{4,0},{5,1},{6,10},{7,11},{8,4},{9,5},{10,14},{11,15},... | collective-permute-start | bytes 2359304 | tf_op jit(solution)/shard_map/ppermute | solution.py:56
  38.8 21.1 %collective-permute-start.7 = (bf16[512,768]{1,0:T(8,128)(2,1)}, bf16[512,768]{1,0:T(8,128)(2,1)S(1)}, u32[]{:S(2)}, u32[]{:S(2)}) collective-permute-start(bf16[512,768]{1,0:T(8,128)(2,1)} %get-tuple-element.102.refs_0_.tokens), channel_id=1, source_target_pairs={{0,1},{1,0},{2,3},{3,2},{4,5},{5,4},{6,7},{7,6},{8,9},{9,8},{10,11... | collective-permute-start | bytes 2359304 | tf_op jit(solution)/shard_map/ppermute | solution.py:56
  38.9 22.3 %collective-permute-start.3 = (bf16[512,768]{1,0:T(8,128)(2,1)}, bf16[512,768]{1,0:T(8,128)(2,1)S(1)}, u32[]{:S(2)}, u32[]{:S(2)}) collective-permute-start(bf16[512,768]{1,0:T(8,128)(2,1)} %collective-permute-done.refs_1_), channel_id=1, source_target_pairs={{0,4},{1,5},{2,6},{3,7},{4,8},{5,9},{6,10},{7,11},{8,12},{9,13},{1... | collective-permute-start | bytes 2359304 | tf_op jit(solution)/shard_map/ppermute | solution.py:56
  43.5 30.8 %collective-permute-start.4 = (bf16[512,768]{1,0:T(8,128)(2,1)}, bf16[512,768]{1,0:T(8,128)(2,1)S(1)}, u32[]{:S(2)}, u32[]{:S(2)}) collective-permute-start(bf16[512,768]{1,0:T(8,128)(2,1)} %collective-permute-done.refs_1_), channel_id=1, source_target_pairs={{4,0},{5,1},{6,2},{7,3},{8,4},{9,5},{10,6},{11,7},{12,8},{13,9},{1... | collective-permute-start | bytes 2359304 | tf_op jit(solution)/shard_map/ppermute | solution.py:56
  44.8 29.6 %collective-permute-start.8 = (bf16[512,768]{1,0:T(8,128)(2,1)}, bf16[512,768]{1,0:T(8,128)(2,1)S(1)}, u32[]{:S(2)}, u32[]{:S(2)}) collective-permute-start(bf16[512,768]{1,0:T(8,128)(2,1)} %collective-permute-done.refs_1_), channel_id=1, source_target_pairs={{0,1},{1,0},{2,3},{3,2},{4,5},{5,4},{6,7},{7,6},{8,9},{9,8},{10,11... | collective-permute-start | bytes 2359304 | tf_op jit(solution)/shard_map/ppermute | solution.py:56
  59.9 15.0 %collective-permute-start.6 = (bf16[512,768]{1,0:T(8,128)(2,1)S(1)}, bf16[512,768]{1,0:T(8,128)(2,1)S(1)}, u32[]{:S(2)}, u32[]{:S(2)}) collective-permute-start(bf16[512,768]{1,0:T(8,128)(2,1)S(1)} %collective-permute-done.5), channel_id=1, source_target_pairs={{0,2},{1,3},{2,0},{3,1},{4,6},{5,7},{6,4},{7,5},{8,10},{9,11},{10,... | collective-permute-start | bytes 2359304 | tf_op jit(solution)/shard_map/ppermute | solution.py:56
  59.9 15.1 %collective-permute-start.10 = (bf16[512,768]{1,0:T(8,128)(2,1)}, bf16[512,768]{1,0:T(8,128)(2,1)S(1)}, u32[]{:S(2)}, u32[]{:S(2)}) collective-permute-start(bf16[512,768]{1,0:T(8,128)(2,1)} %collective-permute-done.2.refs_3_), channel_id=1, source_target_pairs={{0,1},{1,0},{2,3},{3,2},{4,5},{5,4},{6,7},{7,6},{8,9},{9,8},{10,11... | collective-permute-start | bytes 2359304 | tf_op jit(solution)/shard_map/ppermute | solution.py:56
  61.2 13.8 %collective-permute-start.9 = (bf16[512,768]{1,0:T(8,128)(2,1)S(1)}, bf16[512,768]{1,0:T(8,128)(2,1)S(1)}, u32[]{:S(2)}, u32[]{:S(2)}) collective-permute-start(bf16[512,768]{1,0:T(8,128)(2,1)S(1)} %collective-permute-done.1.refs_2_), channel_id=1, source_target_pairs={{0,1},{1,0},{2,3},{3,2},{4,5},{5,4},{6,7},{7,6},{8,9},{9,8},{10,11... | collective-permute-start | bytes 2359304 | tf_op jit(solution)/shard_map/ppermute | solution.py:56
  74.3 2.3 collective-permute-start.11
  74.4 3.4 collective-permute-start.12
  74.9 4.0 collective-permute-start.13
  79.8 236.8 %all-gather.9.cloned.1.call-start = ((), (), s32[]{:S(2)}) async-start(), calls=%async_computation.1 | async-start | bytes 14622720 | tf_op jit(solution)/shard_map/all_gather | solution.py:69
  210.1 225.9 %all-gather.11.cloned.1.call-start = ((), (), s32[]{:S(2)}) async-start(), calls=%async_computation.2 | async-start | bytes 14622720 | tf_op jit(solution)/shard_map/all_gather | solution.py:69
  271.3 465.2 %all-reduce.5.cloned.1.call-start = ((), (), s32[]{:S(2)}) async-start(), calls=%async_computation.3 | async-start | bytes 22855680 | tf_op jit(solution)/shard_map/psum | solution.py:870
  493.9 4.7 collective-permute-start.14
  503.0 112.9 %collective-permute-start.15 = (bf16[384,768]{1,0:T(8,128)(2,1)}, bf16[384,768]{1,0:T(8,128)(2,1)S(1)}, u32[]{:S(2)}, u32[]{:S(2)}) collective-permute-start(bf16[384,768]{1,0:T(8,128)(2,1)} %get-tuple-element.221), channel_id=1, source_target_pairs={{0,2},{1,3},{2,0},{3,1},{4,6},{5,7},{6,4},{7,5},{8,10},{9,11},{10,... | collective-permute-start | bytes 1769480 | tf_op jit(solution)/shard_map/ppermute | solution.py:752
  599.7 32.0 %collective-permute-start.16 = (bf16[384,768]{1,0:T(8,128)(2,1)}, bf16[384,768]{1,0:T(8,128)(2,1)}, u32[]{:S(2)}, u32[]{:S(2)}) collective-permute-start(bf16[384,768]{1,0:T(8,128)(2,1)} %get-tuple-element.223), channel_id=1, source_target_pairs={{0,16},{1,17},{2,18},{3,19},{4,20},{5,21},{6,22},{7,23},{8,24},{9,... | collective-permute-start | bytes 1769480 | tf_op jit(solution)/shard_map/ppermute | solution.py:752
  599.7 32.0 %collective-permute-start.17 = (bf16[384,768]{1,0:T(8,128)(2,1)S(1)}, bf16[384,768]{1,0:T(8,128)(2,1)}, u32[]{:S(2)}, u32[]{:S(2)}) collective-permute-start(bf16[384,768]{1,0:T(8,128)(2,1)S(1)} %get-tuple-element.222), channel_id=1, source_target_pairs={{0,18},{1,19},{2,16},{3,17},{4,22},{5,23},{6,20},{7,21},{8,26},{9,... | collective-permute-start | bytes 1769480 | tf_op jit(solution)/shard_map/ppermute | solution.py:752
  633.3 10.3 %collective-permute-start.18 = (bf16[96,768]{1,0:T(8,128)(2,1)S(1)}, bf16[96,768]{1,0:T(8,128)(2,1)S(1)}, u32[]{:S(2)}, u32[]{:S(2)}) collective-permute-start(bf16[96,768]{1,0:T(8,128)(2,1)S(1)} %get-tuple-element.228), channel_id=1, source_target_pairs={{0,4},{1,5},{2,6},{3,7},{4,0},{5,1},{6,2},{7,3},{8,12},{9,13},{10,... | collective-permute-start | bytes 442376 | tf_op jit(solution)/shard_map/ppermute | solution.py:752
  635.9 20.7 %collective-permute-start.19 = (bf16[96,768]{1,0:T(8,128)(2,1)S(1)}, bf16[96,768]{1,0:T(8,128)(2,1)S(1)}, u32[]{:S(2)}, u32[]{:S(2)}) collective-permute-start(bf16[96,768]{1,0:T(8,128)(2,1)S(1)} %get-tuple-element.230), channel_id=1, source_target_pairs={{0,8},{1,9},{2,10},{3,11},{4,12},{5,13},{6,14},{7,15},{8,0},{9,1},... | collective-permute-start | bytes 442376 | tf_op jit(solution)/shard_map/ppermute | solution.py:752
  635.9 20.7 %collective-permute-start.20 = (bf16[96,768]{1,0:T(8,128)(2,1)S(1)}, bf16[96,768]{1,0:T(8,128)(2,1)S(1)}, u32[]{:S(2)}, u32[]{:S(2)}) collective-permute-start(bf16[96,768]{1,0:T(8,128)(2,1)S(1)} %get-tuple-element.229), channel_id=1, source_target_pairs={{0,12},{1,13},{2,14},{3,15},{4,8},{5,9},{6,10},{7,11},{8,4},{9,5},... | collective-permute-start | bytes 442376 | tf_op jit(solution)/shard_map/ppermute | solution.py:752
  656.7 11.2 %collective-permute-start.21 = (bf16[96,768]{1,0:T(8,128)(2,1)S(1)}, bf16[96,768]{1,0:T(8,128)(2,1)S(1)}, u32[]{:S(2)}, u32[]{:S(2)}) collective-permute-start(bf16[96,768]{1,0:T(8,128)(2,1)S(1)} %get-tuple-element.217), channel_id=1, source_target_pairs={{0,4},{1,5},{2,6},{3,7},{4,0},{5,1},{6,2},{7,3},{8,12},{9,13},{10,... | collective-permute-start | bytes 442376 | tf_op jit(solution)/shard_map/ppermute | solution.py:752
  662.7 15.9 %collective-permute-start.22 = (bf16[96,768]{1,0:T(8,128)(2,1)S(1)}, bf16[96,768]{1,0:T(8,128)(2,1)S(1)}, u32[]{:S(2)}, u32[]{:S(2)}) collective-permute-start(bf16[96,768]{1,0:T(8,128)(2,1)S(1)} %get-tuple-element.217), channel_id=1, source_target_pairs={{0,8},{1,9},{2,10},{3,11},{4,12},{5,13},{6,14},{7,15},{8,0},{9,1},... | collective-permute-start | bytes 442376 | tf_op jit(solution)/shard_map/ppermute | solution.py:752
  665.3 14.2 %collective-permute-start.23 = (bf16[96,768]{1,0:T(8,128)(2,1)S(1)}, bf16[96,768]{1,0:T(8,128)(2,1)S(1)}, u32[]{:S(2)}, u32[]{:S(2)}) collective-permute-start(bf16[96,768]{1,0:T(8,128)(2,1)S(1)} %get-tuple-element.217), channel_id=1, source_target_pairs={{0,12},{1,13},{2,14},{3,15},{4,8},{5,9},{6,10},{7,11},{8,4},{9,5},... | collective-permute-start | bytes 442376 | tf_op jit(solution)/shard_map/ppermute | solution.py:752
  750.1 16.2 %collective-permute-start.24 = (bf16[384,768]{1,0:T(8,128)(2,1)S(1)}, bf16[384,768]{1,0:T(8,128)(2,1)S(1)}, u32[]{:S(2)}, u32[]{:S(2)}) collective-permute-start(bf16[384,768]{1,0:T(8,128)(2,1)S(1)} %constant_dynamic-update-slice_fusion.6), channel_id=1, source_target_pairs={{0,2},{1,3},{2,0},{3,1},{4,6},{5,7},{6,4},{7,5},{8,10},{9,11},{10,... | collective-permute-start | bytes 1769480 | tf_op jit(solution)/shard_map/ppermute | solution.py:752
  751.0 27.6 %collective-permute-start.25 = (bf16[384,768]{1,0:T(8,128)(2,1)S(1)}, bf16[384,768]{1,0:T(8,128)(2,1)S(1)}, u32[]{:S(2)}, u32[]{:S(2)}) collective-permute-start(bf16[384,768]{1,0:T(8,128)(2,1)S(1)} %constant_dynamic-update-slice_fusion.6), channel_id=1, source_target_pairs={{0,16},{1,17},{2,18},{3,19},{4,20},{5,21},{6,22},{7,23},{8,24},{9,... | collective-permute-start | bytes 1769480 | tf_op jit(solution)/shard_map/ppermute | solution.py:752
  752.4 26.3 %collective-permute-start.26 = (bf16[384,768]{1,0:T(8,128)(2,1)S(1)}, bf16[384,768]{1,0:T(8,128)(2,1)S(1)}, u32[]{:S(2)}, u32[]{:S(2)}) collective-permute-start(bf16[384,768]{1,0:T(8,128)(2,1)S(1)} %constant_dynamic-update-slice_fusion.6), channel_id=1, source_target_pairs={{0,18},{1,19},{2,16},{3,17},{4,22},{5,23},{6,20},{7,21},{8,26},{9,... | collective-permute-start | bytes 1769480 | tf_op jit(solution)/shard_map/ppermute | solution.py:752
  778.7 9.8 %collective-permute-start.27 = (bf16[1536,768]{1,0:T(8,128)(2,1)S(1)}, bf16[1536,768]{1,0:T(8,128)(2,1)}, u32[]{:S(2)}, u32[]{:S(2)}) collective-permute-start(bf16[1536,768]{1,0:T(8,128)(2,1)S(1)} %constant_dynamic-update-slice_fusion.2), channel_id=1, source_target_pairs={{0,1},{1,0},{2,3},{3,2},{4,5},{5,4},{6,7},{7,6},{8,9},{9,8},{10,11... | collective-permute-start | bytes 7077896 | tf_op jit(solution)/shard_map/ppermute | solution.py:752
  (53 other events, 1222.1 us)
Sparse Core Ops, SparseCore 0:
  80.0 100.9 all-gather.6
  210.2 106.3 all-gather.8
  319.5 108.5 all-gather.10
  436.1 300.3 all-reduce.4

commit v4 on v3

--- a/solution.py
+++ b/solution.py
@@ -57,12 +57,26 @@
 
 
 def gather_near(value):
+    steps = near_steps(value)
+    parts = next(steps)
+    while True:
+        try:
+            parts = steps.send(parts)
+        except StopIteration as done:
+            return done.value
+
+
+def near_steps(value):
     side = (lax.axis_index("blk") >> 1) & 1
-    below, above, beside = move(value, UP), move(value, DOWN), move(value, SIDE)
+    below, above, beside = yield [move(value, pairs) for pairs in (UP, DOWN, SIDE)]
     far = move(jnp.where(side == 1, below, above), OUTWARD)
-    moved = [move(beside, UP), move(beside, DOWN), move(far, SIDE)]
-    here = [value, beside, below, above] + moved
-    return here + [move(part, CORE) for part in here]
+    moved = [far, move(beside, UP), move(beside, DOWN)]
+    cores = [move(part, CORE) for part in (value, beside, below, above)]
+    far, beside_below, beside_above, *cores = yield moved + cores
+    far = move(far, SIDE)
+    far, *more = yield [far] + [move(part, CORE) for part in (beside_below, beside_above)]
+    here = [value, beside, below, above, beside_below, beside_above, far]
+    return here + cores + more + [move(far, CORE)]
 
 
 def gather_all(value):
@@ -808,6 +822,9 @@
         attended, lse, *chain_rows = attend_forward(
             meta, pieces[b], memory[b], (query_proj, query_bias, key_proj, value_proj, value_bias)
         )
+        if b == 1:
+            attended, parts = lax.optimization_barrier((attended, parts))
+            parts = steps.send(parts)
         (
             final, final_mem, payload, mem_grad, mem_stats, own_stats, res_grad, rows,
             attended_low, branch, first_low, inner, active, outer, sums, inner_sum,
@@ -820,6 +837,12 @@
         )
         if b + 1 < batches:
             meta_of[b + 1], payload = lax.optimization_barrier((meta_of[b + 1], payload))
+        if b == 0:
+            steps = near_steps(payload)
+            parts = next(steps)
+        if b == 1:
+            payload, parts = lax.optimization_barrier((payload, parts))
+            parts = steps.send(parts)
         states.append(
             dict(
                 meta=meta, rows=rows, chain_rows=chain_rows, payload=payload, mem_grad=mem_grad,
@@ -854,10 +877,15 @@
             0,
         ),
     )
-    early, *held = lax.optimization_barrier((early, *[s["meta"] for s in states]))
+    early, parts, *held = lax.optimization_barrier((early, parts, *[s["meta"] for s in states]))
     for s, meta in zip(states, held):
         s["meta"] = meta
-        s["gathered"] = gather_all(s["payload"])
+        if s is not states[0]:
+            s["gathered"] = gather_all(s["payload"])
+    try:
+        steps.send(parts)
+    except StopIteration as done:
+        states[0]["gathered"] = done.value
     for s in states:
         s["grads"] = attend_backward(
             s["meta"], s["gathered"], s["chain_rows"], s["mem_grad"], s["mem_stats"],

time: 789 us -> 835 us (1.058); the launches traced: 802 us -> 839 us
  starting transfers between devices: 132 us -> 241 us
  Pallas kernels: 358 us -> 257 us
  waiting for transfers between devices: 217 us -> 243 us
    ppermute x14 -> x28, starting transfers between devices: 16.1 us -> 131 us  [move(): return lax.ppermute(value, 'blk', pairs)]
    pallas_call x2, Pallas kernels: 160 us -> 108 us  [attend_backward(): pl.pallas_call(functools.partial(backward_body, start, count), grid_spec=...]
    pallas_call x2, Pallas kernels: 121 us -> 72.8 us  [attend_forward(): pl.pallas_call(forward_body, grid_spec=pltpu.PrefetchScalarGridSpec(num_s...]
    ppermute x14 -> x28, waiting for transfers between devices: 51.4 us -> 81.6 us  [move(): return lax.ppermute(value, 'blk', pairs)]
    ppermute x14, waiting for transfers between devices: 87.8 us -> 78.6 us  [swap(): lax.ppermute(value, ('dp', 'blk'), [(i, i ^ mask) for i in range(sizes)])]
    all_gather x3 -> x2, waiting for transfers between devices: 21 us -> 26.9 us  [gather_all(): return [lax.all_gather(value, 'blk')]]
  transfers between devices with their start and end apart: 32 -> 45, of which waited for: 20 -> 22; matrix products, arithmetic and copies ran while one was open for 7% -> 6% of each run, Pallas kernels for 45% -> 31%
where the time goes in v4:
time: 835 us; the launch traced here: 839 us
  Pallas kernels  257 us (31%)
  waiting for transfers between devices  243 us (29%)
  starting transfers between devices  241 us (29%)
  other arithmetic  31.7 us (4%)
  local copies, waits for them, and re-layouts  27.3 us (3%)
  matrix products  24 us (3%)
  between operations  15 us (2%)
    ppermute x28, starting transfers between devices, move(): return lax.ppermute(value, 'blk', pairs)  131 us
    ppermute x14, starting transfers between devices, swap(): lax.ppermute(value, ('dp', 'blk'), [(i, i ^ mask) for i in range(sizes)])  110 us
    pallas_call x2, Pallas kernels, attend_backward(): pl.pallas_call(functools.partial(backward_body, start, count), grid_spec=...  108 us
    ppermute x28, waiting for transfers between devices, move(): return lax.ppermute(value, 'blk', pairs)  81.6 us
    ppermute x14, waiting for transfers between devices, swap(): lax.ppermute(value, ('dp', 'blk'), [(i, i ^ mask) for i in range(sizes)])  78.6 us
    pallas_call x2, Pallas kernels, attend_forward(): pl.pallas_call(forward_body, grid_spec=pltpu.PrefetchScalarGridSpec(num_s...  72.8 us
    pallas_call x2, Pallas kernels, middle(): pl.pallas_call(middle_body, in_specs=[pl.BlockSpec(memory_space=pltpu.SME...  59.3 us
    psum x1, waiting for transfers between devices, local(): early = lax.psum(early, ('dp', 'blk'))  55.8 us
  transfers between devices with their start and end apart: 45, of which 22 were waited for; matrix products, arithmetic and copies ran while one was open for 6% of the time, Pallas kernels for 31%

profile of v4, /device:TPU:0, one launch (start us, length us, event | category | flops | bytes accessed | tf_op | source)
XLA Modules:
  0.0 838.9 jit_solution(5616753390165484639)
XLA Ops:
  10.0 5.1 collective-permute-start.1
  17.9 14.2 %collective-permute-done.1.refs_2_ = bf16[512,768]{1,0:T(8,128)(2,1)S(1)} collective-permute-done((bf16[512,768]{1,0:T(8,128)(2,1)}, bf16[512,768]{1,0:T(8,128)(2,1)S(1)}, u32[]{:S(2)}, u32[]{:S(2)}) %collective-permute-start.1) | collective-permute-done | bytes 786464 | tf_op jit(solution)/shard_map/ppermute | solution.py:56
  32.1 4.2 collective-permute-done.2.refs_3_
  38.9 4.6 collective-permute-start.3
  45.1 14.8 %collective-permute-done.5 = bf16[512,768]{1,0:T(8,128)(2,1)S(1)} collective-permute-done((bf16[512,768]{1,0:T(8,128)(2,1)S(1)}, bf16[512,768]{1,0:T(8,128)(2,1)S(1)}, u32[]{:S(2)}, u32[]{:S(2)}) %collective-permute-start.5) | collective-permute-done | bytes 786464 | tf_op jit(solution)/shard_map/ppermute | solution.py:56
  61.2 13.1 %collective-permute-done.4.refs_5_ = bf16[512,768]{1,0:T(8,128)(2,1)S(1)} collective-permute-done((bf16[512,768]{1,0:T(8,128)(2,1)}, bf16[512,768]{1,0:T(8,128)(2,1)S(1)}, u32[]{:S(2)}, u32[]{:S(2)}) %collective-permute-start.4) | collective-permute-done | bytes 786464 | tf_op jit(solution)/shard_map/ppermute | solution.py:56
  90.2 26.1 %attend_forward.2 = (f32[544,768]{1,0:T(8,128)}, f32[544,128]{1,0:T(8,128)}, bf16[4096,768]{1,0:T(8,128)(2,1)}, bf16[4096,768]{1,0:T(8,128)(2,1)}, bf16[4096,768]{1,0:T(8,128)(2,1)}) custom-call(s32[16]{0:T(128)} %get-tuple-element.167.meta, bf16[512,768]{1,0:T(8,128)(2,1)} %get-tuple-element.117.refs_0_.tokens, ...), custom_call_target="tpu_custom_call" | custom-call | flops 40000000000 | bytes 30000000 | tf_op jit(solution)/shard_map/attend_forward/pallas_call | solution.py:300
  116.3 29.7 %middle.2 = (bf16[512,768]{1,0:T(8,128)(2,1)}, bf16[32,768]{1,0:T(8,128)(2,1)}, bf16[560,768]{1,0:T(8,128)(2,1)}, bf16[32,768]{1,0:T(8,128)(2,1)}, f32[24,128]{1...) custom-call(s32[16]{0:T(128)} %get-tuple-element.167.meta, ...), custom_call_target="tpu_custom_call" | custom-call | flops 12000000000 | bytes 40000000 | tf_op jit(solution)/shard_map/middle/pallas_call | solution.py:647
  146.0 27.9 %collective-permute-start.14 = (bf16[560,768]{1,0:T(8,128)(2,1)}, bf16[560,768]{1,0:T(8,128)(2,1)S(1)}, u32[]{:S(2)}, u32[]{:S(2)}) collective-permute-start(bf16[560,768]{1,0:T(8,128)(2,1)} %get-tuple-element.138.refs_0_), channel_id=1, source_target_pairs={{0,4},{1,5},{2,6},{3,7},{4,8},{5,9},{6,10},{7,11},{8,12},{9,13},{1... | collective-permute-start | bytes 2580488 | tf_op jit(solution)/shard_map/ppermute | solution.py:56
  175.2 41.3 %collective-permute-start.16 = (bf16[560,768]{1,0:T(8,128)(2,1)}, bf16[560,768]{1,0:T(8,128)(2,1)S(1)}, u32[]{:S(2)}, u32[]{:S(2)}) collective-permute-start(bf16[560,768]{1,0:T(8,128)(2,1)} %get-tuple-element.138.refs_0_), channel_id=1, source_target_pairs={{0,2},{1,3},{2,0},{3,1},{4,6},{5,7},{6,4},{7,5},{8,10},{9,11},{10,... | collective-permute-start | bytes 2580488 | tf_op jit(solution)/shard_map/ppermute | solution.py:56
  216.5 46.7 %attend_forward.3 = (f32[544,768]{1,0:T(8,128)}, f32[544,128]{1,0:T(8,128)}, bf16[4096,768]{1,0:T(8,128)(2,1)}, bf16[4096,768]{1,0:T(8,128)(2,1)}, bf16[4096,768]{1,0:T(8,128)(2,1)}) custom-call(s32[16]{0:T(128)} %get-tuple-element.195.meta, bf16[16,512,768]{2,1,0:T(8,128)(2,1)} %bitcast.59, bf16[4,32,768]{2,1,0:T(8,128)(2,1)} %get-tuple-element.263.refs_1_.memory, ...), custom_call_target="tpu_custom_call" | custom-call | flops 40000000000 | bytes 30000000 | tf_op jit(solution)/shard_map/attend_forward/pallas_call | solution.py:300
  264.7 40.2 %collective-permute-start.18 = (bf16[560,768]{1,0:T(8,128)(2,1)S(1)}, bf16[560,768]{1,0:T(8,128)(2,1)}, u32[]{:S(2)}, u32[]{:S(2)}) collective-permute-start(bf16[560,768]{1,0:T(8,128)(2,1)S(1)} %collective-permute-done.16.refs_1_), channel_id=1, source_target_pairs={{0,4},{1,5},{2,6},{3,7},{4,8},{5,9},{6,10},{7,11},{8,12},{9,13},{1... | collective-permute-start | bytes 2580488 | tf_op jit(solution)/shard_map/ppermute | solution.py:56
  306.8 15.2 %collective-permute-done.17 = bf16[560,768]{1,0:T(8,128)(2,1)S(1)} collective-permute-done((bf16[560,768]{1,0:T(8,128)(2,1)S(1)}, bf16[560,768]{1,0:T(8,128)(2,1)S(1)}, u32[]{:S(2)}, u32[]{:S(2)}) %collective-permute-start.17) | collective-permute-done | bytes 860192 | tf_op jit(solution)/shard_map/ppermute | solution.py:56
  323.0 29.6 %middle.3 = (bf16[512,768]{1,0:T(8,128)(2,1)}, bf16[32,768]{1,0:T(8,128)(2,1)}, bf16[560,768]{1,0:T(8,128)(2,1)}, bf16[32,768]{1,0:T(8,128)(2,1)}, f32[24,128]{1...) custom-call(s32[16]{0:T(128)} %get-tuple-element.195.meta, ...), custom_call_target="tpu_custom_call" | custom-call | flops 12000000000 | bytes 40000000 | tf_op jit(solution)/shard_map/middle/pallas_call | solution.py:647
  361.4 8.2 fusion.8
  370.0 8.0 fusion.11
  378.0 12.5 %collective-permute-done.24.refs_6_ = bf16[560,768]{1,0:T(8,128)(2,1)S(1)} collective-permute-done((bf16[560,768]{1,0:T(8,128)(2,1)S(1)}, bf16[560,768]{1,0:T(8,128)(2,1)S(1)}, u32[]{:S(2)}, u32[]{:S(2)}) %collective-permute-start.24) | collective-permute-done | bytes 860192 | tf_op jit(solution)/shard_map/ppermute | solution.py:56
  394.0 42.1 %attend_backward.2 = (bf16[544,768]{1,0:T(8,128)(2,1)}, bf16[544,768]{1,0:T(8,128)(2,1)}, bf16[544,768]{1,0:T(8,128)(2,1)}) custom-call(s32[16]{0:T(128)} %get-tuple-element.167.meta, bf16[560,768]{1,0:T(8,128)(2,1)} %get-tuple-element.138.refs_0_, bf16[560,768]{1,0:T(8,128)(2,1)} %copy-done.33, bf16[560,768]{1,0:T(8,128)(2,1)} %copy-done.10, ...), custom_call_target="tpu_custom_call" | custom-call | flops 10000000000 | bytes 1000000 | tf_op jit(solution)/shard_map/attend_backward/pallas_call | solution.py:441
  436.0 26.9 %all-gather.7.cloned.1.call-done = bf16[8960,768]{1,0:T(8,128)(2,1)} async-done(((bf16[560,768]{1,0:T(8,128)(2,1)}), bf16[8960,768]{1,0:T(8,128)(2,1)}) %all-gather.7.cloned.1.call-update) | async-done | bytes 13762576 | tf_op jit(solution)/shard_map/all_gather | solution.py:83
  463.0 66.3 %attend_backward.3 = (bf16[544,768]{1,0:T(8,128)(2,1)}, bf16[544,768]{1,0:T(8,128)(2,1)}, bf16[544,768]{1,0:T(8,128)(2,1)}) custom-call(s32[16]{0:T(128)} %get-tuple-element.195.meta, bf16[16,560,768]{2,1,0:T(8,128)(2,1)} %bitcast.58, bf16[4096,768]{1,0:T(8,128)(2,1)} %get-tuple-element.197.refs_1_, bf16[4096,768]{1,0:T(8,128)(2,1)} %get-tuple-element.198.refs_2_, ...), custom_call_target="tpu_custom_call" | custom-call | flops 10000000000 | bytes 1000000 | tf_op jit(solution)/shard_map/attend_backward/pallas_call | solution.py:441
  529.3 15.0 %late_sums.1 = bf16[3072,768]{1,0:T(8,128)(2,1)} custom-call(s32[2,16]{1,0:T(2,128)} %find_chain.1.metas, s32[1]{0:T(128)} %bitcast.24.group, bf16[544,768]{1,0:T(8,128)(2,1)} %get-tuple-element.206.refs_0_, bf16[544,768]{1,0:T(8,128)(2,1)} %get-tuple-element.207.refs_1_, f32[544,768]{1,0:T(8,128)} %get-tuple-element.190.refs_2_, ...), custom_call_target="tpu_custom_call" | custom-call | tf_op jit(solution)/shard_map/late_sums/pallas_call | solution.py:749
  546.5 4.8 collective-permute-done.28
  555.7 79.4 %collective-permute-start.31 = (bf16[384,768]{1,0:T(8,128)(2,1)}, bf16[384,768]{1,0:T(8,128)(2,1)S(1)}, u32[]{:S(2)}, u32[]{:S(2)}) collective-permute-start(bf16[384,768]{1,0:T(8,128)(2,1)} %get-tuple-element.252), channel_id=1, source_target_pairs={{0,18},{1,19},{2,16},{3,17},{4,22},{5,23},{6,20},{7,21},{8,26},{9,... | collective-permute-start | bytes 1769480 | tf_op jit(solution)/shard_map/ppermute | solution.py:766
  637.5 13.9 %collective-permute-done.31 = bf16[384,768]{1,0:T(8,128)(2,1)S(1)} collective-permute-done((bf16[384,768]{1,0:T(8,128)(2,1)}, bf16[384,768]{1,0:T(8,128)(2,1)S(1)}, u32[]{:S(2)}, u32[]{:S(2)}) %collective-permute-start.31) | collective-permute-done | bytes 589856 | tf_op jit(solution)/shard_map/ppermute | solution.py:766
  651.4 14.3 %collective-permute-done.30 = bf16[384,768]{1,0:T(8,128)(2,1)} collective-permute-done((bf16[384,768]{1,0:T(8,128)(2,1)}, bf16[384,768]{1,0:T(8,128)(2,1)}, u32[]{:S(2)}, u32[]{:S(2)}) %collective-permute-start.30) | collective-permute-done | bytes 589856 | tf_op jit(solution)/shard_map/ppermute | solution.py:766
  667.5 19.6 %collective-permute-start.33 = (bf16[96,768]{1,0:T(8,128)(2,1)S(1)}, bf16[96,768]{1,0:T(8,128)(2,1)S(1)}, u32[]{:S(2)}, u32[]{:S(2)}) collective-permute-start(bf16[96,768]{1,0:T(8,128)(2,1)S(1)} %get-tuple-element.260), channel_id=1, source_target_pairs={{0,8},{1,9},{2,10},{3,11},{4,12},{5,13},{6,14},{7,15},{8,0},{9,1},... | collective-permute-start | bytes 442376 | tf_op jit(solution)/shard_map/ppermute | solution.py:766
  687.5 12.4 %collective-permute-done.33 = bf16[96,768]{1,0:T(8,128)(2,1)S(1)} collective-permute-done((bf16[96,768]{1,0:T(8,128)(2,1)S(1)}, bf16[96,768]{1,0:T(8,128)(2,1)S(1)}, u32[]{:S(2)}, u32[]{:S(2)}) %collective-permute-start.33) | collective-permute-done | bytes 147488 | tf_op jit(solution)/shard_map/ppermute | solution.py:766
  717.5 55.8 %all-reduce.5.cloned.1.call-done = (bf16[524,768]{1,0:T(8,128)(2,1)}, bf16[768,3072]{1,0:T(8,128)(2,1)}, bf16[3072,768]{1,0:T(8,128)(2,1)}, bf16[768,768]{1,0:T(8,128)(2,1)}) async-done(((bf16[524,768]{1,0:T(8,128)(2,1)}, bf16[768,3072]{1,0:T(8,128)(2,1)}, bf16[3072,768]{1,0:T(8,128)(2,1)}, bf16[768,768]{1,0:T(8,128)(2,1)}), (bf16[524,768]{1,0:T(8,128)(2,1)}, bf16[768,3072]{1,0:T(8,128)(2,1)}, ...) | async-done | bytes 11421712 | tf_op jit(solution)/shard_map/psum | solution.py:898
  773.3 7.5 convert_element_type.148
  780.8 4.5 convert_element_type.149
  792.3 10.8 %collective-permute-done.38 = bf16[384,768]{1,0:T(8,128)(2,1)S(1)} collective-permute-done((bf16[384,768]{1,0:T(8,128)(2,1)S(1)}, bf16[384,768]{1,0:T(8,128)(2,1)S(1)}, u32[]{:S(2)}, u32[]{:S(2)}) %collective-permute-start.38) | collective-permute-done | bytes 589856 | tf_op jit(solution)/shard_map/ppermute | solution.py:766
  803.1 12.2 %collective-permute-done.39 = bf16[384,768]{1,0:T(8,128)(2,1)S(1)} collective-permute-done((bf16[384,768]{1,0:T(8,128)(2,1)S(1)}, bf16[384,768]{1,0:T(8,128)(2,1)S(1)}, u32[]{:S(2)}, u32[]{:S(2)}) %collective-permute-start.39) | collective-permute-done | bytes 589856 | tf_op jit(solution)/shard_map/ppermute | solution.py:766
  (270 shorter events, 97.0 us)
Async XLA Ops:
  7.2 209.3 %all-gather.5.cloned.1.call-start = ((), (), s32[]{:S(2)}) async-start(), calls=%async_computation | async-start | bytes 13369344 | tf_op jit(solution)/shard_map/all_gather | solution.py:83
  10.0 22.2 %collective-permute-start.1 = (bf16[512,768]{1,0:T(8,128)(2,1)}, bf16[512,768]{1,0:T(8,128)(2,1)S(1)}, u32[]{:S(2)}, u32[]{:S(2)}) collective-permute-start(bf16[512,768]{1,0:T(8,128)(2,1)} %get-tuple-element.117.refs_0_.tokens), channel_id=1, source_target_pairs={{0,4},{1,5},{2,6},{3,7},{4,8},{5,9},{6,10},{7,11},{8,12},{9,13},{1... | collective-permute-start | bytes 2359304 | tf_op jit(solution)/shard_map/ppermute | solution.py:56
  15.1 21.2 %collective-permute-start.2 = (bf16[512,768]{1,0:T(8,128)(2,1)}, bf16[512,768]{1,0:T(8,128)(2,1)}, u32[]{:S(2)}, u32[]{:S(2)}) collective-permute-start(bf16[512,768]{1,0:T(8,128)(2,1)} %get-tuple-element.117.refs_0_.tokens), channel_id=1, source_target_pairs={{4,0},{5,1},{6,2},{7,3},{8,4},{9,5},{10,6},{11,7},{12,8},{13,9},{1... | collective-permute-start | bytes 2359304 | tf_op jit(solution)/shard_map/ppermute | solution.py:56
  16.4 22.5 %collective-permute-start = (bf16[512,768]{1,0:T(8,128)(2,1)}, bf16[512,768]{1,0:T(8,128)(2,1)}, u32[]{:S(2)}, u32[]{:S(2)}) collective-permute-start(bf16[512,768]{1,0:T(8,128)(2,1)} %get-tuple-element.117.refs_0_.tokens), channel_id=1, source_target_pairs={{0,2},{1,3},{2,0},{3,1},{4,6},{5,7},{6,4},{7,5},{8,10},{9,11},{10,... | collective-permute-start | bytes 2359304 | tf_op jit(solution)/shard_map/ppermute | solution.py:56
  37.5 22.4 %collective-permute-start.5 = (bf16[512,768]{1,0:T(8,128)(2,1)S(1)}, bf16[512,768]{1,0:T(8,128)(2,1)S(1)}, u32[]{:S(2)}, u32[]{:S(2)}) collective-permute-start(bf16[512,768]{1,0:T(8,128)(2,1)S(1)} %broadcast_select_fusion.1), channel_id=1, source_target_pairs={{2,6},{3,7},{4,0},{5,1},{6,10},{7,11},{8,4},{9,5},{10,14},{11,15},... | collective-permute-start | bytes 2359304 | tf_op jit(solution)/shard_map/ppermute | solution.py:56
  38.8 21.1 %collective-permute-start.7 = (bf16[512,768]{1,0:T(8,128)(2,1)}, bf16[512,768]{1,0:T(8,128)(2,1)S(1)}, u32[]{:S(2)}, u32[]{:S(2)}) collective-permute-start(bf16[512,768]{1,0:T(8,128)(2,1)} %get-tuple-element.117.refs_0_.tokens), channel_id=1, source_target_pairs={{0,1},{1,0},{2,3},{3,2},{4,5},{5,4},{6,7},{7,6},{8,9},{9,8},{10,11... | collective-permute-start | bytes 2359304 | tf_op jit(solution)/shard_map/ppermute | solution.py:56
  38.9 22.3 %collective-permute-start.3 = (bf16[512,768]{1,0:T(8,128)(2,1)}, bf16[512,768]{1,0:T(8,128)(2,1)S(1)}, u32[]{:S(2)}, u32[]{:S(2)}) collective-permute-start(bf16[512,768]{1,0:T(8,128)(2,1)} %collective-permute-done.refs_1_), channel_id=1, source_target_pairs={{0,4},{1,5},{2,6},{3,7},{4,8},{5,9},{6,10},{7,11},{8,12},{9,13},{1... | collective-permute-start | bytes 2359304 | tf_op jit(solution)/shard_map/ppermute | solution.py:56
  43.5 30.8 %collective-permute-start.4 = (bf16[512,768]{1,0:T(8,128)(2,1)}, bf16[512,768]{1,0:T(8,128)(2,1)S(1)}, u32[]{:S(2)}, u32[]{:S(2)}) collective-permute-start(bf16[512,768]{1,0:T(8,128)(2,1)} %collective-permute-done.refs_1_), channel_id=1, source_target_pairs={{4,0},{5,1},{6,2},{7,3},{8,4},{9,5},{10,6},{11,7},{12,8},{13,9},{1... | collective-permute-start | bytes 2359304 | tf_op jit(solution)/shard_map/ppermute | solution.py:56
  44.8 29.6 %collective-permute-start.8 = (bf16[512,768]{1,0:T(8,128)(2,1)}, bf16[512,768]{1,0:T(8,128)(2,1)S(1)}, u32[]{:S(2)}, u32[]{:S(2)}) collective-permute-start(bf16[512,768]{1,0:T(8,128)(2,1)} %collective-permute-done.refs_1_), channel_id=1, source_target_pairs={{0,1},{1,0},{2,3},{3,2},{4,5},{5,4},{6,7},{7,6},{8,9},{9,8},{10,11... | collective-permute-start | bytes 2359304 | tf_op jit(solution)/shard_map/ppermute | solution.py:56
  79.8 383.1 %all-gather.7.cloned.1.call-start = ((), (), s32[]{:S(2)}) async-start(), calls=%async_computation.1 | async-start | bytes 14622720 | tf_op jit(solution)/shard_map/all_gather | solution.py:83
  146.0 117.3 %collective-permute-start.14 = (bf16[560,768]{1,0:T(8,128)(2,1)}, bf16[560,768]{1,0:T(8,128)(2,1)S(1)}, u32[]{:S(2)}, u32[]{:S(2)}) collective-permute-start(bf16[560,768]{1,0:T(8,128)(2,1)} %get-tuple-element.138.refs_0_), channel_id=1, source_target_pairs={{0,4},{1,5},{2,6},{3,7},{4,8},{5,9},{6,10},{7,11},{8,12},{9,13},{1... | collective-permute-start | bytes 2580488 | tf_op jit(solution)/shard_map/ppermute | solution.py:56
  173.9 89.4 %collective-permute-start.15 = (bf16[560,768]{1,0:T(8,128)(2,1)}, bf16[560,768]{1,0:T(8,128)(2,1)S(1)}, u32[]{:S(2)}, u32[]{:S(2)}) collective-permute-start(bf16[560,768]{1,0:T(8,128)(2,1)} %get-tuple-element.138.refs_0_), channel_id=1, source_target_pairs={{4,0},{5,1},{6,2},{7,3},{8,4},{9,5},{10,6},{11,7},{12,8},{13,9},{1... | collective-permute-start | bytes 2580488 | tf_op jit(solution)/shard_map/ppermute | solution.py:56
  175.2 88.1 %collective-permute-start.16 = (bf16[560,768]{1,0:T(8,128)(2,1)}, bf16[560,768]{1,0:T(8,128)(2,1)S(1)}, u32[]{:S(2)}, u32[]{:S(2)}) collective-permute-start(bf16[560,768]{1,0:T(8,128)(2,1)} %get-tuple-element.138.refs_0_), channel_id=1, source_target_pairs={{0,2},{1,3},{2,0},{3,1},{4,6},{5,7},{6,4},{7,5},{8,10},{9,11},{10,... | collective-permute-start | bytes 2580488 | tf_op jit(solution)/shard_map/ppermute | solution.py:56
  216.5 90.1 %collective-permute-start.20 = (bf16[560,768]{1,0:T(8,128)(2,1)}, bf16[560,768]{1,0:T(8,128)(2,1)S(1)}, u32[]{:S(2)}, u32[]{:S(2)}) collective-permute-start(bf16[560,768]{1,0:T(8,128)(2,1)} %get-tuple-element.138.refs_0_), channel_id=1, source_target_pairs={{0,1},{1,0},{2,3},{3,2},{4,5},{5,4},{6,7},{7,6},{8,9},{9,8},{10,11... | collective-permute-start | bytes 2580488 | tf_op jit(solution)/shard_map/ppermute | solution.py:56
  263.4 58.6 %collective-permute-start.17 = (bf16[560,768]{1,0:T(8,128)(2,1)S(1)}, bf16[560,768]{1,0:T(8,128)(2,1)S(1)}, u32[]{:S(2)}, u32[]{:S(2)}) collective-permute-start(bf16[560,768]{1,0:T(8,128)(2,1)S(1)} %broadcast_select_fusion), channel_id=1, source_target_pairs={{2,6},{3,7},{4,0},{5,1},{6,10},{7,11},{8,4},{9,5},{10,14},{11,15},... | collective-permute-start | bytes 2580488 | tf_op jit(solution)/shard_map/ppermute | solution.py:56
  264.7 87.9 %collective-permute-start.18 = (bf16[560,768]{1,0:T(8,128)(2,1)S(1)}, bf16[560,768]{1,0:T(8,128)(2,1)}, u32[]{:S(2)}, u32[]{:S(2)}) collective-permute-start(bf16[560,768]{1,0:T(8,128)(2,1)S(1)} %collective-permute-done.16.refs_1_), channel_id=1, source_target_pairs={{0,4},{1,5},{2,6},{3,7},{4,8},{5,9},{6,10},{7,11},{8,12},{9,13},{1... | collective-permute-start | bytes 2580488 | tf_op jit(solution)/shard_map/ppermute | solution.py:56
  305.0 47.7 %collective-permute-start.19 = (bf16[560,768]{1,0:T(8,128)(2,1)S(1)}, bf16[560,768]{1,0:T(8,128)(2,1)}, u32[]{:S(2)}, u32[]{:S(2)}) collective-permute-start(bf16[560,768]{1,0:T(8,128)(2,1)S(1)} %collective-permute-done.16.refs_1_), channel_id=1, source_target_pairs={{4,0},{5,1},{6,2},{7,3},{8,4},{9,5},{10,6},{11,7},{12,8},{13,9},{1... | collective-permute-start | bytes 2580488 | tf_op jit(solution)/shard_map/ppermute | solution.py:56
  306.2 46.4 %collective-permute-start.21 = (bf16[560,768]{1,0:T(8,128)(2,1)S(1)}, bf16[560,768]{1,0:T(8,128)(2,1)}, u32[]{:S(2)}, u32[]{:S(2)}) collective-permute-start(bf16[560,768]{1,0:T(8,128)(2,1)S(1)} %collective-permute-done.16.refs_1_), channel_id=1, source_target_pairs={{0,1},{1,0},{2,3},{3,2},{4,5},{5,4},{6,7},{7,6},{8,9},{9,8},{10,11... | collective-permute-start | bytes 2580488 | tf_op jit(solution)/shard_map/ppermute | solution.py:56
  306.7 46.0 %collective-permute-start.22 = (bf16[560,768]{1,0:T(8,128)(2,1)S(1)}, bf16[560,768]{1,0:T(8,128)(2,1)}, u32[]{:S(2)}, u32[]{:S(2)}) collective-permute-start(bf16[560,768]{1,0:T(8,128)(2,1)S(1)} %collective-permute-done.14.refs_2_), channel_id=1, source_target_pairs={{0,1},{1,0},{2,3},{3,2},{4,5},{5,4},{6,7},{7,6},{8,9},{9,8},{10,11... | collective-permute-start | bytes 2580488 | tf_op jit(solution)/shard_map/ppermute | solution.py:56
  322.1 30.6 %collective-permute-start.23 = (bf16[560,768]{1,0:T(8,128)(2,1)S(1)}, bf16[560,768]{1,0:T(8,128)(2,1)}, u32[]{:S(2)}, u32[]{:S(2)}) collective-permute-start(bf16[560,768]{1,0:T(8,128)(2,1)S(1)} %collective-permute-done.15.refs_3_), channel_id=1, source_target_pairs={{0,1},{1,0},{2,3},{3,2},{4,5},{5,4},{6,7},{7,6},{8,9},{9,8},{10,11... | collective-permute-start | bytes 2580488 | tf_op jit(solution)/shard_map/ppermute | solution.py:56
  352.7 420.6 %all-reduce.5.cloned.1.call-start = ((), (), s32[]{:S(2)}) async-start(), calls=%async_computation.2 | async-start | bytes 22855680 | tf_op jit(solution)/shard_map/psum | solution.py:898
  369.5 21.0 %collective-permute-start.24 = (bf16[560,768]{1,0:T(8,128)(2,1)S(1)}, bf16[560,768]{1,0:T(8,128)(2,1)S(1)}, u32[]{:S(2)}, u32[]{:S(2)}) collective-permute-start(bf16[560,768]{1,0:T(8,128)(2,1)S(1)} %copy-done.36), channel_id=1, source_target_pairs={{0,2},{1,3},{2,0},{3,1},{4,6},{5,7},{6,4},{7,5},{8,10},{9,11},{10,... | collective-permute-start | bytes 2580488 | tf_op jit(solution)/shard_map/ppermute | solution.py:56
  369.5 21.0 %collective-permute-start.25 = (bf16[560,768]{1,0:T(8,128)(2,1)}, bf16[560,768]{1,0:T(8,128)(2,1)S(1)}, u32[]{:S(2)}, u32[]{:S(2)}) collective-permute-start(bf16[560,768]{1,0:T(8,128)(2,1)} %collective-permute-done.18.refs_4_), channel_id=1, source_target_pairs={{0,1},{1,0},{2,3},{3,2},{4,5},{5,4},{6,7},{7,6},{8,9},{9,8},{10,11... | collective-permute-start | bytes 2580488 | tf_op jit(solution)/shard_map/ppermute | solution.py:56
  369.5 21.0 %collective-permute-start.26 = (bf16[560,768]{1,0:T(8,128)(2,1)}, bf16[560,768]{1,0:T(8,128)(2,1)S(1)}, u32[]{:S(2)}, u32[]{:S(2)}) collective-permute-start(bf16[560,768]{1,0:T(8,128)(2,1)} %collective-permute-done.19.refs_5_), channel_id=1, source_target_pairs={{0,1},{1,0},{2,3},{3,2},{4,5},{5,4},{6,7},{7,6},{8,9},{9,8},{10,11... | collective-permute-start | bytes 2580488 | tf_op jit(solution)/shard_map/ppermute | solution.py:56
  555.7 95.7 %collective-permute-start.31 = (bf16[384,768]{1,0:T(8,128)(2,1)}, bf16[384,768]{1,0:T(8,128)(2,1)S(1)}, u32[]{:S(2)}, u32[]{:S(2)}) collective-permute-start(bf16[384,768]{1,0:T(8,128)(2,1)} %get-tuple-element.252), channel_id=1, source_target_pairs={{0,18},{1,19},{2,16},{3,17},{4,22},{5,23},{6,20},{7,21},{8,26},{9,... | collective-permute-start | bytes 1769480 | tf_op jit(solution)/shard_map/ppermute | solution.py:766
  635.1 30.6 %collective-permute-start.30 = (bf16[384,768]{1,0:T(8,128)(2,1)}, bf16[384,768]{1,0:T(8,128)(2,1)}, u32[]{:S(2)}, u32[]{:S(2)}) collective-permute-start(bf16[384,768]{1,0:T(8,128)(2,1)} %get-tuple-element.253), channel_id=1, source_target_pairs={{0,16},{1,17},{2,18},{3,19},{4,20},{5,21},{6,22},{7,23},{8,24},{9,... | collective-permute-start | bytes 1769480 | tf_op jit(solution)/shard_map/ppermute | solution.py:766
  636.1 29.7 %collective-permute-start.29 = (bf16[384,768]{1,0:T(8,128)(2,1)S(1)}, bf16[384,768]{1,0:T(8,128)(2,1)}, u32[]{:S(2)}, u32[]{:S(2)}) collective-permute-start(bf16[384,768]{1,0:T(8,128)(2,1)S(1)} %get-tuple-element.251), channel_id=1, source_target_pairs={{0,2},{1,3},{2,0},{3,1},{4,6},{5,7},{6,4},{7,5},{8,10},{9,11},{10,... | collective-permute-start | bytes 1769480 | tf_op jit(solution)/shard_map/ppermute | solution.py:766
  667.4 20.1 %collective-permute-start.34 = (bf16[96,768]{1,0:T(8,128)(2,1)S(1)}, bf16[96,768]{1,0:T(8,128)(2,1)S(1)}, u32[]{:S(2)}, u32[]{:S(2)}) collective-permute-start(bf16[96,768]{1,0:T(8,128)(2,1)S(1)} %get-tuple-element.259), channel_id=1, source_target_pairs={{0,12},{1,13},{2,14},{3,15},{4,8},{5,9},{6,10},{7,11},{8,4},{9,5},... | collective-permute-start | bytes 442376 | tf_op jit(solution)/shard_map/ppermute | solution.py:766
  667.5 32.5 %collective-permute-start.33 = (bf16[96,768]{1,0:T(8,128)(2,1)S(1)}, bf16[96,768]{1,0:T(8,128)(2,1)S(1)}, u32[]{:S(2)}, u32[]{:S(2)}) collective-permute-start(bf16[96,768]{1,0:T(8,128)(2,1)S(1)} %get-tuple-element.260), channel_id=1, source_target_pairs={{0,8},{1,9},{2,10},{3,11},{4,12},{5,13},{6,14},{7,15},{8,0},{9,1},... | collective-permute-start | bytes 442376 | tf_op jit(solution)/shard_map/ppermute | solution.py:766
  786.9 16.2 %collective-permute-start.38 = (bf16[384,768]{1,0:T(8,128)(2,1)S(1)}, bf16[384,768]{1,0:T(8,128)(2,1)S(1)}, u32[]{:S(2)}, u32[]{:S(2)}) collective-permute-start(bf16[384,768]{1,0:T(8,128)(2,1)S(1)} %constant_dynamic-update-slice_fusion.6), channel_id=1, source_target_pairs={{0,2},{1,3},{2,0},{3,1},{4,6},{5,7},{6,4},{7,5},{8,10},{9,11},{10,... | collective-permute-start | bytes 1769480 | tf_op jit(solution)/shard_map/ppermute | solution.py:766
  787.9 27.5 %collective-permute-start.39 = (bf16[384,768]{1,0:T(8,128)(2,1)S(1)}, bf16[384,768]{1,0:T(8,128)(2,1)S(1)}, u32[]{:S(2)}, u32[]{:S(2)}) collective-permute-start(bf16[384,768]{1,0:T(8,128)(2,1)S(1)} %constant_dynamic-update-slice_fusion.6), channel_id=1, source_target_pairs={{0,16},{1,17},{2,18},{3,19},{4,20},{5,21},{6,22},{7,23},{8,24},{9,... | collective-permute-start | bytes 1769480 | tf_op jit(solution)/shard_map/ppermute | solution.py:766
  790.4 25.0 %collective-permute-start.40 = (bf16[384,768]{1,0:T(8,128)(2,1)S(1)}, bf16[384,768]{1,0:T(8,128)(2,1)S(1)}, u32[]{:S(2)}, u32[]{:S(2)}) collective-permute-start(bf16[384,768]{1,0:T(8,128)(2,1)S(1)} %constant_dynamic-update-slice_fusion.6), channel_id=1, source_target_pairs={{0,18},{1,19},{2,16},{3,17},{4,22},{5,23},{6,20},{7,21},{8,26},{9,... | collective-permute-start | bytes 1769480 | tf_op jit(solution)/shard_map/ppermute | solution.py:766
  (76 other events, 1676.2 us)
Sparse Core Ops, SparseCore 0:
  80.0 100.9 all-gather.4
  352.8 110.0 all-gather.6
  470.0 303.2 all-reduce.4

commit v5 on v3

--- a/solution.py
+++ b/solution.py
@@ -229,20 +229,20 @@
     qown[SEG:OWN, :] = qc[0:MEMP, :]
     near = longest(qown[...].astype(F32)) * key_top <= SHIFT_FREE**2
 
-    def head(index, carry):
-        cols = pl.ds(pl.multiple_of((index // 2) * PAIR, PAIR), PAIR)
-        half = index % 2
+    def pair(index, carry):
+        cols = pl.ds(pl.multiple_of(index * PAIR, PAIR), PAIR)
         lane = lax.broadcasted_iota(jnp.int32, (OWN, PAIR), 1)
-        mine = (lane // HD) == half
-        query = qown[:, cols]
-        query = jnp.where(mine, query, jnp.zeros_like(query))
+        halves = (0, 1)
+        mine = [(lane // HD) == half for half in halves]
+        numbers = [lane == quad * 4 + index * 2 + half for half in halves]
+        both = qown[:, cols]
+        queries = [jnp.where(mine[half], both, jnp.zeros_like(both)) for half in halves]
         acc[...] = jnp.zeros_like(acc)
-        number = lane == quad * 4 + index
-
-        def score(span):
-            return lax.dot_general(query, kc[span, cols], LAST, preferred_element_type=F32)
-
-        def gather(span, terms):
+
+        def score(half, span):
+            return lax.dot_general(queries[half], kc[span, cols], LAST, preferred_element_type=F32)
+
+        def gather(half, span, terms):
             values = extended[half, span, cols]
             return jnp.dot(terms.astype(BF16), values, preferred_element_type=F32)
 
@@ -250,32 +250,38 @@
         def _():
             def run(first, count):
                 span = span_of(first, count)
-                acc[...] += gather(span, jnp.exp(score(span)))
+                for half in halves:
+                    acc[half] += gather(half, span, jnp.exp(score(half, span)))
 
             by_chunks(blocks, run)
-            lse[...] = jnp.where(number, 0.0, lse[...])
 
         @pl.when(jnp.logical_not(near))
         def _():
-            def run(block, top):
-                span = span_of(block, 1)
-                column = block * SEG + lax.broadcasted_iota(jnp.int32, (OWN, SEG), 1)
-                dead = (column >= meta[M_ROWS]) | ((column >= meta[M_MEM]) & (column < MEMP))
-                scores = jnp.where(dead, NEG, score(span))
-                new = jnp.maximum(top, jnp.max(scores, axis=1, keepdims=True))
-                acc[...] = acc[...] * jnp.exp(top - new) + gather(span, jnp.exp(scores - new))
-                return new
-
-            top = lax.fori_loop(0, blocks, run, jnp.full((OWN, 1), NEG, F32))
-            lse[...] = jnp.where(number, top, lse[...])
-
-        sums = acc[...]
-        total = jnp.where(mine, pltpu.roll(sums, HD, 1), sums)
-        out[:, cols] = jnp.where(mine, sums * (1.0 / total), out[:, cols])
-        lse[...] += jnp.where(number, jnp.log(total), 0.0)
+            for half in halves:
+                def run(block, top):
+                    span = span_of(block, 1)
+                    column = block * SEG + lax.broadcasted_iota(jnp.int32, (OWN, SEG), 1)
+                    dead = (column >= meta[M_ROWS]) | ((column >= meta[M_MEM]) & (column < MEMP))
+                    scores = jnp.where(dead, NEG, score(half, span))
+                    new = jnp.maximum(top, jnp.max(scores, axis=1, keepdims=True))
+                    terms = gather(half, span, jnp.exp(scores - new))
+                    acc[half] = acc[half] * jnp.exp(top - new) + terms
+                    return new
+
+                top = lax.fori_loop(0, blocks, run, jnp.full((OWN, 1), NEG, F32))
+                lse[...] = jnp.where(numbers[half], top, lse[...])
+
+        sums = [acc[half] for half in halves]
+        value = jnp.where(mine[0], sums[0], sums[1])
+        total = pltpu.roll(jnp.where(mine[0], sums[1], sums[0]), HD, 1)
+        out[:, cols] = value * (1.0 / total)
+        turned_total = pltpu.roll(total, HD, 1)
+        for half in halves:
+            spread = jnp.where(mine[half], total, turned_total)
+            lse[...] += jnp.where(numbers[half], jnp.log(spread), 0.0)
         return carry
 
-    lax.fori_loop(0, 4, head, 0)
+    lax.fori_loop(0, 2, pair, 0)
 
 
 def attend_forward(meta, pieces, mem, weights):
@@ -297,7 +303,7 @@
                 pltpu.VMEM((CAP, width), BF16),
                 pltpu.VMEM((OWN, QUAD), BF16),
                 pltpu.VMEM((2, CAP, QUAD), BF16),
-                pltpu.VMEM((OWN, PAIR), F32),
+                pltpu.VMEM((2, OWN, PAIR), F32),
                 pltpu.SemaphoreType.DMA((LONG,)),
             ],
         ),
@@ -771,11 +777,14 @@
         got = [swap(part(k), mask) for k, mask in enumerate(masks) if k]
         value = sum((g.astype(F32) for g in got), part(0).astype(F32)).astype(BF16)
     for index, group in enumerate(reversed(groups)):
-        if index == 1:
-            value, beside = lax.optimization_barrier((value, beside))
         masks, own = masks_of(group), own_of(group)
         size = value.shape[0]
+        if index == len(groups) - 2:
+            value, beside = lax.optimization_barrier((value, beside))
         got = [value] + [swap(value, mask) for mask in masks[1:]]
+        if index == len(groups) - 2:
+            beside = [part.astype(F32) for part in beside]
+            got[-1], beside = lax.optimization_barrier((got[-1], beside))
         value = jnp.zeros((size * len(masks), value.shape[1]), BF16)
         for k, part in enumerate(got):
             value = lax.dynamic_update_slice_in_dim(value, part, (own ^ k) * size, 0)
@@ -880,8 +889,9 @@
         rows = rows.reshape(groups, batches, chains, MEMP, width)
         return lax.dynamic_index_in_dim(rows, group, keepdims=False)[:, :, :mem_rows]
 
-    wide_early = [part.astype(F32) for part in (grad_inner, grad_outer, grad_output)]
-    late, (grad_inner, grad_outer, grad_output) = sum_everywhere(late, wide_early)
+    late, (grad_inner, grad_outer, grad_output) = sum_everywhere(
+        late, [grad_inner, grad_outer, grad_output]
+    )
     grad_query, grad_key, grad_value = (late[i * width : (i + 1) * width] for i in range(3))
     biases = late[3 * width : 3 * width + 2].astype(F32)
     count = groups * batches * chains * MEMP

time: 789 us -> 770 us (0.976); the launches traced: 802 us -> 759 us
  starting transfers between devices: 132 us -> 64.7 us
  waiting for transfers between devices: 217 us -> 268 us
  Pallas kernels: 358 us -> 331 us
    all_gather x3, waiting for transfers between devices: 21 us -> 98.1 us  [gather_all(): return [lax.all_gather(value, 'blk')]]
    ppermute x14, starting transfers between devices: 116 us -> 48.4 us  [swap(): lax.ppermute(value, ('dp', 'blk'), [(i, i ^ mask) for i in range(sizes)])]
    ppermute x14, waiting for transfers between devices: 87.8 us -> 69.3 us  [swap(): lax.ppermute(value, ('dp', 'blk'), [(i, i ^ mask) for i in range(sizes)])]
    pallas_call x2, Pallas kernels: 121 us -> 105 us  [attend_forward(): pl.pallas_call(forward_body, grid_spec=pltpu.PrefetchScalarGridSpec(num_s...]
    pallas_call x2, Pallas kernels: 160 us -> 149 us  [attend_backward(): pl.pallas_call(functools.partial(backward_body, start, count), grid_spec=...]
    psum x1, waiting for transfers between devices: 56.9 us -> 48.9 us  [local(): early = lax.psum(early, ('dp', 'blk'))]
  transfers between devices with their start and end apart: 32 -> 32, of which waited for: 20 -> 21; matrix products, arithmetic and copies ran while one was open for 7% -> 9% of each run, Pallas kernels for 45% -> 44%
where the time goes in v5:
time: 770 us; the launch traced here: 759 us
  Pallas kernels  331 us (43%)
  waiting for transfers between devices  268 us (35%)
  starting transfers between devices  64.7 us (8%)
  other arithmetic  29.8 us (4%)
  local copies, waits for them, and re-layouts  25.7 us (3%)
  matrix products  25.5 us (3%)
  between operations  15 us (2%)
    pallas_call x2, Pallas kernels, attend_backward(): pl.pallas_call(functools.partial(backward_body, start, count), grid_spec=...  149 us
    pallas_call x2, Pallas kernels, attend_forward(): pl.pallas_call(forward_body, grid_spec=pltpu.PrefetchScalarGridSpec(num_s...  105 us
    all_gather x3, waiting for transfers between devices, gather_all(): return [lax.all_gather(value, 'blk')]  98.1 us
    ppermute x14, waiting for transfers between devices, swap(): lax.ppermute(value, ('dp', 'blk'), [(i, i ^ mask) for i in range(sizes)])  69.3 us
    pallas_call x2, Pallas kernels, middle(): pl.pallas_call(middle_body, in_specs=[pl.BlockSpec(memory_space=pltpu.SME...  59.6 us
    ppermute x14, waiting for transfers between devices, move(): return lax.ppermute(value, 'blk', pairs)  51.2 us
    psum x1, waiting for transfers between devices, local(): early = lax.psum(early, ('dp', 'blk'))  48.9 us
    ppermute x14, starting transfers between devices, swap(): lax.ppermute(value, ('dp', 'blk'), [(i, i ^ mask) for i in range(sizes)])  48.4 us
  transfers between devices with their start and end apart: 32, of which 21 were waited for; matrix products, arithmetic and copies ran while one was open for 9% of the time, Pallas kernels for 44%

profile of v5, /device:TPU:0, one launch (start us, length us, event | category | flops | bytes accessed | tf_op | source)
XLA Modules:
  0.0 758.9 jit_solution(13154385267739590560)
XLA Ops:
  9.7 5.1 collective-permute-start.1
  17.7 13.9 %collective-permute-done.1.refs_2_ = bf16[512,768]{1,0:T(8,128)(2,1)S(1)} collective-permute-done((bf16[512,768]{1,0:T(8,128)(2,1)S(1)}, bf16[512,768]{1,0:T(8,128)(2,1)S(1)}, u32[]{:S(2)}, u32[]{:S(2)}) %collective-permute-start.1) | collective-permute-done | bytes 786464 | tf_op jit(solution)/shard_map/ppermute | solution.py:56
  31.6 4.3 collective-permute-done.2.refs_3_
  38.5 4.6 collective-permute-start.3
  44.6 14.8 %collective-permute-done.5 = bf16[512,768]{1,0:T(8,128)(2,1)S(1)} collective-permute-done((bf16[512,768]{1,0:T(8,128)(2,1)S(1)}, bf16[512,768]{1,0:T(8,128)(2,1)S(1)}, u32[]{:S(2)}, u32[]{:S(2)}) %collective-permute-start.5) | collective-permute-done | bytes 786464 | tf_op jit(solution)/shard_map/ppermute | solution.py:56
  60.8 13.1 %collective-permute-done.4.refs_5_ = bf16[512,768]{1,0:T(8,128)(2,1)S(1)} collective-permute-done((bf16[512,768]{1,0:T(8,128)(2,1)}, bf16[512,768]{1,0:T(8,128)(2,1)S(1)}, u32[]{:S(2)}, u32[]{:S(2)}) %collective-permute-start.4) | collective-permute-done | bytes 786464 | tf_op jit(solution)/shard_map/ppermute | solution.py:56
  90.7 23.9 %attend_forward.2 = (f32[544,768]{1,0:T(8,128)}, f32[544,128]{1,0:T(8,128)}, bf16[4096,768]{1,0:T(8,128)(2,1)}, bf16[4096,768]{1,0:T(8,128)(2,1)}, bf16[4096,768]{1,0:T(8,128)(2,1)}) custom-call(s32[16]{0:T(128)} %get-tuple-element.147.meta, bf16[512,768]{1,0:T(8,128)(2,1)} %copy-done.17, bf16[512,768]{1,0:T(8,128)(2,1)} %collective-permute-done.refs_1_, ...), custom_call_target="tpu_custom_call" | custom-call | flops 40000000000 | bytes 30000000 | tf_op jit(solution)/shard_map/attend_forward/pallas_call | solution.py:292
  114.6 29.8 %middle.2 = (bf16[512,768]{1,0:T(8,128)(2,1)}, bf16[32,768]{1,0:T(8,128)(2,1)}, bf16[560,768]{1,0:T(8,128)(2,1)}, bf16[32,768]{1,0:T(8,128)(2,1)}, f32[24,128]{1...) custom-call(s32[16]{0:T(128)} %get-tuple-element.147.meta, ...), custom_call_target="tpu_custom_call" | custom-call | flops 12000000000 | bytes 40000000 | tf_op jit(solution)/shard_map/middle/pallas_call | solution.py:639
  144.4 36.0 %all-gather.7.cloned.1.call-done = bf16[8192,768]{1,0:T(8,128)(2,1)} async-done(((bf16[512,768]{1,0:T(8,128)(2,1)}), bf16[8192,768]{1,0:T(8,128)(2,1)}) %all-gather.7.cloned.1.call-update) | async-done | bytes 12582928 | tf_op jit(solution)/shard_map/all_gather | solution.py:69
  180.5 81.4 %attend_forward.3 = (f32[544,768]{1,0:T(8,128)}, f32[544,128]{1,0:T(8,128)}, bf16[4096,768]{1,0:T(8,128)(2,1)}, bf16[4096,768]{1,0:T(8,128)(2,1)}, bf16[4096,768]{1,0:T(8,128)(2,1)}) custom-call(s32[16]{0:T(128)} %get-tuple-element.169.meta, bf16[16,512,768]{2,1,0:T(8,128)(2,1)} %bitcast.63, bf16[4,32,768]{2,1,0:T(8,128)(2,1)} %get-tuple-element.241.refs_1_.memory, ...), custom_call_target="tpu_custom_call" | custom-call | flops 40000000000 | bytes 30000000 | tf_op jit(solution)/shard_map/attend_forward/pallas_call | solution.py:292
  262.0 29.8 %middle.3 = (bf16[512,768]{1,0:T(8,128)(2,1)}, bf16[32,768]{1,0:T(8,128)(2,1)}, bf16[560,768]{1,0:T(8,128)(2,1)}, bf16[32,768]{1,0:T(8,128)(2,1)}, f32[24,128]{1...) custom-call(s32[16]{0:T(128)} %get-tuple-element.169.meta, ...), custom_call_target="tpu_custom_call" | custom-call | flops 12000000000 | bytes 40000000 | tf_op jit(solution)/shard_map/middle/pallas_call | solution.py:639
  300.2 8.0 %fusion.11 = bf16[768,3072]{1,0:T(8,128)(2,1)} fusion(bf16[544,3072]{1,0:T(8,128)(2,1)S(1)} %copy-done.43, bf16[544,3072]{1,0:T(8,128)(2,1)S(1)} %copy-done.42, bf16[544,768]{1,0:T(8,128)(2,1)S(1)} %copy-done.49, bf16[544,768]{1,0:T(8,128)(2,1)S(1)} %copy-done.48), kind=kOutput, calls=%fused_computation.9 | convolution fusion | flops 5152899072 | bytes 13074432 | tf_op jit(solution)/shard_map/dot_general | solution.py:753
  308.2 8.2 %fusion.8 = bf16[3072,768]{1,0:T(8,128)(2,1)} fusion(bf16[544,3072]{1,0:T(8,128)(2,1)S(1)} %copy-done.51, bf16[544,3072]{1,0:T(8,128)(2,1)S(1)} %copy-done.50, bf16[544,768]{1,0:T(8,128)(2,1)S(1)} %copy-done.53, bf16[544,768]{1,0:T(8,128)(2,1)S(1)} %copy-done.52), kind=kOutput, calls=%fused_computation.8 | convolution fusion | flops 5152899072 | bytes 13074432 | tf_op jit(solution)/shard_map/dot_general | solution.py:753
  316.4 42.0 %attend_backward.2 = (bf16[544,768]{1,0:T(8,128)(2,1)}, bf16[544,768]{1,0:T(8,128)(2,1)}, bf16[544,768]{1,0:T(8,128)(2,1)}) custom-call(s32[16]{0:T(128)} %get-tuple-element.147.meta, bf16[16,560,768]{2,1,0:T(8,128)(2,1)} %bitcast.61, bf16[4096,768]{1,0:T(8,128)(2,1)} %get-tuple-element.149.refs_1_, bf16[4096,768]{1,0:T(8,128)(2,1)} %get-tuple-element.150.refs_2_, ...), custom_call_target="tpu_custom_call" | custom-call | flops 10000000000 | bytes 1000000 | tf_op jit(solution)/shard_map/attend_backward/pallas_call | solution.py:433
  358.4 62.0 %all-gather.11.cloned.1.call-done = bf16[8960,768]{1,0:T(8,128)(2,1)} async-done(((bf16[560,768]{1,0:T(8,128)(2,1)}), bf16[8960,768]{1,0:T(8,128)(2,1)}) %all-gather.11.cloned.1.call-update) | async-done | bytes 13762576 | tf_op jit(solution)/shard_map/all_gather | solution.py:69
  420.4 107.3 %attend_backward.3 = (bf16[544,768]{1,0:T(8,128)(2,1)}, bf16[544,768]{1,0:T(8,128)(2,1)}, bf16[544,768]{1,0:T(8,128)(2,1)}) custom-call(s32[16]{0:T(128)} %get-tuple-element.169.meta, bf16[16,560,768]{2,1,0:T(8,128)(2,1)} %bitcast.62, bf16[4096,768]{1,0:T(8,128)(2,1)} %get-tuple-element.171.refs_1_, bf16[4096,768]{1,0:T(8,128)(2,1)} %get-tuple-element.172.refs_2_, ...), custom_call_target="tpu_custom_call" | custom-call | flops 10000000000 | bytes 1000000 | tf_op jit(solution)/shard_map/attend_backward/pallas_call | solution.py:433
  527.7 14.9 %late_sums.1 = bf16[3072,768]{1,0:T(8,128)(2,1)} custom-call(s32[2,16]{1,0:T(2,128)} %find_chain.1.metas, s32[1]{0:T(128)} %bitcast.25.group, bf16[544,768]{1,0:T(8,128)(2,1)} %get-tuple-element.180.refs_0_, bf16[544,768]{1,0:T(8,128)(2,1)} %get-tuple-element.181.refs_1_, f32[544,768]{1,0:T(8,128)} %get-tuple-element.164.refs_2_, ...), custom_call_target="tpu_custom_call" | custom-call | tf_op jit(solution)/shard_map/late_sums/pallas_call | solution.py:741
  544.7 4.5 collective-permute-done.14
  549.2 3.0 add_convert_fusion
  556.8 12.9 %collective-permute-done.15 = bf16[384,768]{1,0:T(8,128)(2,1)S(1)} collective-permute-done((bf16[384,768]{1,0:T(8,128)(2,1)}, bf16[384,768]{1,0:T(8,128)(2,1)S(1)}, u32[]{:S(2)}, u32[]{:S(2)}) %collective-permute-start.15) | collective-permute-done | bytes 589856 | tf_op jit(solution)/shard_map/ppermute | solution.py:758
  569.7 16.3 %collective-permute-done.16 = bf16[384,768]{1,0:T(8,128)(2,1)} collective-permute-done((bf16[384,768]{1,0:T(8,128)(2,1)}, bf16[384,768]{1,0:T(8,128)(2,1)}, u32[]{:S(2)}, u32[]{:S(2)}) %collective-permute-start.16) | collective-permute-done | bytes 589856 | tf_op jit(solution)/shard_map/ppermute | solution.py:758
  587.5 32.5 %collective-permute-start.18 = (bf16[96,768]{1,0:T(8,128)(2,1)S(1)}, bf16[96,768]{1,0:T(8,128)(2,1)S(1)}, u32[]{:S(2)}, u32[]{:S(2)}) collective-permute-start(bf16[96,768]{1,0:T(8,128)(2,1)S(1)} %get-tuple-element.236), channel_id=1, source_target_pairs={{0,4},{1,5},{2,6},{3,7},{4,0},{5,1},{6,2},{7,3},{8,12},{9,13},{10,... | collective-permute-start | bytes 442376 | tf_op jit(solution)/shard_map/ppermute | solution.py:758
  624.2 7.9 %collective-permute-done.19 = bf16[96,768]{1,0:T(8,128)(2,1)S(1)} collective-permute-done((bf16[96,768]{1,0:T(8,128)(2,1)S(1)}, bf16[96,768]{1,0:T(8,128)(2,1)S(1)}, u32[]{:S(2)}, u32[]{:S(2)}) %collective-permute-start.19) | collective-permute-done | bytes 147488 | tf_op jit(solution)/shard_map/ppermute | solution.py:758
  632.2 3.7 collective-permute-start.21
  641.1 4.7 collective-permute-done.21
  645.8 3.9 collective-permute-done.22
  649.7 7.2 collective-permute-done.23
  656.9 48.9 %all-reduce.5.cloned.1.call-done = (bf16[524,768]{1,0:T(8,128)(2,1)}, bf16[768,3072]{1,0:T(8,128)(2,1)}, bf16[3072,768]{1,0:T(8,128)(2,1)}, bf16[768,768]{1,0:T(8,128)(2,1)}) async-done(((bf16[524,768]{1,0:T(8,128)(2,1)}, bf16[768,3072]{1,0:T(8,128)(2,1)}, bf16[3072,768]{1,0:T(8,128)(2,1)}, bf16[768,768]{1,0:T(8,128)(2,1)}), (bf16[524,768]{1,0:T(8,128)(2,1)}, bf16[768,3072]{1,0:T(8,128)(2,1)}, ...) | async-done | bytes 11421712 | tf_op jit(solution)/shard_map/psum | solution.py:879
  712.2 5.0 convert_element_type.148
  717.3 4.5 convert_element_type.149
  723.6 10.2 %collective-permute-done.24 = bf16[384,768]{1,0:T(8,128)(2,1)S(1)} collective-permute-done((bf16[384,768]{1,0:T(8,128)(2,1)S(1)}, bf16[384,768]{1,0:T(8,128)(2,1)S(1)}, u32[]{:S(2)}, u32[]{:S(2)}) %collective-permute-start.24) | collective-permute-done | bytes 589856 | tf_op jit(solution)/shard_map/ppermute | solution.py:758
  747.0 3.1 slice_convert_fusion
  (231 shorter events, 76.5 us)
Async XLA Ops:
  7.2 173.3 %all-gather.7.cloned.1.call-start = ((), (), s32[]{:S(2)}) async-start(), calls=%async_computation | async-start | bytes 13369344 | tf_op jit(solution)/shard_map/all_gather | solution.py:69
  9.7 21.8 %collective-permute-start.1 = (bf16[512,768]{1,0:T(8,128)(2,1)S(1)}, bf16[512,768]{1,0:T(8,128)(2,1)S(1)}, u32[]{:S(2)}, u32[]{:S(2)}) collective-permute-start(bf16[512,768]{1,0:T(8,128)(2,1)S(1)} %get-tuple-element.106.refs_0_.tokens), channel_id=1, source_target_pairs={{0,4},{1,5},{2,6},{3,7},{4,8},{5,9},{6,10},{7,11},{8,12},{9,13},{1... | collective-permute-start | bytes 2359304 | tf_op jit(solution)/shard_map/ppermute | solution.py:56
  14.8 21.0 %collective-permute-start.2 = (bf16[512,768]{1,0:T(8,128)(2,1)S(1)}, bf16[512,768]{1,0:T(8,128)(2,1)}, u32[]{:S(2)}, u32[]{:S(2)}) collective-permute-start(bf16[512,768]{1,0:T(8,128)(2,1)S(1)} %get-tuple-element.106.refs_0_.tokens), channel_id=1, source_target_pairs={{4,0},{5,1},{6,2},{7,3},{8,4},{9,5},{10,6},{11,7},{12,8},{13,9},{1... | collective-permute-start | bytes 2359304 | tf_op jit(solution)/shard_map/ppermute | solution.py:56
  16.1 22.3 %collective-permute-start = (bf16[512,768]{1,0:T(8,128)(2,1)S(1)}, bf16[512,768]{1,0:T(8,128)(2,1)}, u32[]{:S(2)}, u32[]{:S(2)}) collective-permute-start(bf16[512,768]{1,0:T(8,128)(2,1)S(1)} %get-tuple-element.106.refs_0_.tokens), channel_id=1, source_target_pairs={{0,2},{1,3},{2,0},{3,1},{4,6},{5,7},{6,4},{7,5},{8,10},{9,11},{10,... | collective-permute-start | bytes 2359304 | tf_op jit(solution)/shard_map/ppermute | solution.py:56
  37.1 22.4 %collective-permute-start.5 = (bf16[512,768]{1,0:T(8,128)(2,1)S(1)}, bf16[512,768]{1,0:T(8,128)(2,1)S(1)}, u32[]{:S(2)}, u32[]{:S(2)}) collective-permute-start(bf16[512,768]{1,0:T(8,128)(2,1)S(1)} %broadcast_select_fusion), channel_id=1, source_target_pairs={{2,6},{3,7},{4,0},{5,1},{6,10},{7,11},{8,4},{9,5},{10,14},{11,15},... | collective-permute-start | bytes 2359304 | tf_op jit(solution)/shard_map/ppermute | solution.py:56
  38.4 21.1 %collective-permute-start.7 = (bf16[512,768]{1,0:T(8,128)(2,1)S(1)}, bf16[512,768]{1,0:T(8,128)(2,1)S(1)}, u32[]{:S(2)}, u32[]{:S(2)}) collective-permute-start(bf16[512,768]{1,0:T(8,128)(2,1)S(1)} %get-tuple-element.106.refs_0_.tokens), channel_id=1, source_target_pairs={{0,1},{1,0},{2,3},{3,2},{4,5},{5,4},{6,7},{7,6},{8,9},{9,8},{10,11... | collective-permute-start | bytes 2359304 | tf_op jit(solution)/shard_map/ppermute | solution.py:56
  38.5 22.3 %collective-permute-start.3 = (bf16[512,768]{1,0:T(8,128)(2,1)}, bf16[512,768]{1,0:T(8,128)(2,1)S(1)}, u32[]{:S(2)}, u32[]{:S(2)}) collective-permute-start(bf16[512,768]{1,0:T(8,128)(2,1)} %collective-permute-done.refs_1_), channel_id=1, source_target_pairs={{0,4},{1,5},{2,6},{3,7},{4,8},{5,9},{6,10},{7,11},{8,12},{9,13},{1... | collective-permute-start | bytes 2359304 | tf_op jit(solution)/shard_map/ppermute | solution.py:56
  43.1 30.8 %collective-permute-start.4 = (bf16[512,768]{1,0:T(8,128)(2,1)}, bf16[512,768]{1,0:T(8,128)(2,1)S(1)}, u32[]{:S(2)}, u32[]{:S(2)}) collective-permute-start(bf16[512,768]{1,0:T(8,128)(2,1)} %collective-permute-done.refs_1_), channel_id=1, source_target_pairs={{4,0},{5,1},{6,2},{7,3},{8,4},{9,5},{10,6},{11,7},{12,8},{13,9},{1... | collective-permute-start | bytes 2359304 | tf_op jit(solution)/shard_map/ppermute | solution.py:56
  44.4 29.6 %collective-permute-start.8 = (bf16[512,768]{1,0:T(8,128)(2,1)}, bf16[512,768]{1,0:T(8,128)(2,1)S(1)}, u32[]{:S(2)}, u32[]{:S(2)}) collective-permute-start(bf16[512,768]{1,0:T(8,128)(2,1)} %collective-permute-done.refs_1_), channel_id=1, source_target_pairs={{0,1},{1,0},{2,3},{3,2},{4,5},{5,4},{6,7},{7,6},{8,9},{9,8},{10,11... | collective-permute-start | bytes 2359304 | tf_op jit(solution)/shard_map/ppermute | solution.py:56
  59.4 15.0 %collective-permute-start.6 = (bf16[512,768]{1,0:T(8,128)(2,1)S(1)}, bf16[512,768]{1,0:T(8,128)(2,1)S(1)}, u32[]{:S(2)}, u32[]{:S(2)}) collective-permute-start(bf16[512,768]{1,0:T(8,128)(2,1)S(1)} %collective-permute-done.5), channel_id=1, source_target_pairs={{0,2},{1,3},{2,0},{3,1},{4,6},{5,7},{6,4},{7,5},{8,10},{9,11},{10,... | collective-permute-start | bytes 2359304 | tf_op jit(solution)/shard_map/ppermute | solution.py:56
  59.5 15.1 %collective-permute-start.10 = (bf16[512,768]{1,0:T(8,128)(2,1)}, bf16[512,768]{1,0:T(8,128)(2,1)S(1)}, u32[]{:S(2)}, u32[]{:S(2)}) collective-permute-start(bf16[512,768]{1,0:T(8,128)(2,1)} %collective-permute-done.2.refs_3_), channel_id=1, source_target_pairs={{0,1},{1,0},{2,3},{3,2},{4,5},{5,4},{6,7},{7,6},{8,9},{9,8},{10,11... | collective-permute-start | bytes 2359304 | tf_op jit(solution)/shard_map/ppermute | solution.py:56
  60.8 13.8 %collective-permute-start.9 = (bf16[512,768]{1,0:T(8,128)(2,1)S(1)}, bf16[512,768]{1,0:T(8,128)(2,1)S(1)}, u32[]{:S(2)}, u32[]{:S(2)}) collective-permute-start(bf16[512,768]{1,0:T(8,128)(2,1)S(1)} %collective-permute-done.1.refs_2_), channel_id=1, source_target_pairs={{0,1},{1,0},{2,3},{3,2},{4,5},{5,4},{6,7},{7,6},{8,9},{9,8},{10,11... | collective-permute-start | bytes 2359304 | tf_op jit(solution)/shard_map/ppermute | solution.py:56
  73.9 2.3 collective-permute-start.11
  73.9 3.4 collective-permute-start.12
  74.4 4.0 collective-permute-start.13
  79.4 237.0 %all-gather.9.cloned.1.call-start = ((), (), s32[]{:S(2)}) async-start(), calls=%async_computation.1 | async-start | bytes 14622720 | tf_op jit(solution)/shard_map/all_gather | solution.py:69
  144.4 276.0 %all-gather.11.cloned.1.call-start = ((), (), s32[]{:S(2)}) async-start(), calls=%async_computation.2 | async-start | bytes 14622720 | tf_op jit(solution)/shard_map/all_gather | solution.py:69
  291.9 413.9 %all-reduce.5.cloned.1.call-start = ((), (), s32[]{:S(2)}) async-start(), calls=%async_computation.3 | async-start | bytes 22855680 | tf_op jit(solution)/shard_map/psum | solution.py:879
  544.4 4.7 collective-permute-start.14
  553.3 16.4 %collective-permute-start.15 = (bf16[384,768]{1,0:T(8,128)(2,1)}, bf16[384,768]{1,0:T(8,128)(2,1)S(1)}, u32[]{:S(2)}, u32[]{:S(2)}) collective-permute-start(bf16[384,768]{1,0:T(8,128)(2,1)} %get-tuple-element.229), channel_id=1, source_target_pairs={{0,2},{1,3},{2,0},{3,1},{4,6},{5,7},{6,4},{7,5},{8,10},{9,11},{10,... | collective-permute-start | bytes 1769480 | tf_op jit(solution)/shard_map/ppermute | solution.py:758
  553.9 32.0 %collective-permute-start.16 = (bf16[384,768]{1,0:T(8,128)(2,1)}, bf16[384,768]{1,0:T(8,128)(2,1)}, u32[]{:S(2)}, u32[]{:S(2)}) collective-permute-start(bf16[384,768]{1,0:T(8,128)(2,1)} %get-tuple-element.231), channel_id=1, source_target_pairs={{0,16},{1,17},{2,18},{3,19},{4,20},{5,21},{6,22},{7,23},{8,24},{9,... | collective-permute-start | bytes 1769480 | tf_op jit(solution)/shard_map/ppermute | solution.py:758
  553.9 32.0 %collective-permute-start.17 = (bf16[384,768]{1,0:T(8,128)(2,1)S(1)}, bf16[384,768]{1,0:T(8,128)(2,1)}, u32[]{:S(2)}, u32[]{:S(2)}) collective-permute-start(bf16[384,768]{1,0:T(8,128)(2,1)S(1)} %get-tuple-element.230), channel_id=1, source_target_pairs={{0,18},{1,19},{2,16},{3,17},{4,22},{5,23},{6,20},{7,21},{8,26},{9,... | collective-permute-start | bytes 1769480 | tf_op jit(solution)/shard_map/ppermute | solution.py:758
  587.5 36.7 %collective-permute-start.18 = (bf16[96,768]{1,0:T(8,128)(2,1)S(1)}, bf16[96,768]{1,0:T(8,128)(2,1)S(1)}, u32[]{:S(2)}, u32[]{:S(2)}) collective-permute-start(bf16[96,768]{1,0:T(8,128)(2,1)S(1)} %get-tuple-element.236), channel_id=1, source_target_pairs={{0,4},{1,5},{2,6},{3,7},{4,0},{5,1},{6,2},{7,3},{8,12},{9,13},{10,... | collective-permute-start | bytes 442376 | tf_op jit(solution)/shard_map/ppermute | solution.py:758
  620.0 12.1 %collective-permute-start.19 = (bf16[96,768]{1,0:T(8,128)(2,1)S(1)}, bf16[96,768]{1,0:T(8,128)(2,1)S(1)}, u32[]{:S(2)}, u32[]{:S(2)}) collective-permute-start(bf16[96,768]{1,0:T(8,128)(2,1)S(1)} %get-tuple-element.238), channel_id=1, source_target_pairs={{0,8},{1,9},{2,10},{3,11},{4,12},{5,13},{6,14},{7,15},{8,0},{9,1},... | collective-permute-start | bytes 442376 | tf_op jit(solution)/shard_map/ppermute | solution.py:758
  620.0 12.1 %collective-permute-start.20 = (bf16[96,768]{1,0:T(8,128)(2,1)S(1)}, bf16[96,768]{1,0:T(8,128)(2,1)S(1)}, u32[]{:S(2)}, u32[]{:S(2)}) collective-permute-start(bf16[96,768]{1,0:T(8,128)(2,1)S(1)} %get-tuple-element.237), channel_id=1, source_target_pairs={{0,12},{1,13},{2,14},{3,15},{4,8},{5,9},{6,10},{7,11},{8,4},{9,5},... | collective-permute-start | bytes 442376 | tf_op jit(solution)/shard_map/ppermute | solution.py:758
  632.2 13.6 %collective-permute-start.21 = (bf16[96,768]{1,0:T(8,128)(2,1)S(1)}, bf16[96,768]{1,0:T(8,128)(2,1)S(1)}, u32[]{:S(2)}, u32[]{:S(2)}) collective-permute-start(bf16[96,768]{1,0:T(8,128)(2,1)S(1)} %get-tuple-element.225), channel_id=1, source_target_pairs={{0,4},{1,5},{2,6},{3,7},{4,0},{5,1},{6,2},{7,3},{8,12},{9,13},{10,... | collective-permute-start | bytes 442376 | tf_op jit(solution)/shard_map/ppermute | solution.py:758
  636.0 13.7 %collective-permute-start.22 = (bf16[96,768]{1,0:T(8,128)(2,1)S(1)}, bf16[96,768]{1,0:T(8,128)(2,1)S(1)}, u32[]{:S(2)}, u32[]{:S(2)}) collective-permute-start(bf16[96,768]{1,0:T(8,128)(2,1)S(1)} %get-tuple-element.225), channel_id=1, source_target_pairs={{0,8},{1,9},{2,10},{3,11},{4,12},{5,13},{6,14},{7,15},{8,0},{9,1},... | collective-permute-start | bytes 442376 | tf_op jit(solution)/shard_map/ppermute | solution.py:758
  638.7 18.2 %collective-permute-start.23 = (bf16[96,768]{1,0:T(8,128)(2,1)S(1)}, bf16[96,768]{1,0:T(8,128)(2,1)S(1)}, u32[]{:S(2)}, u32[]{:S(2)}) collective-permute-start(bf16[96,768]{1,0:T(8,128)(2,1)S(1)} %get-tuple-element.225), channel_id=1, source_target_pairs={{0,12},{1,13},{2,14},{3,15},{4,8},{5,9},{6,10},{7,11},{8,4},{9,5},... | collective-permute-start | bytes 442376 | tf_op jit(solution)/shard_map/ppermute | solution.py:758
  705.8 17.8 %collective-permute-start.26 = (bf16[384,768]{1,0:T(8,128)(2,1)S(1)}, bf16[384,768]{1,0:T(8,128)(2,1)S(1)}, u32[]{:S(2)}, u32[]{:S(2)}) collective-permute-start(bf16[384,768]{1,0:T(8,128)(2,1)S(1)} %constant_dynamic-update-slice_fusion.6), channel_id=1, source_target_pairs={{0,18},{1,19},{2,16},{3,17},{4,22},{5,23},{6,20},{7,21},{8,26},{9,... | collective-permute-start | bytes 1769480 | tf_op jit(solution)/shard_map/ppermute | solution.py:758
  708.0 25.9 %collective-permute-start.24 = (bf16[384,768]{1,0:T(8,128)(2,1)S(1)}, bf16[384,768]{1,0:T(8,128)(2,1)S(1)}, u32[]{:S(2)}, u32[]{:S(2)}) collective-permute-start(bf16[384,768]{1,0:T(8,128)(2,1)S(1)} %constant_dynamic-update-slice_fusion.6), channel_id=1, source_target_pairs={{0,2},{1,3},{2,0},{3,1},{4,6},{5,7},{6,4},{7,5},{8,10},{9,11},{10,... | collective-permute-start | bytes 1769480 | tf_op jit(solution)/shard_map/ppermute | solution.py:758
  708.4 25.6 %collective-permute-start.25 = (bf16[384,768]{1,0:T(8,128)(2,1)S(1)}, bf16[384,768]{1,0:T(8,128)(2,1)S(1)}, u32[]{:S(2)}, u32[]{:S(2)}) collective-permute-start(bf16[384,768]{1,0:T(8,128)(2,1)S(1)} %constant_dynamic-update-slice_fusion.6), channel_id=1, source_target_pairs={{0,16},{1,17},{2,18},{3,19},{4,20},{5,21},{6,22},{7,23},{8,24},{9,... | collective-permute-start | bytes 1769480 | tf_op jit(solution)/shard_map/ppermute | solution.py:758
  734.1 10.9 %collective-permute-start.27 = (bf16[1536,768]{1,0:T(8,128)(2,1)S(1)}, bf16[1536,768]{1,0:T(8,128)(2,1)}, u32[]{:S(2)}, u32[]{:S(2)}) collective-permute-start(bf16[1536,768]{1,0:T(8,128)(2,1)S(1)} %constant_dynamic-update-slice_fusion.2), channel_id=1, source_target_pairs={{0,1},{1,0},{2,3},{3,2},{4,5},{5,4},{6,7},{7,6},{8,9},{9,8},{10,11... | collective-permute-start | bytes 7077896 | tf_op jit(solution)/shard_map/ppermute | solution.py:758
  (56 other events, 1377.1 us)
Sparse Core Ops, SparseCore 0:
  79.5 100.9 all-gather.6
  183.3 126.0 all-gather.8
  312.3 108.0 all-gather.10
  427.2 278.4 all-reduce.4
